TPU v7x, 32 devices: a whole 2x2x4 slice. The times are simulated.
32 devices in a mesh: dp: 16 (over z, y, core), cp: 2 (over x).
Axes of the slice: x: 2, y: 2, z: 4, core: 2. Of those that a mesh axis runs over, the one named last changes fastest.
Arguments:
- tokens: bfloat16 [4096, 768], P(('dp', 'cp')), may hold values from -6 to 6
- segment_ids: int32 [4096], P(('dp', 'cp')), may hold values from 0 to 2, as said below
- cotangent: bfloat16 [4096, 768], P(('dp', 'cp')), may hold values from -6 to 6
- qkv_weight: bfloat16 [2, 768, 2304], P(None, ('dp', 'cp')), may hold values from -0.21875 to 0.21875
- qkv_bias: bfloat16 [2, 2304], P(None, ('dp', 'cp')), may hold values from -3 to 3
- attn_weight: bfloat16 [2, 768, 768], P(None, ('dp', 'cp')), may hold values from -1.75 to 1.75
- attn_bias: bfloat16 [2, 768], P(None, ('dp', 'cp')), may hold values from -2 to 2
- up_weight: bfloat16 [2, 768, 3072], P(None, ('dp', 'cp')), may hold values from -0.21875 to 0.21875
- up_bias: bfloat16 [2, 3072], P(None, ('dp', 'cp')), may hold values from -3 to 3
- down_weight: bfloat16 [2, 3072, 768], P(None, ('dp', 'cp')), may hold values from -0.109375 to 0.109375
- down_bias: bfloat16 [2, 768], P(None, ('dp', 'cp')), may hold values from -2 to 2
- attn_gain: bfloat16 [2, 768], P(None, ('dp', 'cp')), may hold values from 0.5 to 1.5
- attn_shift: bfloat16 [2, 768], P(None, ('dp', 'cp')), may hold values from -2 to 2
- mlp_gain: bfloat16 [2, 768], P(None, ('dp', 'cp')), may hold values from 0.5 to 1.5
- mlp_shift: bfloat16 [2, 768], P(None, ('dp', 'cp')), may hold values from -2 to 2
Outputs:
- activations: bfloat16 [4096, 768], P(('dp', 'cp'))
- input_grad: float32 [4096, 768], P(('dp', 'cp'))
- qkv_weight_grad: float32 [2, 768, 2304], P(None, ('dp', 'cp'))
- qkv_bias_grad: float32 [2, 2304], P(None, ('dp', 'cp'))
- attn_weight_grad: float32 [2, 768, 768], P(None, ('dp', 'cp'))
- attn_bias_grad: float32 [2, 768], P(None, ('dp', 'cp'))
- up_weight_grad: float32 [2, 768, 3072], P(None, ('dp', 'cp'))
- up_bias_grad: float32 [2, 3072], P(None, ('dp', 'cp'))
- down_weight_grad: float32 [2, 3072, 768], P(None, ('dp', 'cp'))
- down_bias_grad: float32 [2, 768], P(None, ('dp', 'cp'))
- attn_gain_grad: float32 [2, 768], P(None, ('dp', 'cp'))
- attn_shift_grad: float32 [2, 768], P(None, ('dp', 'cp'))
- mlp_gain_grad: float32 [2, 768], P(None, ('dp', 'cp'))
- mlp_shift_grad: float32 [2, 768], P(None, ('dp', 'cp'))
Inputs may be any that keep to these rules, and one draw needn't show every extreme that they name: `segment_ids`: within each group of 256 consecutive tokens the ids never fall; ids 0, 1 and 2 all occur, and id 1 runs from a position before 128 // 8 + 1 to one at or after 256 - 128 // 8 - 1.
All inputs are finite; a program needn't handle non-finite values.
Results may differ from a plain program's by a relative error of at most 0.02.
Values may be sent and summed in bfloat16 or wider, within the bound.
No kernel may reach another device: no remote copies, remote signals or barrier semaphores. Data moves between devices by JAX's collectives and lax.ppermute only.
A program may use at most 192 MiB of HBM per device.

v0:
```python
from functools import partial
import math

import jax
import jax.numpy as jnp
from jax import lax
from jax.experimental import pallas as pl
from jax.experimental.pallas import tpu as pltpu
from jax.sharding import Mesh, PartitionSpec as P

D = 768
HEADS = 12
HEAD = 64
FF = 3072
ROT = 16
LAYERS = 2


def layer_norm(stream, norm_gain, norm_shift):
    centered = stream - jnp.mean(stream, axis=-1, keepdims=True)
    spread = jnp.mean(centered * centered, axis=-1, keepdims=True)
    return centered * lax.rsqrt(spread + 1e-05) * norm_gain + norm_shift


def both_norms(stream, gain_attn, shift_attn, gain_mlp, shift_mlp):
    return (layer_norm(stream, gain_attn, shift_attn), layer_norm(stream, gain_mlp, shift_mlp))


def angles(positions):
    inverse = 10000.0 ** (-jnp.arange(0, ROT, 2, dtype=jnp.float32) / ROT)
    phases = positions.astype(jnp.float32)[:, None] * inverse[None, :]
    return (jnp.cos(phases)[:, None, :], jnp.sin(phases)[:, None, :])


def rotate(heads_in, cosine_table, sine_table):
    half_rot = cosine_table.shape[-1]
    first_half = heads_in[..., :half_rot]
    second_half = heads_in[..., half_rot : 2 * half_rot]
    untouched = heads_in[..., 2 * half_rot :]
    return jnp.concatenate(
        [
            first_half * cosine_table - second_half * sine_table,
            second_half * cosine_table + first_half * sine_table,
            untouched,
        ],
        axis=-1,
    )


def split_blocks(update, running, key_piece, value_piece, offset):
    piece_rows = key_piece.shape[0]
    block_rows = 512 if piece_rows > 512 and piece_rows % 512 == 0 else piece_rows
    block_count = piece_rows // block_rows
    if block_count == 1:
        return update(running, key_piece, value_piece, offset)

    def advance(state, inputs):
        key_block, value_block, start = inputs
        return (update(state, key_block, value_block, offset + start), None)

    starts = jnp.arange(block_count, dtype=jnp.int32) * block_rows
    state, _ = lax.scan(
        advance,
        running,
        (
            key_piece.reshape(block_count, block_rows, -1),
            value_piece.reshape(block_count, block_rows, -1),
            starts,
        ),
    )
    return state


def stack_layers(per_layer, member):
    return jnp.stack([layer_entry[member] for layer_entry in per_layer])


def flatten_rows(matrix):
    return matrix.reshape(matrix.shape[:-2] + (-1, 128))


def local(
    tokens,
    segment_ids,
    cotangent,
    qkv_weight,
    qkv_bias,
    attn_weight,
    attn_bias,
    up_weight,
    up_bias,
    down_weight,
    down_bias,
    attn_gain,
    attn_shift,
    mlp_gain,
    mlp_shift,
):
    tok_rows = tokens.shape[0]
    group_rows = tok_rows * lax.axis_size("cp")
    score_scale = 1.0 / math.sqrt(HEAD)
    all_segments = lax.all_gather(segment_ids, "cp", axis=0, tiled=True)
    row_index = lax.axis_index("cp") * tok_rows + jnp.arange(tok_rows, dtype=jnp.int32)
    positions = row_index - jnp.sum(
        (all_segments[None, :] < segment_ids[:, None]).astype(jnp.int32), axis=1
    )
    cosine_table, sine_table = angles(positions)

    def visible_mask(offset, block_rows):
        key_index = offset + jnp.arange(block_rows, dtype=jnp.int32)
        key_segment = lax.dynamic_slice_in_dim(all_segments, offset, block_rows)
        return (key_index[None, :] <= row_index[:, None]) & (
            key_segment[None, :] == segment_ids[:, None]
        )

    def online_step(query_heads, running, key_block, value_block, offset):
        row_max, denominator, weighted = running
        block_rows = key_block.shape[0]
        key_heads = key_block.reshape(block_rows, HEADS, HEAD)
        value_heads = value_block.reshape(block_rows, HEADS, HEAD)
        scores = (
            jnp.einsum("qhd,khd->hqk", query_heads, key_heads, preferred_element_type=jnp.float32)
            * score_scale
        )
        visible = visible_mask(offset, block_rows)
        scores = jnp.where(visible[None], scores, -1e30)
        new_max = jnp.maximum(row_max, jnp.max(scores, axis=-1))
        rescale = jnp.exp(row_max - new_max)
        weights = jnp.where(visible[None], jnp.exp(scores - new_max[..., None]), 0.0)
        denominator = denominator * rescale + jnp.sum(weights, axis=-1)
        weighted = weighted * rescale[..., None] + jnp.einsum(
            "hqk,khd->hqd",
            weights.astype(jnp.bfloat16),
            value_heads,
            preferred_element_type=jnp.float32,
        )
        return (new_max, denominator, weighted)

    stream = tokens.astype(jnp.float32)
    stored = []
    for depth in range(LAYERS):
        params = (
            lax.all_gather(qkv_weight[depth], ("dp", "cp"), axis=0, tiled=True),
            lax.all_gather(qkv_bias[depth], ("dp", "cp"), axis=0, tiled=True),
            lax.all_gather(attn_weight[depth], ("dp", "cp"), axis=0, tiled=True),
            lax.all_gather(attn_bias[depth], ("dp", "cp"), axis=0, tiled=True),
            lax.all_gather(up_weight[depth], ("dp", "cp"), axis=0, tiled=True),
            lax.all_gather(up_bias[depth], ("dp", "cp"), axis=0, tiled=True),
            lax.all_gather(down_weight[depth], ("dp", "cp"), axis=0, tiled=True),
            lax.all_gather(down_bias[depth], ("dp", "cp"), axis=0, tiled=True),
            lax.all_gather(attn_gain[depth], ("dp", "cp"), axis=0, tiled=True),
            lax.all_gather(attn_shift[depth], ("dp", "cp"), axis=0, tiled=True),
            lax.all_gather(mlp_gain[depth], ("dp", "cp"), axis=0, tiled=True),
            lax.all_gather(mlp_shift[depth], ("dp", "cp"), axis=0, tiled=True),
        )
        (
            proj_qkv,
            bias_qkv,
            proj_attn,
            bias_attn,
            proj_up,
            bias_up,
            proj_down,
            bias_down,
            gain_attn,
            shift_attn,
            gain_mlp,
            shift_mlp,
        ) = params
        normed_attn, normed_mlp = both_norms(
            stream,
            gain_attn.astype(jnp.float32),
            shift_attn.astype(jnp.float32),
            gain_mlp.astype(jnp.float32),
            shift_mlp.astype(jnp.float32),
        )
        normed_attn = normed_attn.astype(jnp.bfloat16)
        normed_mlp = normed_mlp.astype(jnp.bfloat16)
        projected = jnp.dot(
            normed_attn, proj_qkv, preferred_element_type=jnp.float32
        ) + bias_qkv.astype(jnp.float32)
        queries = rotate(
            projected[:, :D].reshape(tok_rows, HEADS, HEAD), cosine_table, sine_table
        ).astype(jnp.bfloat16)
        key_rows = (
            rotate(projected[:, D : 2 * D].reshape(tok_rows, HEADS, HEAD), cosine_table, sine_table)
            .astype(jnp.bfloat16)
            .reshape(tok_rows, D)
        )
        values = projected[:, 2 * D :].astype(jnp.bfloat16)
        initial = (
            jnp.full((HEADS, tok_rows), -1e30, jnp.float32),
            jnp.zeros((HEADS, tok_rows), jnp.float32),
            jnp.zeros((HEADS, tok_rows, HEAD), jnp.float32),
        )
        row_max, denominator, weighted = split_blocks(
            partial(online_step, queries),
            initial,
            lax.all_gather(key_rows, "cp", axis=0, tiled=True),
            lax.all_gather(values, "cp", axis=0, tiled=True),
            jnp.int32(0),
        )
        attended = jnp.transpose(weighted / denominator[..., None], (1, 0, 2)).reshape(tok_rows, D)
        log_total = row_max + jnp.log(denominator)
        attended_low = attended.astype(jnp.bfloat16)
        attn_branch = jnp.dot(
            attended_low, proj_attn, preferred_element_type=jnp.float32
        ) + bias_attn.astype(jnp.float32)
        hidden_pre = jnp.dot(
            normed_mlp, proj_up, preferred_element_type=jnp.float32
        ) + bias_up.astype(jnp.float32)
        hidden = jax.nn.gelu(hidden_pre, approximate=False).astype(jnp.bfloat16)
        mlp_branch = jnp.dot(
            hidden, proj_down, preferred_element_type=jnp.float32
        ) + bias_down.astype(jnp.float32)
        stored.append(
            (
                stream,
                normed_attn,
                normed_mlp,
                queries,
                key_rows,
                values,
                attended,
                attended_low,
                log_total,
                hidden_pre,
                hidden,
            )
        )
        stream = stream + attn_branch + mlp_branch
    grad_stream = cotangent.astype(jnp.float32)
    per_layer = [None] * LAYERS
    for depth in reversed(range(LAYERS)):
        (
            saved_stream,
            normed_attn,
            normed_mlp,
            queries,
            key_rows,
            values,
            attended,
            attended_low,
            log_total,
            hidden_pre,
            hidden,
        ) = stored[depth]
        params = (
            lax.all_gather(qkv_weight[depth], ("dp", "cp"), axis=0, tiled=True),
            lax.all_gather(qkv_bias[depth], ("dp", "cp"), axis=0, tiled=True),
            lax.all_gather(attn_weight[depth], ("dp", "cp"), axis=0, tiled=True),
            lax.all_gather(attn_bias[depth], ("dp", "cp"), axis=0, tiled=True),
            lax.all_gather(up_weight[depth], ("dp", "cp"), axis=0, tiled=True),
            lax.all_gather(up_bias[depth], ("dp", "cp"), axis=0, tiled=True),
            lax.all_gather(down_weight[depth], ("dp", "cp"), axis=0, tiled=True),
            lax.all_gather(down_bias[depth], ("dp", "cp"), axis=0, tiled=True),
            lax.all_gather(attn_gain[depth], ("dp", "cp"), axis=0, tiled=True),
            lax.all_gather(attn_shift[depth], ("dp", "cp"), axis=0, tiled=True),
            lax.all_gather(mlp_gain[depth], ("dp", "cp"), axis=0, tiled=True),
            lax.all_gather(mlp_shift[depth], ("dp", "cp"), axis=0, tiled=True),
        )
        (
            proj_qkv,
            bias_qkv,
            proj_attn,
            bias_attn,
            proj_up,
            bias_up,
            proj_down,
            bias_down,
            gain_attn,
            shift_attn,
            gain_mlp,
            shift_mlp,
        ) = params
        grad_low = grad_stream.astype(jnp.bfloat16)
        bias_grad = jnp.sum(grad_low.astype(jnp.float32), axis=0)
        attn_weight_grad = jnp.einsum(
            "td,te->de", attended_low, grad_low, preferred_element_type=jnp.float32
        )
        down_weight_grad = jnp.einsum(
            "tf,te->fe", hidden, grad_low, preferred_element_type=jnp.float32
        )
        grad_attended = jnp.einsum(
            "te,de->td", grad_low, proj_attn, preferred_element_type=jnp.float32
        ).astype(jnp.bfloat16)
        grad_hidden = jnp.einsum(
            "te,fe->tf", grad_low, proj_down, preferred_element_type=jnp.float32
        )
        _, gelu_pull = jax.vjp(partial(jax.nn.gelu, approximate=False), hidden_pre)
        grad_pre = gelu_pull(grad_hidden)[0].astype(jnp.bfloat16)
        up_weight_grad = jnp.einsum(
            "td,tf->df", normed_mlp, grad_pre, preferred_element_type=jnp.float32
        )
        up_bias_grad = jnp.sum(grad_pre.astype(jnp.float32), axis=0)
        grad_normed_mlp = jnp.einsum(
            "tf,df->td", grad_pre, proj_up, preferred_element_type=jnp.float32
        )
        all_keys, all_values = (
            lax.all_gather(key_rows, "cp", axis=0, tiled=True),
            lax.all_gather(values, "cp", axis=0, tiled=True),
        )
        grad_heads = grad_attended.reshape(tok_rows, HEADS, HEAD)
        row_dot = jnp.transpose(
            jnp.sum(
                grad_heads.astype(jnp.float32) * attended.reshape(tok_rows, HEADS, HEAD), axis=-1
            )
        )
        block_rows = 512 if group_rows > 512 and group_rows % 512 == 0 else group_rows
        block_count = group_rows // block_rows
        starts = jnp.arange(block_count, dtype=jnp.int32) * block_rows

        def back_step(grad_query, inputs):
            key_block, value_block, offset = inputs
            key_heads = key_block.reshape(block_rows, HEADS, HEAD)
            value_heads = value_block.reshape(block_rows, HEADS, HEAD)
            scores = (
                jnp.einsum("qhd,khd->hqk", queries, key_heads, preferred_element_type=jnp.float32)
                * score_scale
            )
            visible = visible_mask(offset, block_rows)
            weights = jnp.where(visible[None], jnp.exp(scores - log_total[..., None]), 0.0)
            grad_weights = jnp.einsum(
                "qhd,khd->hqk", grad_heads, value_heads, preferred_element_type=jnp.float32
            )
            grad_scores = (weights * (grad_weights - row_dot[..., None])).astype(jnp.bfloat16)
            grad_query = grad_query + jnp.einsum(
                "hqk,khd->hqd", grad_scores, key_heads, preferred_element_type=jnp.float32
            )
            key_grad = (
                jnp.einsum("hqk,qhd->khd", grad_scores, queries, preferred_element_type=jnp.float32)
                * score_scale
            )
            value_grad = jnp.einsum(
                "hqk,qhd->khd",
                weights.astype(jnp.bfloat16),
                grad_heads,
                preferred_element_type=jnp.float32,
            )
            return (
                grad_query,
                (key_grad.reshape(block_rows, D), value_grad.reshape(block_rows, D)),
            )

        grad_query, (key_grads, value_grads) = lax.scan(
            back_step,
            jnp.zeros((HEADS, tok_rows, HEAD), jnp.float32),
            (
                all_keys.reshape(block_count, block_rows, D),
                all_values.reshape(block_count, block_rows, D),
                starts,
            ),
        )
        local_key_grad, local_value_grad = (
            lax.psum_scatter(
                key_grads.reshape(group_rows, D).astype(jnp.bfloat16),
                "cp",
                scatter_dimension=0,
                tiled=True,
            ).astype(jnp.float32),
            lax.psum_scatter(
                value_grads.reshape(group_rows, D).astype(jnp.bfloat16),
                "cp",
                scatter_dimension=0,
                tiled=True,
            ).astype(jnp.float32),
        )
        query_raw = rotate(
            jnp.transpose(grad_query * score_scale, (1, 0, 2)), cosine_table, -sine_table
        )
        key_raw = rotate(local_key_grad.reshape(tok_rows, HEADS, HEAD), cosine_table, -sine_table)
        grad_projected = jnp.concatenate(
            [query_raw.reshape(tok_rows, D), key_raw.reshape(tok_rows, D), local_value_grad], axis=1
        ).astype(jnp.bfloat16)
        qkv_weight_grad = jnp.einsum(
            "td,te->de", normed_attn, grad_projected, preferred_element_type=jnp.float32
        )
        qkv_bias_grad = jnp.sum(grad_projected.astype(jnp.float32), axis=0)
        grad_normed_attn = jnp.einsum(
            "te,de->td", grad_projected, proj_qkv, preferred_element_type=jnp.float32
        )
        _, norm_pull = jax.vjp(
            both_norms,
            saved_stream,
            gain_attn.astype(jnp.float32),
            shift_attn.astype(jnp.float32),
            gain_mlp.astype(jnp.float32),
            shift_mlp.astype(jnp.float32),
        )
        grad_input, attn_gain_grad, attn_shift_grad, mlp_gain_grad, mlp_shift_grad = norm_pull(
            (grad_normed_attn, grad_normed_mlp)
        )
        grad_stream = grad_stream + grad_input
        summed = (
            lax.psum_scatter(
                flatten_rows(qkv_weight_grad), ("dp", "cp"), scatter_dimension=0, tiled=True
            ),
            lax.psum_scatter(qkv_bias_grad, ("dp", "cp"), scatter_dimension=0, tiled=True),
            lax.psum_scatter(
                flatten_rows(attn_weight_grad), ("dp", "cp"), scatter_dimension=0, tiled=True
            ),
            lax.psum_scatter(bias_grad, ("dp", "cp"), scatter_dimension=0, tiled=True),
            lax.psum_scatter(
                flatten_rows(up_weight_grad), ("dp", "cp"), scatter_dimension=0, tiled=True
            ),
            lax.psum_scatter(up_bias_grad, ("dp", "cp"), scatter_dimension=0, tiled=True),
            lax.psum_scatter(
                flatten_rows(down_weight_grad), ("dp", "cp"), scatter_dimension=0, tiled=True
            ),
            lax.psum_scatter(bias_grad, ("dp", "cp"), scatter_dimension=0, tiled=True),
            lax.psum_scatter(attn_gain_grad, ("dp", "cp"), scatter_dimension=0, tiled=True),
            lax.psum_scatter(attn_shift_grad, ("dp", "cp"), scatter_dimension=0, tiled=True),
            lax.psum_scatter(mlp_gain_grad, ("dp", "cp"), scatter_dimension=0, tiled=True),
            lax.psum_scatter(mlp_shift_grad, ("dp", "cp"), scatter_dimension=0, tiled=True),
        )
        per_layer[depth] = (
            summed[0].reshape(-1, 3 * D),
            summed[1],
            summed[2].reshape(-1, D),
            summed[3],
            summed[4].reshape(-1, FF),
            summed[5],
            summed[6].reshape(-1, D),
            summed[7],
            summed[8],
            summed[9],
            summed[10],
            summed[11],
        )
    stacked = [stack_layers(per_layer, member) for member in range(12)]
    return (
        stream.astype(jnp.bfloat16),
        grad_stream,
        stacked[0],
        stacked[1],
        stacked[2],
        stacked[3],
        stacked[4],
        stacked[5],
        stacked[6],
        stacked[7],
        stacked[8],
        stacked[9],
        stacked[10],
        stacked[11],
    )


TEAM = 4
TEAM_AXES = ("core", "x")
LINE_AXES = ("z", "y")
LINE = 4
MINE = (3 * D) // TEAM
HCOLS = D // TEAM
UCOLS = FF // TEAM
VMEM_BYTES = 56 * 1024 * 1024
BF = jnp.bfloat16
F32 = jnp.float32


def call(body, out_shape, name, operands, scratch=()):
    return pl.pallas_call(
        body,
        out_shape=out_shape,
        scratch_shapes=list(scratch),
        compiler_params=pltpu.CompilerParams(vmem_limit_bytes=VMEM_BYTES),
        name=name,
    )(*operands)


def shape(dims, kind):
    return jax.ShapeDtypeStruct(dims, kind)


def mm(left, right):
    return jnp.dot(left, right, preferred_element_type=F32)


def mm_t(left, right):
    return lax.dot_general(left, right, (((1,), (1,)), ((), ())), preferred_element_type=F32)


def t_mm(left, right):
    return lax.dot_general(left, right, (((0,), (0,)), ((), ())), preferred_element_type=F32)


def pick(member, pieces, wanted):
    chosen = pieces[0]
    for s in range(1, TEAM):
        chosen = jnp.where((member ^ s) == wanted, pieces[s], chosen)
    return chosen


def small_rows(vectors, depth):
    rows = []
    for vector in vectors:
        values = vector[depth : depth + 1].astype(F32)
        rows.append(
            jnp.concatenate([values, jnp.zeros((1, 128 - values.shape[1]), F32)], axis=1)
        )
    return jnp.concatenate(rows, axis=0)


def pack_body(me_ref, qkv_ref, up_ref, *refs):
    vectors, outs = [r[...] for r in refs[:8]], refs[8:]
    me = me_ref[0]
    small = jnp.concatenate([small_rows(vectors, depth) for depth in range(LAYERS)], axis=0)
    small = jnp.concatenate([small, jnp.zeros((small.shape[0], UCOLS - 128), F32)], axis=1)
    parts = [[] for _ in range(TEAM)]
    for depth in range(LAYERS):
        rows = qkv_ref.shape[1]
        qkv = qkv_ref[depth].astype(F32)
        up = up_ref[depth].astype(F32)
        blocks = up.shape[1] // (TEAM * 96)
        for p in range(TEAM):
            parts[p].append(
                jnp.concatenate(
                    [up[:, 96 * (TEAM * b + p) : 96 * (TEAM * b + p + 1)] for b in range(blocks)],
                    axis=1,
                )
            )
            parts[p].append(
                jnp.concatenate(
                    [qkv[:, D * t + HCOLS * p : D * t + HCOLS * (p + 1)] for t in range(3)]
                    + [jnp.zeros((rows, UCOLS - MINE), F32)],
                    axis=1,
                )
            )
    parts = [jnp.concatenate(group, axis=0) for group in parts]
    for s in range(TEAM):
        chosen = parts[0]
        for p in range(1, TEAM):
            chosen = jnp.where((me ^ s) == p, parts[p], chosen)
        outs[s][...] = jnp.concatenate([chosen, small], axis=0).astype(BF)


def assemble_body(me_ref, p0, p1, p2, p3, attn_ref, down_ref, *outs):
    me = me_ref[0]
    slots = [r[...].astype(F32) for r in (p0, p1, p2, p3)]
    ordered = [pick(me, slots, p) for p in range(TEAM)]
    for depth, out in enumerate(outs):
        base = 48 * depth
        up = jnp.concatenate([piece[base : base + 24] for piece in ordered], axis=0)
        qkv = jnp.concatenate([piece[base + 24 : base + 48] for piece in ordered], axis=0)
        attn = attn_ref[depth].astype(F32)
        side = jnp.concatenate([attn[:, HCOLS * n : HCOLS * (n + 1)] for n in range(4)], axis=0)
        out[0:96] = up.astype(BF)
        out[96:192] = down_ref[depth]
        out[192:288] = jnp.concatenate([qkv[:, :MINE], side], axis=1).astype(BF)
        if out.shape[0] > 288:
            small = jnp.concatenate(
                [piece[96:112, :128] for piece in ordered] + [jnp.zeros((16, D - 4 * 128), F32)],
                axis=1,
            )
            out[288:304] = small.astype(BF)


def source_team(me_ref, index):
    shift, flip = index % LINE, index // LINE
    return 2 * lax.rem(me_ref[1] + LINE - shift, LINE) + (me_ref[2] ^ flip)


def target_team(me_ref, index):
    shift, flip = index % LINE, index // LINE
    return 2 * lax.rem(me_ref[1] + shift, LINE) + (me_ref[2] ^ flip)


def place(me_ref, pieces, whole):
    for index, piece in enumerate(pieces):
        whole[source_team(me_ref, index)] = piece[...]


def hand_out(me_ref, whole, keep, send):
    for s in range(LINE):
        keep[s] = whole[target_team(me_ref, s)]
        send[s] = whole[target_team(me_ref, LINE + s)]


def add_body(me_ref, keep, received, *outs):
    for s, out in enumerate(outs):
        out[...] = (keep[s + 1].astype(F32) + received[s + 1].astype(F32)).astype(BF)


def layer_vectors(me_ref, whole, depth):
    me = me_ref[0]
    small = [whole[k].astype(F32) for k in range(2 * LINE)]
    fields = [block[8 * depth : 8 * (depth + 1)] for block in small]
    shared = jnp.concatenate(
        [block[2:8, 128 * p : 128 * p + 24] for block in fields for p in range(TEAM)], axis=1
    )
    up_rows, qkv_rows = [], []
    qkv = jnp.concatenate(
        [block[0:1, 128 * p : 128 * p + 72] for block in fields for p in range(TEAM)], axis=1
    )
    for p in range(TEAM):
        up_rows.append(
            jnp.concatenate([block[1:2, 128 * p : 128 * p + 96] for block in fields], axis=1)
        )
        qkv_rows.append(
            jnp.concatenate(
                [qkv[:, D * t + HCOLS * p : D * t + HCOLS * (p + 1)] for t in range(3)]
                + [jnp.zeros((1, D - MINE), F32)],
                axis=1,
            )
        )
    up_mine, qkv_mine = up_rows[0], qkv_rows[0]
    for p in range(1, TEAM):
        up_mine = jnp.where(me == p, up_rows[p], up_mine)
        qkv_mine = jnp.where(me == p, qkv_rows[p], qkv_mine)
    return jnp.concatenate([shared, up_mine, qkv_mine], axis=0)


def attn_weights(whole):
    qkv = whole[:, 0:96, :][:, :, :MINE].reshape(D, MINE)
    side = whole[:, 0:96, MINE:].astype(F32)
    out = jnp.concatenate(
        [side[:, 24 * n : 24 * (n + 1), :].reshape(HCOLS, HCOLS) for n in range(4)], axis=1
    )
    return qkv, out.astype(BF)


def project(scaled, vec, weight, cosine, sine):
    normed = (scaled * vec[0:1] + vec[1:2]).astype(BF)
    projected = mm(normed, weight) + vec[7:8, :MINE]
    turned = turn(projected[:, : 2 * HCOLS], cosine, sine)
    queries = (turned[:, :HCOLS] * 0.125).astype(BF)
    keys = turned[:, HCOLS:].astype(BF)
    values = projected[:, 2 * HCOLS :].astype(BF)
    return normed, queries, keys, values


def attend_body(me_ref, x0, x1, x2, x3, *refs):
    pieces, smalls = refs[:8], refs[8:16]
    cos_ref, sin_ref, mask_ref, y_ref, vec_ref, whole, small = refs[16:]
    place(me_ref, pieces, whole)
    place(me_ref, smalls, small)
    for depth in range(LAYERS):
        vec_ref[depth] = layer_vectors(me_ref, small, depth)
    vec = vec_ref[0]
    weight, out_weight = attn_weights(whole)
    for g, (first, second) in enumerate(((x0, x1), (x2, x3))):
        rows = pl.ds(PAIR * g, PAIR)
        scaled, _ = norm_parts(two_slots(first[...], second[...]))
        _, queries, keys, values = project(scaled, vec, weight, cos_ref[rows, :], sin_ref[rows, :])
        total = jnp.zeros((PAIR, HCOLS), F32)
        for head in range(HEADS // TEAM):
            owned = head_mask(PAIR, head)
            scores = mm_t(jnp.where(owned, queries, jnp.zeros_like(queries)), keys) + mask_ref[g]
            weights = jnp.exp(scores - jnp.max(scores, axis=-1, keepdims=True))
            below = jnp.sum(weights, axis=-1, keepdims=True)
            total = total + jnp.where(owned, mm(weights.astype(BF), values) / below, 0.0)
        y_ref[rows, :] = mm(total.astype(BF), out_weight)


def mlp_body(me_ref, x0, x1, x2, x3, *refs):
    pieces, (vec_ref, a_ref, y0, y1, y2, y3, whole) = refs[:8], refs[8:]
    place(me_ref, pieces, whole)
    vec = vec_ref[0]
    up = whole[:, 0:96, :].reshape(D, UCOLS)
    down = whole[:, 96:192, :].reshape(UCOLS, D)
    for g, (first, second, y_first, y_second) in enumerate(((x0, x1, y0, y1), (x2, x3, y2, y3))):
        rows = pl.ds(PAIR * g, PAIR)
        scaled, _ = norm_parts(two_slots(first[...], second[...]))
        normed = (scaled * vec[2:3] + vec[3:4]).astype(BF)
        before = mm(normed, up) + vec[6:7]
        hidden = (before * (0.5 * (1.0 + lax.erf(before * (1.0 / math.sqrt(2.0)))))).astype(BF)
        result = mm(hidden, down) + a_ref[rows, :]
        y_first[...] = result[0:TOK].astype(y_first.dtype)
        y_second[...] = result[TOK:].astype(y_second.dtype)


def mlp_both_body(depth, last, me_ref, x0, x1, x2, x3, g0, g1, g2, g3, *refs):
    pieces, vec_ref, blocks = refs[:8], refs[8], refs[9:11]
    dn_ref, sum_ref = refs[11:13]
    whole, grads, c_s, hid_s, du_s, gb_s = refs[-6:]
    place(me_ref, pieces, whole)
    vec = vec_ref[depth]
    up = whole[:, 0:96, :].reshape(D, UCOLS)
    down = whole[:, 96:192, :].reshape(UCOLS, D)
    gain_sum = jnp.zeros((1, D), F32)
    shift_sum = jnp.zeros((1, D), F32)
    bias_sum = jnp.zeros((1, D), F32)
    up_sum = jnp.zeros((1, UCOLS), F32)
    for g, (first, second, g_first, g_second) in enumerate(((x0, x1, g0, g1), (x2, x3, g2, g3))):
        rows = pl.ds(PAIR * g, PAIR)
        scaled, _ = norm_parts(two_slots(first[...], second[...]))
        normed = (scaled * vec[2:3] + vec[3:4]).astype(BF)
        c_s[rows, :] = normed
        low = jnp.concatenate([g_first[...], g_second[...]], axis=0)
        gb_s[rows, :] = low
        hidden, slope = gelu_parts(mm(normed, up) + vec[6:7])
        hidden = hidden.astype(BF)
        hid_s[rows, :] = hidden
        if last:
            refs[13][rows, :] = mm(hidden, down)
        du = (mm_t(low, down) * slope).astype(BF)
        du_s[rows, :] = du
        dc = mm_t(du, up)
        dn_ref[rows, :] = dc * vec[2:3]
        gain_sum = gain_sum + jnp.sum(dc * scaled, axis=0, keepdims=True)
        shift_sum = shift_sum + jnp.sum(dc, axis=0, keepdims=True)
        bias_sum = bias_sum + jnp.sum(low.astype(F32), axis=0, keepdims=True)
        up_sum = up_sum + jnp.sum(du.astype(F32), axis=0, keepdims=True)
    grads[:, 0:96, :] = t_mm(c_s[...], du_s[...]).reshape(-1, 96, UCOLS).astype(BF)
    grads[:, 96:192, :] = t_mm(hid_s[...], gb_s[...]).reshape(-1, 96, D).astype(BF)
    hand_out(me_ref, grads, *blocks)
    sum_ref[...] = jnp.concatenate(
        [bias_sum, up_sum, gain_sum, shift_sum, jnp.zeros((4, D), F32)], axis=0
    )


def attend_both_body(depth, last, me_ref, x0, x1, x2, x3, g0, g1, g2, g3, *refs):
    pieces, (vec_ref, cos_ref, sin_ref, mask_ref, dn_ref, sum_ref) = refs[:8], refs[8:14]
    refs = refs[14:]
    if last:
        y_ref, refs = refs[0], refs[1:]
    blocks, (n0, n1, n2, n3) = refs[:2], refs[2:6]
    whole, grads, a_s, dp_s, o_s, gb_s = refs[-6:]
    place(me_ref, pieces, whole)
    vec = vec_ref[depth]
    weight, out_weight = attn_weights(whole)
    gain_sum = jnp.zeros((1, D), F32)
    shift_sum = jnp.zeros((1, D), F32)
    bias_sum = jnp.zeros((1, MINE), F32)
    for g, (first, second, g_first, g_second, n_first, n_second) in enumerate(
        ((x0, x1, g0, g1, n0, n1), (x2, x3, g2, g3, n2, n3))
    ):
        rows = pl.ds(PAIR * g, PAIR)
        cosine, sine = cos_ref[rows, :], sin_ref[rows, :]
        scaled, _ = norm_parts(two_slots(first[...], second[...]))
        normed, queries, keys, values = project(scaled, vec, weight, cosine, sine)
        a_s[rows, :] = normed
        low = jnp.concatenate([g_first[...], g_second[...]], axis=0)
        gb_s[rows, :] = low
        grad_o = mm_t(low, out_weight).astype(BF)
        zero = jnp.zeros_like(queries)
        out = jnp.zeros((PAIR, HCOLS), F32)
        dq = jnp.zeros((PAIR, HCOLS), F32)
        dk = jnp.zeros((PAIR, HCOLS), F32)
        dv = jnp.zeros((PAIR, HCOLS), F32)
        for head in range(HEADS // TEAM):
            owned = head_mask(PAIR, head)
            scores = mm_t(jnp.where(owned, queries, zero), keys) + mask_ref[g]
            weights = jnp.exp(scores - jnp.max(scores, axis=-1, keepdims=True))
            weights = weights / jnp.sum(weights, axis=-1, keepdims=True)
            rounded = weights.astype(BF)
            dweights = mm_t(jnp.where(owned, grad_o, zero), values)
            delta = jnp.sum(weights * dweights, axis=-1, keepdims=True)
            dscores = (weights * (dweights - delta)).astype(BF)
            out = out + jnp.where(owned, mm(rounded, values), 0.0)
            dq = dq + jnp.where(owned, mm(dscores, keys), 0.0)
            dk = dk + jnp.where(owned, t_mm(dscores, queries), 0.0)
            dv = dv + jnp.where(owned, t_mm(rounded, grad_o), 0.0)
        o_s[rows, :] = out.astype(BF)
        both = turn(jnp.concatenate([dq * 0.125, dk], axis=1), cosine, -sine)
        dproj = jnp.concatenate([both, dv], axis=1).astype(BF)
        dp_s[rows, :] = dproj
        bias_sum = bias_sum + jnp.sum(dproj.astype(F32), axis=0, keepdims=True)
        da = mm_t(dproj, weight)
        gain_sum = gain_sum + jnp.sum(da * scaled, axis=0, keepdims=True)
        shift_sum = shift_sum + jnp.sum(da, axis=0, keepdims=True)
        dn = dn_ref[rows, :] + da * vec[0:1]
        n_first[...] = dn[0:TOK].astype(n_first.dtype)
        n_second[...] = dn[TOK:].astype(n_second.dtype)
        if last:
            result = y_ref[rows, :] + mm(out.astype(BF), out_weight)
            y_first, y_second = refs[6 + 2 * g], refs[7 + 2 * g]
            y_first[...] = result[0:TOK].astype(y_first.dtype)
            y_second[...] = result[TOK:].astype(y_second.dtype)
    qkv_grad = t_mm(a_s[...], dp_s[...]).reshape(-1, 96, MINE)
    out_grad = t_mm(o_s[...], gb_s[...])
    side = jnp.concatenate(
        [out_grad[:, HCOLS * n : HCOLS * (n + 1)].reshape(-1, 24, HCOLS) for n in range(4)], axis=1
    )
    grads[:, 0:96, :] = jnp.concatenate([qkv_grad, side], axis=2).astype(BF)
    sums = sum_ref[...]
    vectors = jnp.concatenate([sums[0:2], gain_sum, shift_sum, sums[2:4]], axis=0)
    me = me_ref[0]
    spread = jnp.concatenate(
        [
            jnp.where(me == p, bias_sum[:, HCOLS * t : HCOLS * (t + 1)], 0.0)
            for t in range(3)
            for p in range(TEAM)
        ],
        axis=1,
    )
    for k in range(2 * LINE):
        shared = jnp.concatenate(
            [vectors[:, 96 * k : 96 * (k + 1)], jnp.zeros((6, D - 96), F32)], axis=1
        )
        bias = jnp.concatenate(
            [spread[:, 288 * k : 288 * (k + 1)], jnp.zeros((1, D - 288), F32)], axis=1
        )
        grads[k, 96:112, :] = jnp.concatenate([shared, bias, jnp.zeros((9, D), F32)], axis=0).astype(BF)
    hand_out(me_ref, grads, *blocks)


def residual_body(x_ref, y0, y1, y2, y3, vec_ref, out_ref, low_ref):
    depth = 0 if x_ref.dtype == BF else 1
    total = y0[...] + y1[...].astype(F32) + y2[...].astype(F32) + y3[...].astype(F32)
    result = x_ref[...].astype(F32) + total + (vec_ref[depth, 4:5] + vec_ref[depth, 5:6])
    out_ref[...] = result
    low_ref[...] = result.astype(BF)

def norm_parts(stream):
    centered = stream - jnp.mean(stream, axis=-1, keepdims=True)
    spread = jnp.mean(centered * centered, axis=-1, keepdims=True)
    inverse = lax.rsqrt(spread + 1e-05)
    return centered * inverse, inverse


def two_slots(first, second):
    return jnp.concatenate([first[0:TOK].astype(F32), second[0:TOK].astype(F32)], axis=0)


TOK = 128
PAIR = 2 * TOK


def turn(block, cosine, sine):
    lane = lax.broadcasted_iota(jnp.int32, (block.shape[0], 128), 1) % HEAD
    tiles = []
    for t in range(block.shape[1] // 128):
        tile = block[:, 128 * t : 128 * (t + 1)]
        swapped = jnp.where(
            lane < ROT // 2, pltpu.roll(tile, 128 - ROT // 2, 1), pltpu.roll(tile, ROT // 2, 1)
        )
        tiles.append(tile * cosine + swapped * sine)
    return jnp.concatenate(tiles, axis=1)


def head_mask(rows, head):
    lane = lax.broadcasted_iota(jnp.int32, (rows, HCOLS), 1)
    return (lane >= head * HEAD) & (lane < (head + 1) * HEAD)


def gelu_parts(u):
    cdf = 0.5 * (1.0 + lax.erf(u * (1.0 / math.sqrt(2.0))))
    density = jnp.exp(-0.5 * u * u) * (1.0 / math.sqrt(2.0 * math.pi))
    return u * cdf, cdf + u * density


def norm_back_body(x_ref, g_ref, n0, n1, n2, n3, out_ref, low_ref):
    scaled, inverse = norm_parts(x_ref[...].astype(F32))
    dn = n0[...] + n1[...].astype(F32) + n2[...].astype(F32) + n3[...].astype(F32)
    centered = dn - jnp.mean(dn, axis=-1, keepdims=True)
    moment = jnp.mean(dn * scaled, axis=-1, keepdims=True)
    result = g_ref[...].astype(F32) + inverse * (centered - scaled * moment)
    out_ref[...] = result
    low_ref[...] = result.astype(BF)


def split_body(me_ref, *refs):
    me = me_ref[0]

    def total(group):
        result = group[0][0].astype(F32) + group[1][0].astype(F32)
        for ref in group[2:]:
            result = result + ref[...].astype(F32)
        return result

    mlp, attn = total(refs[0:5]), total(refs[5:10])
    outs, (down_ref, attn_ref, small_ref) = refs[10:14], refs[14:]
    up = mlp[0:96]
    down_ref[...] = mlp[96:192]
    side = attn[0:96, MINE:]
    attn_ref[...] = jnp.concatenate(
        [side[24 * n : 24 * (n + 1)] for n in range(4)], axis=1
    ).astype(BF)
    qkv = jnp.concatenate([attn[0:96, :MINE], jnp.zeros((96, UCOLS - MINE), F32)], axis=1)
    small = attn[96:112]
    parts, bias = [], jnp.zeros((1, 24), F32)
    for p in range(TEAM):
        rows = slice(24 * p, 24 * (p + 1))
        gains = jnp.concatenate([small[2:6, rows], jnp.zeros((4, D - 24), F32)], axis=1)
        qkv_bias = jnp.concatenate(
            [small[6:7, 72 * p : 72 * (p + 1)], jnp.zeros((1, D - 72), F32)], axis=1
        )
        parts.append(
            jnp.concatenate([up[rows], qkv[rows], gains, qkv_bias, jnp.zeros((11, D), F32)], axis=0)
        )
        bias = jnp.where(me == p, small[0:1, rows], bias)
    small_ref[...] = jnp.concatenate(
        [
            jnp.concatenate([bias, jnp.zeros((1, 104), F32)], axis=1),
            small[1:2, :128],
            jnp.zeros((6, 128), F32),
        ],
        axis=0,
    )
    for s, out in enumerate(outs):
        piece = parts[0]
        for p in range(1, TEAM):
            piece = jnp.where((me ^ s) == p, parts[p], piece)
        out[...] = piece.astype(BF)


def unpack_body(me_ref, *refs):
    me = me_ref[0]
    (
        qkv_ref, qkv_b_ref, attn_ref, attn_b_ref, up_ref, up_b_ref, down_ref,
        ga_ref, sa_ref, gm_ref, sm_ref,
    ) = refs[7 * LAYERS :]
    gain_refs = (ga_ref, sa_ref, gm_ref, sm_ref)
    for depth in range(LAYERS):
        group = refs[7 * depth : 7 * (depth + 1)]
        slots = [r[...].astype(F32) for r in group[:TEAM]]
        own_small, attn_rows, down_rows = group[TEAM:]
        ordered = [pick(me, slots, p) for p in range(TEAM)]
        blocks = FF // (96 * TEAM)
        up_ref[depth] = jnp.concatenate(
            [ordered[p][0:24, 96 * b : 96 * (b + 1)] for b in range(blocks) for p in range(TEAM)],
            axis=1,
        )
        qkv_ref[depth] = jnp.concatenate(
            [
                ordered[p][24:48, HCOLS * t : HCOLS * (t + 1)]
                for t in range(3)
                for p in range(TEAM)
            ],
            axis=1,
        )
        attn_ref[depth] = attn_rows[...].astype(F32)
        down_ref[depth] = down_rows[...]
        small = slots[0][48:56, :128] + slots[1][48:56, :128]
        small = small + slots[2][48:56, :128] + slots[3][48:56, :128]
        for n, ref in enumerate(gain_refs):
            ref[depth : depth + 1] = small[n : n + 1, :24]
        qkv_b_ref[depth : depth + 1] = small[4:5, :72]
        attn_b_ref[depth : depth + 1] = own_small[0:1, :24]
        up_b_ref[depth : depth + 1] = own_small[1:2, :96]


def team_send(piece, slot):
    flips = [(m, m ^ slot) for m in range(TEAM)]
    return lax.ppermute(piece, TEAM_AXES, flips)


def line_shift(piece, shift):
    size = lax.axis_size("z")
    return lax.ppermute(piece, "z", [(i, (i + shift) % size) for i in range(size)])


def line_flip(piece):
    return lax.ppermute(piece, "y", [(0, 1), (1, 0)])


def after(value, *others):
    return lax.optimization_barrier((value, *others))[0]


def line_near(piece):
    return [piece] + [line_shift(piece, s) for s in range(1, LINE)]


def local_team(
    tokens, segment_ids, cotangent, qkv_weight, qkv_bias, attn_weight, attn_bias,
    up_weight, up_bias, down_weight, down_bias, attn_gain, attn_shift, mlp_gain, mlp_shift,
):
    lines = lax.axis_size("z") * lax.axis_size("y")
    world = lines * TEAM
    member = lax.axis_index("core") * 2 + lax.axis_index("x")
    me = jnp.stack([member, lax.axis_index("z"), lax.axis_index("y")]).astype(jnp.int32)
    everywhere = LINE_AXES + TEAM_AXES
    tok_all = TEAM * TOK
    whole_spec = pl.BlockSpec(memory_space=pltpu.VMEM)

    def run(body, out_shape, name, operands, scratch=()):
        specs = [whole_spec if isinstance(x, jax.Array) else x[1] for x in operands]
        return pl.pallas_call(
            body,
            grid=(1,),
            out_shape=out_shape,
            in_specs=[pl.BlockSpec(memory_space=pltpu.SMEM)] + specs,
            scratch_shapes=[pltpu.VMEM(dims, kind) for dims, kind in scratch],
            compiler_params=pltpu.CompilerParams(vmem_limit_bytes=VMEM_BYTES),
            name=name,
        )(me, *[x if isinstance(x, jax.Array) else x[0] for x in operands])

    def part(rows, start):
        return pl.BlockSpec((rows, D), lambda i: (start // rows, 0))

    def one_of(array, index):
        return (array, pl.BlockSpec((1,) + array.shape[1:], lambda i: (index, 0, 0)))

    def exchange(blocks):
        return [blocks[0]] + [team_send(blocks[s], s) for s in range(1, TEAM)]

    small = (
        qkv_bias, up_bias, attn_gain, attn_shift, mlp_gain, mlp_shift, attn_bias, down_bias
    )
    packed = run(
        pack_body, [shape((112, D), BF)] * TEAM, "pack_weights", (qkv_weight, up_weight, *small)
    )
    spread = [(i, TEAM * (i % lines) + i // lines) for i in range(world)]
    gather_back = [(b, a) for a, b in spread]
    attn_piece = lax.ppermute(attn_weight, everywhere, spread)
    chunks = run(
        assemble_body,
        [shape((304, D), BF), shape((288, D), BF)],
        "assemble_weights",
        (*exchange(packed), attn_piece, down_weight),
    )
    near = line_near(chunks[0])
    pieces = [near + [line_flip(p) for p in near]]
    near = line_near(after(chunks[1], near[2]))
    pieces.append(near + [line_flip(p) for p in near])
    m_parts = [[(p, part(192, 0)) for p in group] for group in pieces]
    a_parts = [[(p, part(96, 192)) for p in group] for group in pieces]
    small_parts = [(p, part(16, 288)) for p in pieces[0]]

    ids_row = jnp.pad(segment_ids.astype(BF)[None, :], ((0, 15), (0, D - TOK)))
    load = jnp.concatenate([tokens, ids_row, cotangent], axis=0)
    loads = [load] + exchange([after(load, chunks[0])] * TEAM)[1:]
    token_slots = [(load, part(TOK, 0)) for load in loads]
    here = lax.axis_index("x")
    rows = jnp.arange(TOK, dtype=jnp.int32)
    places = jnp.concatenate([here * TOK + rows, (1 - here) * TOK + rows])
    masks, cosines, sines = [], [], []
    lane = jnp.arange(128, dtype=jnp.int32) % HEAD
    inverse = 10000.0 ** (-(lane % (ROT // 2) * 2).astype(F32) / ROT)
    for g in range(2):
        ids = jnp.concatenate([load[TOK, :TOK] for load in loads[2 * g : 2 * g + 2]]).astype(F32)
        visible = (places[None, :] <= places[:, None]) & (ids[None, :] == ids[:, None])
        masks.append(jnp.where(visible, 0.0, -1e30).astype(F32))
        position = places - jnp.sum((ids[None, :] < ids[:, None]).astype(jnp.int32), axis=1)
        phases = position.astype(F32)[:, None] * inverse[None, :]
        cosines.append(jnp.where(lane[None, :] < ROT, jnp.cos(phases), 1.0))
        sign = jnp.where(lane < ROT // 2, -1.0, jnp.where(lane < ROT, 1.0, 0.0))
        sines.append(jnp.sin(phases) * sign[None, :])
    mask = jnp.stack(masks)
    cosine, sine = jnp.concatenate(cosines), jnp.concatenate(sines)

    four = [shape((TOK, D), F32)] + [shape((TOK, D), BF)] * 3
    stream_pair = [shape((TOK, D), F32), shape((TOK, D), BF)]
    wide = ((tok_all, D), BF)

    attn_out, vec = run(
        attend_body,
        [shape((tok_all, D), F32), shape((LAYERS, 8, D), F32)],
        "attend_forward",
        (*token_slots, *a_parts[0], *small_parts, cosine, sine, mask),
        [((lines, 96, D), BF), ((lines, 16, D), BF)],
    )
    y = run(
        mlp_body,
        four,
        "mlp_forward",
        (*token_slots, *m_parts[0], vec, attn_out),
        [((lines, 192, D), BF)],
    )

    def residual(stream, blocks):
        return call(residual_body, stream_pair, "residual", (stream, *exchange(blocks), vec))

    stream, low = residual(tokens, y)
    streams = [tokens, stream]
    slots = [token_slots, exchange([low] * TEAM)]

    grad = cotangent
    grad_slots = [load[TOK + 16 :] for load in loads]
    outs = [None] * LAYERS
    block_m, block_a = shape((192, D), BF), shape((112, D), BF)

    def mlp_back(depth, slots, grad_slots):
        last = depth == LAYERS - 1
        result = run(
            partial(mlp_both_body, depth, last),
            [shape((4, 192, D), BF)] * 2
            + [shape((tok_all, D), F32), shape((8, D), F32)]
            + ([shape((tok_all, D), F32)] if last else []),
            "mlp_both",
            (*slots, *grad_slots, *m_parts[depth], vec),
            [((lines, 192, D), BF), ((lines, 192, D), BF), wide, wide, wide, wide],
        )
        return result[0], line_flip(result[1]), result[2:]

    def attend_back(depth, slots, grad_slots, rest):
        last = depth == LAYERS - 1
        result = run(
            partial(attend_both_body, depth, last),
            [shape((4, 112, D), BF)] * 2 + four + (four if last else []),
            "attend_both",
            (*slots, *grad_slots, *a_parts[depth], vec, cosine, sine, mask, *rest),
            [
                ((lines, 96, D), BF),
                ((lines, 112, D), BF),
                wide,
                ((tok_all, MINE), BF),
                ((tok_all, HCOLS), BF),
                wide,
            ],
        )
        return result[0], line_flip(result[1]), result[2:6], result[6:]

    def norm_back(depth, grad, received):
        return call(
            norm_back_body, stream_pair, "norm_backward", (streams[depth], grad, *received)
        )

    def add(kind, keep, other, name):
        return run(add_body, [kind] * 3, name, (keep, other))

    def shifts(sums):
        return [line_shift(piece, s + 1) for s, piece in enumerate(sums)]

    def hand_over(depth, m_keep, m_other, m_sums, a_keep, a_other, a_sums):
        mine = run(
            split_body,
            [shape((64, D), BF)] * TEAM
            + [shape((96, D), F32), shape((24, D), BF), shape((8, 128), F32)],
            "split_gradients",
            (
                one_of(m_keep, 0), one_of(m_other, 0), *m_sums,
                one_of(a_keep, 0), one_of(a_other, 0), *a_sums,
            ),
        )
        attn_rows = lax.ppermute(mine[TEAM + 1], everywhere, gather_back)
        outs[depth] = exchange(mine[:TEAM]) + [mine[TEAM + 2], attn_rows, mine[TEAM]]
        return mine

    m_keep1, m_other1, rest = mlp_back(1, slots[1], grad_slots)
    a_keep1, a_other1, ns, ys = attend_back(1, slots[1], grad_slots, rest)
    received = exchange(ns)
    received[3] = after(received[3], m_other1)
    grad, low = norm_back(1, grad, received)
    m_added1 = add(block_m, m_keep1, after(m_other1, low), "add_mlp")
    m_sums1 = shifts(m_added1)
    grad_slots = exchange([low] * TEAM)
    _, activations = residual(streams[1], [ys[0]] + [after(y, grad_slots[3]) for y in ys[1:]])
    grad_slots[0] = after(grad_slots[0], *m_added1)
    m_keep0, m_other0, rest = mlp_back(0, slots[0], grad_slots)
    a_added1 = add(block_a, a_keep1, after(a_other1, rest[0]), "add_attend")
    a_sums1 = shifts(a_added1)
    a_keep0, a_other0, ns, _ = attend_back(
        0, slots[0], grad_slots, [after(rest[0], *a_added1, *m_sums1), *rest[1:]]
    )
    grad, _ = norm_back(0, grad, exchange(ns))
    mine = hand_over(1, m_keep1, m_other1, m_sums1, a_keep1, a_other1, a_sums1)
    m_added0 = add(block_m, m_keep0, after(m_other0, mine[0]), "add_mlp")
    m_sums0 = shifts(m_added0)
    a_added0 = add(block_a, a_keep0, after(a_other0, *m_added0), "add_attend")
    a_sums0 = shifts(a_added0)
    hand_over(0, m_keep0, m_other0, m_sums0, a_keep0, a_other0, a_sums0)
    row_24 = shape((LAYERS, 24), F32)
    final = run(
        unpack_body,
        [
            shape((LAYERS, 24, 3 * D), F32), shape((LAYERS, 72), F32),
            shape((LAYERS, 24, D), F32), row_24,
            shape((LAYERS, 24, FF), F32), shape((LAYERS, 96), F32),
            shape((LAYERS, 96, D), F32), row_24, row_24, row_24, row_24,
        ],
        "unpack_gradients",
        [array for group in outs for array in group],
    )
    return (activations, grad, *final[:7], final[3], *final[7:])


def whole_mesh_solution(mesh):
    in_specs = (
        P(("dp", "cp"), None),
        P(("dp", "cp")),
        P(("dp", "cp"), None),
        P(None, ("dp", "cp"), None),
        P(None, ("dp", "cp")),
        P(None, ("dp", "cp"), None),
        P(None, ("dp", "cp")),
        P(None, ("dp", "cp"), None),
        P(None, ("dp", "cp")),
        P(None, ("dp", "cp"), None),
        P(None, ("dp", "cp")),
        P(None, ("dp", "cp")),
        P(None, ("dp", "cp")),
        P(None, ("dp", "cp")),
        P(None, ("dp", "cp")),
    )
    out_specs = (
        P(("dp", "cp"), None),
        P(("dp", "cp"), None),
        P(None, ("dp", "cp"), None),
        P(None, ("dp", "cp")),
        P(None, ("dp", "cp"), None),
        P(None, ("dp", "cp")),
        P(None, ("dp", "cp"), None),
        P(None, ("dp", "cp")),
        P(None, ("dp", "cp"), None),
        P(None, ("dp", "cp")),
        P(None, ("dp", "cp")),
        P(None, ("dp", "cp")),
        P(None, ("dp", "cp")),
        P(None, ("dp", "cp")),
    )
    return jax.shard_map(local, mesh=mesh, in_specs=in_specs, out_specs=out_specs, check_vma=False)


def solution(mesh):
    teams = mesh.shape["dp"] // 2
    if mesh.shape["cp"] != 2 or teams != 2 * LINE or teams * TEAM * 24 != D:
        return whole_mesh_solution(mesh)
    split_mesh = Mesh(mesh.devices.reshape(teams // 2, 2, 2, 2), ("z", "y", "core", "x"))
    every = ("z", "y", "core", "x")
    row = P(every, None)
    matrix, vector = P(None, every, None), P(None, every)
    in_specs = (row, P(every), row) + (matrix, vector) * 4 + (vector,) * 4
    out_specs = (row, row) + (matrix, vector) * 4 + (vector,) * 4
    return jax.shard_map(
        local_team, mesh=split_mesh, in_specs=in_specs, out_specs=out_specs, check_vma=False
    )
```

profile of v0, /device:TPU:5, one launch (start us, length us, event | category | flops | bytes accessed | tf_op | source)
XLA Modules:
  0.0 342.2 jit_solution(6238418268215032568)
XLA Ops:
  0.6 5.7 %collective-permute-start.3 = (bf16[2,24,768]{2,1,0:T(8,128)(2,1)}, bf16[2,24,768]{2,1,0:T(8,128)(2,1)S(1)}, u32[]{:S(2)}, u32[]{:S(2)}) collective-permute-start(bf16[2,24,768]{2,1,0:T(8,128)(2,1)} %param.20), channel_id=1, source_target_pairs={{0,0},{1,4},{2,8},{3,12},{4,16},{5,20},{6,24},{7,28},{8,1},{9,5},{... | collective-permute-start | bytes 221192 | tf_op jit(solution)/shard_map/ppermute | solution.py:997
  15.6 3.7 %collective-permute-done.2.p3 = bf16[112,768]{1,0:T(8,128)(2,1)S(1)} collective-permute-done((bf16[112,768]{1,0:T(8,128)(2,1)}, bf16[112,768]{1,0:T(8,128)(2,1)S(1)}, u32[]{:S(2)}, u32[]{:S(2)}) %collective-permute-start.2) | collective-permute-done | bytes 172064 | tf_op jit(solution)/shard_map/ppermute | solution.py:936
  25.5 9.2 %collective-permute-done.6.x3 = bf16[272,768]{1,0:T(8,128)(2,1)S(1)} collective-permute-done((bf16[272,768]{1,0:T(8,128)(2,1)S(1)}, bf16[272,768]{1,0:T(8,128)(2,1)S(1)}, u32[]{:S(2)}, u32[]{:S(2)}) %collective-permute-start.6) | collective-permute-done | bytes 417824 | tf_op jit(solution)/shard_map/ppermute | solution.py:936
  36.1 7.3 %collective-permute-done.4.x1 = bf16[272,768]{1,0:T(8,128)(2,1)S(1)} collective-permute-done((bf16[272,768]{1,0:T(8,128)(2,1)S(1)}, bf16[272,768]{1,0:T(8,128)(2,1)S(1)}, u32[]{:S(2)}, u32[]{:S(2)}) %collective-permute-start.4) | collective-permute-done | bytes 417824 | tf_op jit(solution)/shard_map/ppermute | solution.py:936
  43.9 24.0 %collective-permute-done.8.refs_2_.refs_10_ = bf16[304,768]{1,0:T(8,128)(2,1)S(1)} collective-permute-done((bf16[304,768]{1,0:T(8,128)(2,1)}, bf16[304,768]{1,0:T(8,128)(2,1)S(1)}, u32[]{:S(2)}, u32[]{:S(2)}) %collective-permute-start.8) | collective-permute-done | bytes 466976 | tf_op jit(solution)/shard_map/ppermute | solution.py:941
  74.6 4.4 %collective-permute-done.12.refs_6_.refs_14_ = bf16[304,768]{1,0:T(8,128)(2,1)S(1)} collective-permute-done((bf16[304,768]{1,0:T(8,128)(2,1)S(1)}, bf16[304,768]{1,0:T(8,128)(2,1)S(1)}, u32[]{:S(2)}, u32[]{:S(2)}) %collective-permute-start.12) | collective-permute-done | bytes 466976 | tf_op jit(solution)/shard_map/ppermute | solution.py:945
  79.1 10.0 %collective-permute-done.11.refs_5_.refs_13_ = bf16[304,768]{1,0:T(8,128)(2,1)S(1)} collective-permute-done((bf16[304,768]{1,0:T(8,128)(2,1)S(1)}, bf16[304,768]{1,0:T(8,128)(2,1)S(1)}, u32[]{:S(2)}, u32[]{:S(2)}) %collective-permute-start.11) | collective-permute-done | bytes 466976 | tf_op jit(solution)/shard_map/ppermute | solution.py:945
  89.8 6.2 %attend_forward.1 = (f32[512,768]{1,0:T(8,128)}, f32[2,8,768]{2,1,0:T(8,128)}) custom-call(s32[3]{0:T(128)} %pad_add_fusion.1.me_ref, bf16[272,768]{1,0:T(8,128)(2,1)} %copy-done.7, bf16[272,768]{1,0:T(8,128)(2,1)} %copy-done.10, bf16[272,768]{1,0:T(8,128)(2,1)} %copy-done.9, bf16[272,768]{1,0:T(8,128)(2,1)} %copy-done.8, ...), custom_call_target="tpu_custom_call" | custom-call | tf_op jit(solution)/shard_map/attend_forward/pallas_call | solution.py:970
  96.0 5.0 %mlp_forward.1 = (f32[128,768]{1,0:T(8,128)}, bf16[128,768]{1,0:T(8,128)(2,1)}, bf16[128,768]{1,0:T(8,128)(2,1)}, bf16[128,768]{1,0:T(8,128)(2,1)}) custom-call(s32[3]{0:T(128)} %pad_add_fusion.1.me_ref, bf16[272,768]{1,0:T(8,128)(2,1)} %copy-done.7, bf16[272,768]{1,0:T(8,128)(2,1)} %copy-done.10, bf16[272,768]{1,0:T(8,128)(2,1)} %copy-done.9, ...), custom_call_target="tpu_custom_call" | custom-call | tf_op jit(solution)/shard_map/mlp_forward/pallas_call | solution.py:970
  110.2 4.4 %collective-permute-done.16.y3 = bf16[128,768]{1,0:T(8,128)(2,1)S(1)} collective-permute-done((bf16[128,768]{1,0:T(8,128)(2,1)}, bf16[128,768]{1,0:T(8,128)(2,1)S(1)}, u32[]{:S(2)}, u32[]{:S(2)}) %collective-permute-start.16) | collective-permute-done | bytes 196640 | tf_op jit(solution)/shard_map/ppermute | solution.py:936
  118.8 5.8 %collective-permute-done.19.x3 = bf16[128,768]{1,0:T(8,128)(2,1)S(1)} collective-permute-done((bf16[128,768]{1,0:T(8,128)(2,1)}, bf16[128,768]{1,0:T(8,128)(2,1)S(1)}, u32[]{:S(2)}, u32[]{:S(2)}) %collective-permute-start.19) | collective-permute-done | bytes 196640 | tf_op jit(solution)/shard_map/ppermute | solution.py:936
  131.4 8.2 %collective-permute-done.24.refs_5_ = bf16[288,768]{1,0:T(8,128)(2,1)S(1)} collective-permute-done((bf16[288,768]{1,0:T(8,128)(2,1)S(1)}, bf16[288,768]{1,0:T(8,128)(2,1)S(1)}, u32[]{:S(2)}, u32[]{:S(2)}) %collective-permute-start.24) | collective-permute-done | bytes 442400 | tf_op jit(solution)/shard_map/ppermute | solution.py:945
  140.4 9.0 %mlp_both.2 = (bf16[4,192,768]{2,1,0:T(8,128)(2,1)}, bf16[4,192,768]{2,1,0:T(8,128)(2,1)}, f32[512,768]{1,0:T(8,128)}, f32[8,768]{1,0:T(8,128)}, f32[512,768]{1,0:T(8,128)}) custom-call(s32[3]{0:T(128)} %pad_add_fusion.1.me_ref, bf16[128,768]{1,0:T(8,128)(2,1)} %get-tuple-element.119.x0, bf16[128,768]{1,0:T(8,128)(2,1)} %copy-done.25, ...), custom_call_target="tpu_custom_call" | custom-call | tf_op jit(solution)/shard_map/mlp_both/pallas_call | solution.py:970
  149.5 11.9 %attend_both.2 = (bf16[4,112,768]{2,1,0:T(8,128)(2,1)}, bf16[4,112,768]{2,1,0:T(8,128)(2,1)}, f32[128,768]{1,0:T(8,128)}, bf16[128,768]{1,0:T(8,128)(2,1)}, bf16...) custom-call(s32[3]{0:T(128)} %pad_add_fusion.1.me_ref, ...), custom_call_target="tpu_custom_call" | custom-call | tf_op jit(solution)/shard_map/attend_both/pallas_call | solution.py:970
  165.1 4.1 %collective-permute-done.29.n3 = bf16[128,768]{1,0:T(8,128)(2,1)S(1)} collective-permute-done((bf16[128,768]{1,0:T(8,128)(2,1)}, bf16[128,768]{1,0:T(8,128)(2,1)S(1)}, u32[]{:S(2)}, u32[]{:S(2)}) %collective-permute-start.29) | collective-permute-done | bytes 196640 | tf_op jit(solution)/shard_map/ppermute | solution.py:936
  169.1 7.8 %collective-permute-done.30.received.refs_1_ = bf16[4,192,768]{2,1,0:T(8,128)(2,1)S(1)} collective-permute-done((bf16[4,192,768]{2,1,0:T(8,128)(2,1)}, bf16[4,192,768]{2,1,0:T(8,128)(2,1)S(1)}, u32[]{:S(2)}, u32[]{:S(2)}) %collective-permute-start.30) | collective-permute-done | bytes 1179680 | tf_op jit(solution)/shard_map/ppermute | solution.py:945
  189.1 4.3 %collective-permute-done.31.g3 = bf16[128,768]{1,0:T(8,128)(2,1)S(1)} collective-permute-done((bf16[128,768]{1,0:T(8,128)(2,1)}, bf16[128,768]{1,0:T(8,128)(2,1)S(1)}, u32[]{:S(2)}, u32[]{:S(2)}) %collective-permute-start.31) | collective-permute-done | bytes 196640 | tf_op jit(solution)/shard_map/ppermute | solution.py:936
  194.1 8.1 %mlp_both.3 = (bf16[4,192,768]{2,1,0:T(8,128)(2,1)}, bf16[4,192,768]{2,1,0:T(8,128)(2,1)}, f32[512,768]{1,0:T(8,128)}, f32[8,768]{1,0:T(8,128)}) custom-call(s32[3]{0:T(128)} %pad_add_fusion.1.me_ref, bf16[272,768]{1,0:T(8,128)(2,1)} %copy-done.7, bf16[272,768]{1,0:T(8,128)(2,1)} %copy-done.10, bf16[272,768]{1,0:T(8,128)(2,1)} %copy-done.9, ...), custom_call_target="tpu_custom_call" | custom-call | tf_op jit(solution)/shard_map/mlp_both/pallas_call | solution.py:970
  213.2 13.2 %collective-permute-done.39.refs_3_ = bf16[192,768]{1,0:T(8,128)(2,1)S(1)} collective-permute-done((bf16[192,768]{1,0:T(8,128)(2,1)S(1)}, bf16[192,768]{1,0:T(8,128)(2,1)S(1)}, u32[]{:S(2)}, u32[]{:S(2)}) %collective-permute-start.39) | collective-permute-done | bytes 294944 | tf_op jit(solution)/shard_map/ppermute | solution.py:941
  226.5 11.6 %attend_both.3 = (bf16[4,112,768]{2,1,0:T(8,128)(2,1)}, bf16[4,112,768]{2,1,0:T(8,128)(2,1)}, f32[128,768]{1,0:T(8,128)}, bf16[128,768]{1,0:T(8,128)(2,1)}, bf16...) custom-call(s32[3]{0:T(128)} %pad_add_fusion.1.me_ref, bf16[272,768]{1,0:T(8,128)(2,1)} %copy-done.7, ...), custom_call_target="tpu_custom_call" | custom-call | tf_op jit(solution)/shard_map/attend_both/pallas_call | solution.py:970
  238.3 6.5 %collective-permute-start.45 = (bf16[112,768]{1,0:T(8,128)(2,1)S(1)}, bf16[112,768]{1,0:T(8,128)(2,1)S(1)}, u32[]{:S(2)}, u32[]{:S(2)}) collective-permute-start(bf16[112,768]{1,0:T(8,128)(2,1)S(1)} %copy-done.79), channel_id=1, source_target_pairs={{0,8},{8,16},{16,24},{24,0},{1,9},{9,17},{17,25},{25,1},{2,10},{10... | collective-permute-start | bytes 516104 | tf_op jit(solution)/shard_map/ppermute | solution.py:941
  249.1 8.0 %collective-permute-done.46.refs_8_ = bf16[112,768]{1,0:T(8,128)(2,1)S(1)} collective-permute-done((bf16[112,768]{1,0:T(8,128)(2,1)S(1)}, bf16[112,768]{1,0:T(8,128)(2,1)S(1)}, u32[]{:S(2)}, u32[]{:S(2)}) %collective-permute-start.46) | collective-permute-done | bytes 172064 | tf_op jit(solution)/shard_map/ppermute | solution.py:941
  259.1 2.9 split_gradients.2
  268.7 3.8 %collective-permute-start.52 = (bf16[112,768]{1,0:T(8,128)(2,1)}, bf16[112,768]{1,0:T(8,128)(2,1)S(1)}, u32[]{:S(2)}, u32[]{:S(2)}) collective-permute-start(bf16[112,768]{1,0:T(8,128)(2,1)} %get-tuple-element.171), channel_id=1, source_target_pairs={{0,8},{8,16},{16,24},{24,0},{1,9},{9,17},{17,25},{25,1},{2,10},{10... | collective-permute-start | bytes 516104 | tf_op jit(solution)/shard_map/ppermute | solution.py:941
  272.6 5.5 %collective-permute-start.62 = (bf16[24,768]{1,0:T(8,128)(2,1)S(1)}, bf16[24,768]{1,0:T(8,128)(2,1)S(1)}, u32[]{:S(2)}, u32[]{:S(2)}) collective-permute-start(bf16[24,768]{1,0:T(8,128)(2,1)S(1)} %copy-done.83), channel_id=1, source_target_pairs={{0,0},{4,1},{8,2},{12,3},{16,4},{20,5},{24,6},{28,7},{1,8},{5,9},{... | collective-permute-start | bytes 110600 | tf_op jit(solution)/shard_map/ppermute | solution.py:1118
  280.0 7.0 %collective-permute-done.62.refs_12_ = bf16[24,768]{1,0:T(8,128)(2,1)S(1)} collective-permute-done((bf16[24,768]{1,0:T(8,128)(2,1)S(1)}, bf16[24,768]{1,0:T(8,128)(2,1)S(1)}, u32[]{:S(2)}, u32[]{:S(2)}) %collective-permute-start.62) | collective-permute-done | bytes 36896 | tf_op jit(solution)/shard_map/ppermute | solution.py:1118
  287.1 3.2 collective-permute-start.54
  290.3 21.7 %collective-permute-done.53.refs_8_ = bf16[112,768]{1,0:T(8,128)(2,1)S(1)} collective-permute-done((bf16[112,768]{1,0:T(8,128)(2,1)}, bf16[112,768]{1,0:T(8,128)(2,1)S(1)}, u32[]{:S(2)}, u32[]{:S(2)}) %collective-permute-start.53) | collective-permute-done | bytes 172064 | tf_op jit(solution)/shard_map/ppermute | solution.py:941
  316.5 2.9 split_gradients.3
  319.4 4.0 %collective-permute-done.59.refs_8_ = bf16[64,768]{1,0:T(8,128)(2,1)S(1)} collective-permute-done((bf16[64,768]{1,0:T(8,128)(2,1)S(1)}, bf16[64,768]{1,0:T(8,128)(2,1)S(1)}, u32[]{:S(2)}, u32[]{:S(2)}) %collective-permute-start.59) | collective-permute-done | bytes 98336 | tf_op jit(solution)/shard_map/ppermute | solution.py:936
  328.2 2.9 collective-permute-start.58
  337.6 2.9 unpack_gradients.1
  (303 shorter events, 105.0 us)
Async XLA Ops:
  24.2 19.1 %collective-permute-start.4 = (bf16[272,768]{1,0:T(8,128)(2,1)S(1)}, bf16[272,768]{1,0:T(8,128)(2,1)S(1)}, u32[]{:S(2)}, u32[]{:S(2)}) collective-permute-start(bf16[272,768]{1,0:T(8,128)(2,1)S(1)} %fusion.3.x0), channel_id=1, source_target_pairs={{0,1},{1,0},{2,3},{3,2},{4,5},{5,4},{6,7},{7,6},{8,9},{9,8},{10,11... | collective-permute-start | bytes 1253384 | tf_op jit(solution)/shard_map/ppermute | solution.py:936
  24.5 43.5 %collective-permute-start.10 = (bf16[304,768]{1,0:T(8,128)(2,1)}, bf16[304,768]{1,0:T(8,128)(2,1)S(1)}, u32[]{:S(2)}, u32[]{:S(2)}) collective-permute-start(bf16[304,768]{1,0:T(8,128)(2,1)} %get-tuple-element.110.refs_0_.refs_8_), channel_id=1, source_target_pairs={{0,4},{4,0},{1,5},{5,1},{2,6},{6,2},{3,7},{7,3},{8,12},{12,8},{9,1... | collective-permute-start | bytes 1400840 | tf_op jit(solution)/shard_map/ppermute | solution.py:945
  24.5 19.1 %collective-permute-start.9 = (bf16[304,768]{1,0:T(8,128)(2,1)}, bf16[304,768]{1,0:T(8,128)(2,1)S(1)}, u32[]{:S(2)}, u32[]{:S(2)}) collective-permute-start(bf16[304,768]{1,0:T(8,128)(2,1)} %get-tuple-element.110.refs_0_.refs_8_), channel_id=1, source_target_pairs={{0,24},{8,0},{16,8},{24,16},{1,25},{9,1},{17,9},{25,17},{2,26},{10... | collective-permute-start | bytes 1400840 | tf_op jit(solution)/shard_map/ppermute | solution.py:941
  34.7 33.3 %collective-permute-start.8 = (bf16[304,768]{1,0:T(8,128)(2,1)}, bf16[304,768]{1,0:T(8,128)(2,1)S(1)}, u32[]{:S(2)}, u32[]{:S(2)}) collective-permute-start(bf16[304,768]{1,0:T(8,128)(2,1)} %get-tuple-element.110.refs_0_.refs_8_), channel_id=1, source_target_pairs={{0,16},{8,24},{16,0},{24,8},{1,17},{9,25},{17,1},{25,9},{2,18},{10... | collective-permute-start | bytes 1400840 | tf_op jit(solution)/shard_map/ppermute | solution.py:941
  34.8 33.6 %collective-permute-start.7 = (bf16[304,768]{1,0:T(8,128)(2,1)}, bf16[304,768]{1,0:T(8,128)(2,1)S(1)}, u32[]{:S(2)}, u32[]{:S(2)}) collective-permute-start(bf16[304,768]{1,0:T(8,128)(2,1)} %get-tuple-element.110.refs_0_.refs_8_), channel_id=1, source_target_pairs={{0,8},{8,16},{16,24},{24,0},{1,9},{9,17},{17,25},{25,1},{2,10},{10... | collective-permute-start | bytes 1400840 | tf_op jit(solution)/shard_map/ppermute | solution.py:941
  43.7 26.9 %collective-permute-start.13 = (bf16[304,768]{1,0:T(8,128)(2,1)S(1)}, bf16[304,768]{1,0:T(8,128)(2,1)S(1)}, u32[]{:S(2)}, u32[]{:S(2)}) collective-permute-start(bf16[304,768]{1,0:T(8,128)(2,1)S(1)} %collective-permute-done.9.refs_3_.refs_11_), channel_id=1, source_target_pairs={{0,4},{4,0},{1,5},{5,1},{2,6},{6,2},{3,7},{7,3},{8,12},{12,8},{9,1... | collective-permute-start | bytes 1400840 | tf_op jit(solution)/shard_map/ppermute | solution.py:945
  68.0 35.5 %collective-permute-start.22 = (bf16[288,768]{1,0:T(8,128)(2,1)}, bf16[288,768]{1,0:T(8,128)(2,1)S(1)}, u32[]{:S(2)}, u32[]{:S(2)}) collective-permute-start(bf16[288,768]{1,0:T(8,128)(2,1)} %get-tuple-element.121.refs_0_), channel_id=1, source_target_pairs={{0,24},{8,0},{16,8},{24,16},{1,25},{9,1},{17,9},{25,17},{2,26},{10... | collective-permute-start | bytes 1327112 | tf_op jit(solution)/shard_map/ppermute | solution.py:941
  68.0 38.1 %collective-permute-start.21 = (bf16[288,768]{1,0:T(8,128)(2,1)}, bf16[288,768]{1,0:T(8,128)(2,1)S(1)}, u32[]{:S(2)}, u32[]{:S(2)}) collective-permute-start(bf16[288,768]{1,0:T(8,128)(2,1)} %get-tuple-element.121.refs_0_), channel_id=1, source_target_pairs={{0,16},{8,24},{16,0},{24,8},{1,17},{9,25},{17,1},{25,9},{2,18},{10... | collective-permute-start | bytes 1327112 | tf_op jit(solution)/shard_map/ppermute | solution.py:941
  68.4 20.6 %collective-permute-start.11 = (bf16[304,768]{1,0:T(8,128)(2,1)S(1)}, bf16[304,768]{1,0:T(8,128)(2,1)S(1)}, u32[]{:S(2)}, u32[]{:S(2)}) collective-permute-start(bf16[304,768]{1,0:T(8,128)(2,1)S(1)} %collective-permute-done.7.refs_1_.refs_9_), channel_id=1, source_target_pairs={{0,4},{4,0},{1,5},{5,1},{2,6},{6,2},{3,7},{7,3},{8,12},{12,8},{9,1... | collective-permute-start | bytes 1400840 | tf_op jit(solution)/shard_map/ppermute | solution.py:945
  70.6 38.1 %collective-permute-start.20 = (bf16[288,768]{1,0:T(8,128)(2,1)}, bf16[288,768]{1,0:T(8,128)(2,1)S(1)}, u32[]{:S(2)}, u32[]{:S(2)}) collective-permute-start(bf16[288,768]{1,0:T(8,128)(2,1)} %get-tuple-element.121.refs_0_), channel_id=1, source_target_pairs={{0,8},{8,16},{16,24},{24,0},{1,9},{9,17},{17,25},{25,1},{2,10},{10... | collective-permute-start | bytes 1327112 | tf_op jit(solution)/shard_map/ppermute | solution.py:941
  79.0 39.7 %collective-permute-start.23 = (bf16[288,768]{1,0:T(8,128)(2,1)S(1)}, bf16[288,768]{1,0:T(8,128)(2,1)S(1)}, u32[]{:S(2)}, u32[]{:S(2)}) collective-permute-start(bf16[288,768]{1,0:T(8,128)(2,1)S(1)} %copy-done.15), channel_id=1, source_target_pairs={{0,4},{4,0},{1,5},{5,1},{2,6},{6,2},{3,7},{7,3},{8,12},{12,8},{9,1... | collective-permute-start | bytes 1327112 | tf_op jit(solution)/shard_map/ppermute | solution.py:945
  108.7 22.7 %collective-permute-start.26 = (bf16[288,768]{1,0:T(8,128)(2,1)S(1)}, bf16[288,768]{1,0:T(8,128)(2,1)S(1)}, u32[]{:S(2)}, u32[]{:S(2)}) collective-permute-start(bf16[288,768]{1,0:T(8,128)(2,1)S(1)} %collective-permute-done.22.refs_3_), channel_id=1, source_target_pairs={{0,4},{4,0},{1,5},{5,1},{2,6},{6,2},{3,7},{7,3},{8,12},{12,8},{9,1... | collective-permute-start | bytes 1327112 | tf_op jit(solution)/shard_map/ppermute | solution.py:945
  108.7 22.7 %collective-permute-start.25 = (bf16[288,768]{1,0:T(8,128)(2,1)S(1)}, bf16[288,768]{1,0:T(8,128)(2,1)S(1)}, u32[]{:S(2)}, u32[]{:S(2)}) collective-permute-start(bf16[288,768]{1,0:T(8,128)(2,1)S(1)} %collective-permute-done.21.refs_2_), channel_id=1, source_target_pairs={{0,4},{4,0},{1,5},{5,1},{2,6},{6,2},{3,7},{7,3},{8,12},{12,8},{9,1... | collective-permute-start | bytes 1327112 | tf_op jit(solution)/shard_map/ppermute | solution.py:945
  110.2 29.5 %collective-permute-start.24 = (bf16[288,768]{1,0:T(8,128)(2,1)S(1)}, bf16[288,768]{1,0:T(8,128)(2,1)S(1)}, u32[]{:S(2)}, u32[]{:S(2)}) collective-permute-start(bf16[288,768]{1,0:T(8,128)(2,1)S(1)} %collective-permute-done.20.refs_1_), channel_id=1, source_target_pairs={{0,4},{4,0},{1,5},{5,1},{2,6},{6,2},{3,7},{7,3},{8,12},{12,8},{9,1... | collective-permute-start | bytes 1327112 | tf_op jit(solution)/shard_map/ppermute | solution.py:945
  149.5 27.4 %collective-permute-start.30 = (bf16[4,192,768]{2,1,0:T(8,128)(2,1)}, bf16[4,192,768]{2,1,0:T(8,128)(2,1)S(1)}, u32[]{:S(2)}, u32[]{:S(2)}) collective-permute-start(bf16[4,192,768]{2,1,0:T(8,128)(2,1)} %get-tuple-element.131), channel_id=1, source_target_pairs={{0,4},{4,0},{1,5},{5,1},{2,6},{6,2},{3,7},{7,3},{8,12},{12,8},{9,1... | collective-permute-start | bytes 3538952 | tf_op jit(solution)/shard_map/ppermute | solution.py:945
  162.6 14.3 %collective-permute-start.27 = (bf16[128,768]{1,0:T(8,128)(2,1)}, bf16[128,768]{1,0:T(8,128)(2,1)S(1)}, u32[]{:S(2)}, u32[]{:S(2)}) collective-permute-start(bf16[128,768]{1,0:T(8,128)(2,1)} %get-tuple-element.128), channel_id=1, source_target_pairs={{0,1},{1,0},{2,3},{3,2},{4,5},{5,4},{6,7},{7,6},{8,9},{9,8},{10,11... | collective-permute-start | bytes 589832 | tf_op jit(solution)/shard_map/ppermute | solution.py:936
  163.7 43.8 %collective-permute-start.37 = (bf16[4,112,768]{2,1,0:T(8,128)(2,1)}, bf16[4,112,768]{2,1,0:T(8,128)(2,1)S(1)}, u32[]{:S(2)}, u32[]{:S(2)}) collective-permute-start(bf16[4,112,768]{2,1,0:T(8,128)(2,1)} %get-tuple-element.149), channel_id=1, source_target_pairs={{0,4},{4,0},{1,5},{5,1},{2,6},{6,2},{3,7},{7,3},{8,12},{12,8},{9,1... | collective-permute-start | bytes 2064392 | tf_op jit(solution)/shard_map/ppermute | solution.py:945
  202.2 59.8 %collective-permute-start.44 = (bf16[4,192,768]{2,1,0:T(8,128)(2,1)}, bf16[4,192,768]{2,1,0:T(8,128)(2,1)S(1)}, u32[]{:S(2)}, u32[]{:S(2)}) collective-permute-start(bf16[4,192,768]{2,1,0:T(8,128)(2,1)} %get-tuple-element.162), channel_id=1, source_target_pairs={{0,4},{4,0},{1,5},{5,1},{2,6},{6,2},{3,7},{7,3},{8,12},{12,8},{9,1... | collective-permute-start | bytes 3538952 | tf_op jit(solution)/shard_map/ppermute | solution.py:945
  204.0 22.4 %collective-permute-start.39 = (bf16[192,768]{1,0:T(8,128)(2,1)S(1)}, bf16[192,768]{1,0:T(8,128)(2,1)S(1)}, u32[]{:S(2)}, u32[]{:S(2)}) collective-permute-start(bf16[192,768]{1,0:T(8,128)(2,1)S(1)} %copy-done.69), channel_id=1, source_target_pairs={{0,16},{8,24},{16,0},{24,8},{1,17},{9,25},{17,1},{25,9},{2,18},{10... | collective-permute-start | bytes 884744 | tf_op jit(solution)/shard_map/ppermute | solution.py:941
  206.6 19.9 %collective-permute-start.40 = (bf16[192,768]{1,0:T(8,128)(2,1)S(1)}, bf16[192,768]{1,0:T(8,128)(2,1)S(1)}, u32[]{:S(2)}, u32[]{:S(2)}) collective-permute-start(bf16[192,768]{1,0:T(8,128)(2,1)S(1)} %copy-done.68), channel_id=1, source_target_pairs={{0,24},{8,0},{16,8},{24,16},{1,25},{9,1},{17,9},{25,17},{2,26},{10... | collective-permute-start | bytes 884744 | tf_op jit(solution)/shard_map/ppermute | solution.py:941
  238.2 27.6 %collective-permute-start.51 = (bf16[4,112,768]{2,1,0:T(8,128)(2,1)}, bf16[4,112,768]{2,1,0:T(8,128)(2,1)S(1)}, u32[]{:S(2)}, u32[]{:S(2)}) collective-permute-start(bf16[4,112,768]{2,1,0:T(8,128)(2,1)} %get-tuple-element.169), channel_id=1, source_target_pairs={{0,4},{4,0},{1,5},{5,1},{2,6},{6,2},{3,7},{7,3},{8,12},{12,8},{9,1... | collective-permute-start | bytes 2064392 | tf_op jit(solution)/shard_map/ppermute | solution.py:945
  247.5 25.0 %collective-permute-start.32 = (bf16[128,768]{1,0:T(8,128)(2,1)S(1)}, bf16[128,768]{1,0:T(8,128)(2,1)S(1)}, u32[]{:S(2)}, u32[]{:S(2)}) collective-permute-start(bf16[128,768]{1,0:T(8,128)(2,1)S(1)} %copy-done.73), channel_id=1, source_target_pairs={{0,1},{1,0},{2,3},{3,2},{4,5},{5,4},{6,7},{7,6},{8,9},{9,8},{10,11... | collective-permute-start | bytes 589832 | tf_op jit(solution)/shard_map/ppermute | solution.py:936
  257.1 21.0 %collective-permute-start.33 = (bf16[128,768]{1,0:T(8,128)(2,1)S(1)}, bf16[128,768]{1,0:T(8,128)(2,1)S(1)}, u32[]{:S(2)}, u32[]{:S(2)}) collective-permute-start(bf16[128,768]{1,0:T(8,128)(2,1)S(1)} %copy-done.72), channel_id=1, source_target_pairs={{0,2},{1,3},{2,0},{3,1},{4,6},{5,7},{6,4},{7,5},{8,10},{9,11},{10,... | collective-permute-start | bytes 589832 | tf_op jit(solution)/shard_map/ppermute | solution.py:936
  257.7 20.5 %collective-permute-start.34 = (bf16[128,768]{1,0:T(8,128)(2,1)S(1)}, bf16[128,768]{1,0:T(8,128)(2,1)S(1)}, u32[]{:S(2)}, u32[]{:S(2)}) collective-permute-start(bf16[128,768]{1,0:T(8,128)(2,1)S(1)} %copy-done.71), channel_id=1, source_target_pairs={{0,3},{1,2},{2,1},{3,0},{4,7},{5,6},{6,5},{7,4},{8,11},{9,10},{10,... | collective-permute-start | bytes 589832 | tf_op jit(solution)/shard_map/ppermute | solution.py:936
  268.7 18.3 %collective-permute-start.52 = (bf16[112,768]{1,0:T(8,128)(2,1)}, bf16[112,768]{1,0:T(8,128)(2,1)S(1)}, u32[]{:S(2)}, u32[]{:S(2)}) collective-permute-start(bf16[112,768]{1,0:T(8,128)(2,1)} %get-tuple-element.171), channel_id=1, source_target_pairs={{0,8},{8,16},{16,24},{24,0},{1,9},{9,17},{17,25},{25,1},{2,10},{10... | collective-permute-start | bytes 516104 | tf_op jit(solution)/shard_map/ppermute | solution.py:941
  272.5 41.6 %collective-permute-start.48 = (bf16[192,768]{1,0:T(8,128)(2,1)S(1)}, bf16[192,768]{1,0:T(8,128)(2,1)S(1)}, u32[]{:S(2)}, u32[]{:S(2)}) collective-permute-start(bf16[192,768]{1,0:T(8,128)(2,1)S(1)} %copy-done.67), channel_id=1, source_target_pairs={{0,8},{8,16},{16,24},{24,0},{1,9},{9,17},{17,25},{25,1},{2,10},{10... | collective-permute-start | bytes 884744 | tf_op jit(solution)/shard_map/ppermute | solution.py:941
  272.6 14.4 %collective-permute-start.62 = (bf16[24,768]{1,0:T(8,128)(2,1)S(1)}, bf16[24,768]{1,0:T(8,128)(2,1)S(1)}, u32[]{:S(2)}, u32[]{:S(2)}) collective-permute-start(bf16[24,768]{1,0:T(8,128)(2,1)S(1)} %copy-done.83), channel_id=1, source_target_pairs={{0,0},{4,1},{8,2},{12,3},{16,4},{20,5},{24,6},{28,7},{1,8},{5,9},{... | collective-permute-start | bytes 110600 | tf_op jit(solution)/shard_map/ppermute | solution.py:1118
  278.1 36.7 %collective-permute-start.49 = (bf16[192,768]{1,0:T(8,128)(2,1)S(1)}, bf16[192,768]{1,0:T(8,128)(2,1)S(1)}, u32[]{:S(2)}, u32[]{:S(2)}) collective-permute-start(bf16[192,768]{1,0:T(8,128)(2,1)S(1)} %copy-done.66), channel_id=1, source_target_pairs={{0,16},{8,24},{16,0},{24,8},{1,17},{9,25},{17,1},{25,9},{2,18},{10... | collective-permute-start | bytes 884744 | tf_op jit(solution)/shard_map/ppermute | solution.py:941
  278.2 37.4 %collective-permute-start.50 = (bf16[192,768]{1,0:T(8,128)(2,1)S(1)}, bf16[192,768]{1,0:T(8,128)(2,1)S(1)}, u32[]{:S(2)}, u32[]{:S(2)}) collective-permute-start(bf16[192,768]{1,0:T(8,128)(2,1)S(1)} %copy-done.65), channel_id=1, source_target_pairs={{0,24},{8,0},{16,8},{24,16},{1,25},{9,1},{17,9},{25,17},{2,26},{10... | collective-permute-start | bytes 884744 | tf_op jit(solution)/shard_map/ppermute | solution.py:941
  287.0 25.0 %collective-permute-start.53 = (bf16[112,768]{1,0:T(8,128)(2,1)}, bf16[112,768]{1,0:T(8,128)(2,1)S(1)}, u32[]{:S(2)}, u32[]{:S(2)}) collective-permute-start(bf16[112,768]{1,0:T(8,128)(2,1)} %get-tuple-element.172), channel_id=1, source_target_pairs={{0,16},{8,24},{16,0},{24,8},{1,17},{9,25},{17,1},{25,9},{2,18},{10... | collective-permute-start | bytes 516104 | tf_op jit(solution)/shard_map/ppermute | solution.py:941
  287.1 25.7 %collective-permute-start.54 = (bf16[112,768]{1,0:T(8,128)(2,1)}, bf16[112,768]{1,0:T(8,128)(2,1)S(1)}, u32[]{:S(2)}, u32[]{:S(2)}) collective-permute-start(bf16[112,768]{1,0:T(8,128)(2,1)} %get-tuple-element.173), channel_id=1, source_target_pairs={{0,24},{8,0},{16,8},{24,16},{1,25},{9,1},{17,9},{25,17},{2,26},{10... | collective-permute-start | bytes 516104 | tf_op jit(solution)/shard_map/ppermute | solution.py:941
  312.0 15.0 %collective-permute-start.41 = (bf16[128,768]{1,0:T(8,128)(2,1)S(1)}, bf16[128,768]{1,0:T(8,128)(2,1)S(1)}, u32[]{:S(2)}, u32[]{:S(2)}) collective-permute-start(bf16[128,768]{1,0:T(8,128)(2,1)S(1)} %copy-done.76), channel_id=1, source_target_pairs={{0,1},{1,0},{2,3},{3,2},{4,5},{5,4},{6,7},{7,6},{8,9},{9,8},{10,11... | collective-permute-start | bytes 589832 | tf_op jit(solution)/shard_map/ppermute | solution.py:936
  (115 other events, 1620.3 us)
where the time goes:
time: 349 us; the launch traced here: 342 us
  waiting for transfers between devices  157 us (45%)
  Pallas kernels  84.6 us (24%)
  starting transfers between devices  78.1 us (22%)
  local copies, waits for them, and re-layouts  14.1 us (4%)
  other arithmetic  6.13 us (2%)
    pallas_call x15, Pallas kernels, run(): pl.pallas_call(body, grid=(1,), out_shape=out_shape, in_specs=[pl.BlockSp...  75 us
    ppermute x18, waiting for transfers between devices, line_shift(): lax.ppermute(piece, 'z', [(i, (i + shift) % size) for i in range(size)])  70.3 us
    ppermute x30, waiting for transfers between devices, team_send(): return lax.ppermute(piece, TEAM_AXES, flips)  48.6 us
    ppermute x30, starting transfers between devices, team_send(): return lax.ppermute(piece, TEAM_AXES, flips)  32.5 us
    ppermute x12, waiting for transfers between devices, line_flip(): return lax.ppermute(piece, 'y', [(0, 1), (1, 0)])  30.5 us
    ppermute x18, starting transfers between devices, line_shift(): lax.ppermute(piece, 'z', [(i, (i + shift) % size) for i in range(size)])  26.6 us
    pallas_call x4, Pallas kernels, call(): pl.pallas_call(body, out_shape=out_shape, scratch_shapes=list(scratch), c...  9.65 us
    unnamed x169, local copies, waits for them, and re-layouts  9.27 us
  transfers between devices with their start and end apart: 63, of which 23 were waited for; matrix products, arithmetic and copies ran while one was open for 3% of the time, Pallas kernels for 21%

commit v1 on v0

--- a/solution.py
+++ b/solution.py
@@ -570,15 +570,27 @@
         whole[source_team(me_ref, index)] = piece[...]
 
 
-def hand_out(me_ref, whole, keep, send):
+def hand_out(me_ref, whole, keep, sends, order):
     for s in range(LINE):
         keep[s] = whole[target_team(me_ref, s)]
-        send[s] = whole[target_team(me_ref, LINE + s)]
-
-
-def add_body(me_ref, keep, received, *outs):
-    for s, out in enumerate(outs):
-        out[...] = (keep[s + 1].astype(F32) + received[s + 1].astype(F32)).astype(BF)
+    for send, slots in zip(sends, order):
+        for n, s in enumerate(slots):
+            send[n] = whole[target_team(me_ref, LINE + s)]
+
+
+ALL_SLOTS = (tuple(range(LINE)),)
+HALVES = ((1, 3), (2, 0))
+
+
+def add_body(slots, places, me_ref, keep, received, *outs):
+    for s, n, out in zip(slots, places, outs):
+        out[...] = (keep[s].astype(F32) + received[n].astype(F32)).astype(BF)
+
+
+def line_sum_body(me_ref, own, r1, r2, r3, keep_ref, send_ref):
+    for f, out in enumerate((keep_ref, send_ref)):
+        total = own[f].astype(F32) + r1[f].astype(F32) + r2[f].astype(F32) + r3[f].astype(F32)
+        out[...] = total.astype(out.dtype)
 
 
 def layer_vectors(me_ref, whole, depth):
@@ -652,26 +664,34 @@
         y_ref[rows, :] = mm(total.astype(BF), out_weight)
 
 
+def store_pair(g, result, own, near, far):
+    if g == 0:
+        own[...] = result[0:TOK]
+        near[...] = result[TOK:]
+    else:
+        far[...] = result.astype(BF)
+
+
 def mlp_body(me_ref, x0, x1, x2, x3, *refs):
-    pieces, (vec_ref, a_ref, y0, y1, y2, y3, whole) = refs[:8], refs[8:]
+    pieces, (vec_ref, a_ref, y0, y1, y23, whole) = refs[:8], refs[8:]
     place(me_ref, pieces, whole)
     vec = vec_ref[0]
     up = whole[:, 0:96, :].reshape(D, UCOLS)
     down = whole[:, 96:192, :].reshape(UCOLS, D)
-    for g, (first, second, y_first, y_second) in enumerate(((x0, x1, y0, y1), (x2, x3, y2, y3))):
+    for g, (first, second) in enumerate(((x0, x1), (x2, x3))):
         rows = pl.ds(PAIR * g, PAIR)
         scaled, _ = norm_parts(two_slots(first[...], second[...]))
         normed = (scaled * vec[2:3] + vec[3:4]).astype(BF)
         before = mm(normed, up) + vec[6:7]
         hidden = (before * (0.5 * (1.0 + lax.erf(before * (1.0 / math.sqrt(2.0)))))).astype(BF)
         result = mm(hidden, down) + a_ref[rows, :]
-        y_first[...] = result[0:TOK].astype(y_first.dtype)
-        y_second[...] = result[TOK:].astype(y_second.dtype)
+        store_pair(g, result, y0, y1, y23)
 
 
 def mlp_both_body(depth, last, me_ref, x0, x1, x2, x3, g0, g1, g2, g3, *refs):
-    pieces, vec_ref, blocks = refs[:8], refs[8], refs[9:11]
-    dn_ref, sum_ref = refs[11:13]
+    pieces, vec_ref, (dn_ref, sum_ref), refs = refs[:8], refs[8], refs[9:11], refs[11:]
+    if last:
+        y_ref, refs = refs[0], refs[1:]
     whole, grads, c_s, hid_s, du_s, gb_s = refs[-6:]
     place(me_ref, pieces, whole)
     vec = vec_ref[depth]
@@ -692,7 +712,7 @@
         hidden = hidden.astype(BF)
         hid_s[rows, :] = hidden
         if last:
-            refs[13][rows, :] = mm(hidden, down)
+            y_ref[rows, :] = mm(hidden, down)
         du = (mm_t(low, down) * slope).astype(BF)
         du_s[rows, :] = du
         dc = mm_t(du, up)
@@ -703,7 +723,16 @@
         up_sum = up_sum + jnp.sum(du.astype(F32), axis=0, keepdims=True)
     grads[:, 0:96, :] = t_mm(c_s[...], du_s[...]).reshape(-1, 96, UCOLS).astype(BF)
     grads[:, 96:192, :] = t_mm(hid_s[...], gb_s[...]).reshape(-1, 96, D).astype(BF)
-    hand_out(me_ref, grads, *blocks)
+    if last:
+        for s, out in enumerate(refs[0:LINE]):
+            for f in range(2):
+                out[f] = grads[target_team(me_ref, LINE * f + s), 0:EARLY, :]
+        keep, send = refs[LINE : LINE + 2]
+        for s in range(LINE):
+            keep[s] = grads[target_team(me_ref, s), EARLY:192, :]
+            send[s] = grads[target_team(me_ref, LINE + s), EARLY:192, :]
+    else:
+        hand_out(me_ref, grads, refs[0], refs[1:3], HALVES)
     sum_ref[...] = jnp.concatenate(
         [bias_sum, up_sum, gain_sum, shift_sum, jnp.zeros((4, D), F32)], axis=0
     )
@@ -714,7 +743,7 @@
     refs = refs[14:]
     if last:
         y_ref, refs = refs[0], refs[1:]
-    blocks, (n0, n1, n2, n3) = refs[:2], refs[2:6]
+    blocks, (n0, n1, n23) = refs[:2], refs[2:5]
     whole, grads, a_s, dp_s, o_s, gb_s = refs[-6:]
     place(me_ref, pieces, whole)
     vec = vec_ref[depth]
@@ -722,9 +751,7 @@
     gain_sum = jnp.zeros((1, D), F32)
     shift_sum = jnp.zeros((1, D), F32)
     bias_sum = jnp.zeros((1, MINE), F32)
-    for g, (first, second, g_first, g_second, n_first, n_second) in enumerate(
-        ((x0, x1, g0, g1, n0, n1), (x2, x3, g2, g3, n2, n3))
-    ):
+    for g, (first, second, g_first, g_second) in enumerate(((x0, x1, g0, g1), (x2, x3, g2, g3))):
         rows = pl.ds(PAIR * g, PAIR)
         cosine, sine = cos_ref[rows, :], sin_ref[rows, :]
         scaled, _ = norm_parts(two_slots(first[...], second[...]))
@@ -760,13 +787,10 @@
         gain_sum = gain_sum + jnp.sum(da * scaled, axis=0, keepdims=True)
         shift_sum = shift_sum + jnp.sum(da, axis=0, keepdims=True)
         dn = dn_ref[rows, :] + da * vec[0:1]
-        n_first[...] = dn[0:TOK].astype(n_first.dtype)
-        n_second[...] = dn[TOK:].astype(n_second.dtype)
+        store_pair(g, dn, n0, n1, n23)
         if last:
             result = y_ref[rows, :] + mm(out.astype(BF), out_weight)
-            y_first, y_second = refs[6 + 2 * g], refs[7 + 2 * g]
-            y_first[...] = result[0:TOK].astype(y_first.dtype)
-            y_second[...] = result[TOK:].astype(y_second.dtype)
+            store_pair(g, result, *refs[5:8])
     qkv_grad = t_mm(a_s[...], dp_s[...]).reshape(-1, 96, MINE)
     out_grad = t_mm(o_s[...], gb_s[...])
     side = jnp.concatenate(
@@ -792,12 +816,12 @@
             [spread[:, 288 * k : 288 * (k + 1)], jnp.zeros((1, D - 288), F32)], axis=1
         )
         grads[k, 96:112, :] = jnp.concatenate([shared, bias, jnp.zeros((9, D), F32)], axis=0).astype(BF)
-    hand_out(me_ref, grads, *blocks)
-
-
-def residual_body(x_ref, y0, y1, y2, y3, vec_ref, out_ref, low_ref):
+    hand_out(me_ref, grads, blocks[0], blocks[1:], ALL_SLOTS)
+
+
+def residual_body(me_ref, x_ref, y0, y1, y2, vec_ref, out_ref, low_ref):
     depth = 0 if x_ref.dtype == BF else 1
-    total = y0[...] + y1[...].astype(F32) + y2[...].astype(F32) + y3[...].astype(F32)
+    total = y0[...] + y1[...].astype(F32) + y2[...].astype(F32)
     result = x_ref[...].astype(F32) + total + (vec_ref[depth, 4:5] + vec_ref[depth, 5:6])
     out_ref[...] = result
     low_ref[...] = result.astype(BF)
@@ -814,6 +838,7 @@
 
 
 TOK = 128
+EARLY = 48
 PAIR = 2 * TOK
 
 
@@ -840,9 +865,9 @@
     return u * cdf, cdf + u * density
 
 
-def norm_back_body(x_ref, g_ref, n0, n1, n2, n3, out_ref, low_ref):
+def norm_back_body(me_ref, x_ref, g_ref, n0, n1, n2, out_ref, low_ref):
     scaled, inverse = norm_parts(x_ref[...].astype(F32))
-    dn = n0[...] + n1[...].astype(F32) + n2[...].astype(F32) + n3[...].astype(F32)
+    dn = n0[...] + n1[...].astype(F32) + n2[...].astype(F32)
     centered = dn - jnp.mean(dn, axis=-1, keepdims=True)
     moment = jnp.mean(dn * scaled, axis=-1, keepdims=True)
     result = g_ref[...].astype(F32) + inverse * (centered - scaled * moment)
@@ -850,19 +875,40 @@
     low_ref[...] = result.astype(BF)
 
 
-def split_body(me_ref, *refs):
+def total(group):
+    result = group[0].astype(F32)
+    for term in group[1:]:
+        result = result + term.astype(F32)
+    return result
+
+
+def by_owner(me_ref, parts, outs, start):
     me = me_ref[0]
-
-    def total(group):
-        result = group[0][0].astype(F32) + group[1][0].astype(F32)
-        for ref in group[2:]:
-            result = result + ref[...].astype(F32)
-        return result
-
-    mlp, attn = total(refs[0:5]), total(refs[5:10])
-    outs, (down_ref, attn_ref, small_ref) = refs[10:14], refs[14:]
-    up = mlp[0:96]
-    down_ref[...] = mlp[96:192]
+    for s, out in enumerate(outs):
+        piece = parts[0]
+        for p in range(1, TEAM):
+            piece = jnp.where((me ^ s) == p, parts[p], piece)
+        out[start : start + 32] = piece.astype(BF)
+
+
+def split_body(early, me_ref, *refs):
+    outs, (down_ref, attn_ref, small_ref), refs = refs[-7:-3], refs[-3:], refs[:-7]
+    split_attend(me_ref, refs[:5], outs, attn_ref, small_ref)
+    refs = refs[5:]
+    rest = total([refs[0][0], refs[1][0], refs[2][...], refs[3][...], refs[4][...]])
+    if early:
+        rest = jnp.concatenate([total([refs[5][...], refs[6][...]]), rest], axis=0)
+    down_ref[...] = rest[96:192]
+    blank = jnp.zeros((8, D), F32)
+    parts = [
+        jnp.concatenate([rest[24 * p : 24 * (p + 1)], blank], axis=0) for p in range(TEAM)
+    ]
+    by_owner(me_ref, parts, outs, 0)
+
+
+def split_attend(me_ref, refs, outs, attn_ref, small_ref):
+    me = me_ref[0]
+    attn = total([refs[0][0], refs[1][0], refs[2][...], refs[3][...], refs[4][...]])
     side = attn[0:96, MINE:]
     attn_ref[...] = jnp.concatenate(
         [side[24 * n : 24 * (n + 1)] for n in range(4)], axis=1
@@ -876,9 +922,7 @@
         qkv_bias = jnp.concatenate(
             [small[6:7, 72 * p : 72 * (p + 1)], jnp.zeros((1, D - 72), F32)], axis=1
         )
-        parts.append(
-            jnp.concatenate([up[rows], qkv[rows], gains, qkv_bias, jnp.zeros((11, D), F32)], axis=0)
-        )
+        parts.append(jnp.concatenate([qkv[rows], gains, qkv_bias, jnp.zeros((3, D), F32)], axis=0))
         bias = jnp.where(me == p, small[0:1, rows], bias)
     small_ref[...] = jnp.concatenate(
         [
@@ -888,11 +932,7 @@
         ],
         axis=0,
     )
-    for s, out in enumerate(outs):
-        piece = parts[0]
-        for p in range(1, TEAM):
-            piece = jnp.where((me ^ s) == p, parts[p], piece)
-        out[...] = piece.astype(BF)
+    by_owner(me_ref, parts, outs, 32)
 
 
 def unpack_body(me_ref, *refs):
@@ -904,8 +944,8 @@
     gain_refs = (ga_ref, sa_ref, gm_ref, sm_ref)
     for depth in range(LAYERS):
         group = refs[7 * depth : 7 * (depth + 1)]
+        down_rows, own_small, attn_rows = group[TEAM:]
         slots = [r[...].astype(F32) for r in group[:TEAM]]
-        own_small, attn_rows, down_rows = group[TEAM:]
         ordered = [pick(me, slots, p) for p in range(TEAM)]
         blocks = FF // (96 * TEAM)
         up_ref[depth] = jnp.concatenate(
@@ -914,7 +954,7 @@
         )
         qkv_ref[depth] = jnp.concatenate(
             [
-                ordered[p][24:48, HCOLS * t : HCOLS * (t + 1)]
+                ordered[p][32:56, HCOLS * t : HCOLS * (t + 1)]
                 for t in range(3)
                 for p in range(TEAM)
             ],
@@ -922,8 +962,8 @@
         )
         attn_ref[depth] = attn_rows[...].astype(F32)
         down_ref[depth] = down_rows[...]
-        small = slots[0][48:56, :128] + slots[1][48:56, :128]
-        small = small + slots[2][48:56, :128] + slots[3][48:56, :128]
+        small = slots[0][56:64, :128] + slots[1][56:64, :128]
+        small = small + slots[2][56:64, :128] + slots[3][56:64, :128]
         for n, ref in enumerate(gain_refs):
             ref[depth : depth + 1] = small[n : n + 1, :24]
         qkv_b_ref[depth : depth + 1] = small[4:5, :72]
@@ -950,7 +990,9 @@
 
 
 def line_near(piece):
-    return [piece] + [line_shift(piece, s) for s in range(1, LINE)]
+    first = line_shift(piece, 1)
+    third = line_shift(piece, 3)
+    return [piece, first, line_shift(after(piece, first, third), 2), third]
 
 
 def local_team(
@@ -1003,24 +1045,45 @@
     )
     near = line_near(chunks[0])
     pieces = [near + [line_flip(p) for p in near]]
-    near = line_near(after(chunks[1], near[2]))
+    near = line_near(after(chunks[1], near[2], pieces[0][5], pieces[0][7]))
     pieces.append(near + [line_flip(p) for p in near])
     m_parts = [[(p, part(192, 0)) for p in group] for group in pieces]
     a_parts = [[(p, part(96, 192)) for p in group] for group in pieces]
     small_parts = [(p, part(16, 288)) for p in pieces[0]]
 
-    ids_row = jnp.pad(segment_ids.astype(BF)[None, :], ((0, 15), (0, D - TOK)))
-    load = jnp.concatenate([tokens, ids_row, cotangent], axis=0)
-    loads = [load] + exchange([after(load, chunks[0])] * TEAM)[1:]
-    token_slots = [(load, part(TOK, 0)) for load in loads]
+    def gather_team(piece, *others):
+        other = after(team_send(piece, 1), *others)
+        return piece, other, team_send(jnp.concatenate([piece, other], axis=0), 2)
+
+    def slots_of(gathered, start=0):
+        piece, other, far = gathered
+        size = piece.shape[0]
+        return [
+            (piece, part(TOK, start)), (other, part(TOK, start)),
+            (far, part(TOK, start)), (far, part(TOK, size + start)),
+        ]
+
+    def sum_team(own, near, far, *others):
+        other = after(team_send(far, 2), *others)
+        both = (near + other[TOK:].astype(F32)).astype(BF)
+        return own, (other, part(TOK, 0)), team_send(both, 1)
+
+    ids_rows = jnp.pad(segment_ids.astype(BF)[None, :], ((0, TOK - 1), (0, D - TOK)))
+    load = jnp.concatenate([tokens, cotangent, ids_rows], axis=0)
+    loads = gather_team(after(load, pieces[0][1], pieces[0][3], pieces[0][4]), pieces[0][2], pieces[0][5], pieces[0][7])
+    token_slots = slots_of(loads)
     here = lax.axis_index("x")
     rows = jnp.arange(TOK, dtype=jnp.int32)
     places = jnp.concatenate([here * TOK + rows, (1 - here) * TOK + rows])
     masks, cosines, sines = [], [], []
     lane = jnp.arange(128, dtype=jnp.int32) % HEAD
     inverse = 10000.0 ** (-(lane % (ROT // 2) * 2).astype(F32) / ROT)
+    id_rows = [
+        loads[0][2 * TOK, :TOK], loads[1][2 * TOK, :TOK],
+        loads[2][2 * TOK, :TOK], loads[2][5 * TOK, :TOK],
+    ]
     for g in range(2):
-        ids = jnp.concatenate([load[TOK, :TOK] for load in loads[2 * g : 2 * g + 2]]).astype(F32)
+        ids = jnp.concatenate(id_rows[2 * g : 2 * g + 2]).astype(F32)
         visible = (places[None, :] <= places[:, None]) & (ids[None, :] == ids[:, None])
         masks.append(jnp.where(visible, 0.0, -1e30).astype(F32))
         position = places - jnp.sum((ids[None, :] < ids[:, None]).astype(jnp.int32), axis=1)
@@ -1031,7 +1094,7 @@
     mask = jnp.stack(masks)
     cosine, sine = jnp.concatenate(cosines), jnp.concatenate(sines)
 
-    four = [shape((TOK, D), F32)] + [shape((TOK, D), BF)] * 3
+    partials = [shape((TOK, D), F32)] * 2 + [shape((PAIR, D), BF)]
     stream_pair = [shape((TOK, D), F32), shape((TOK, D), BF)]
     wide = ((tok_all, D), BF)
 
@@ -1044,42 +1107,41 @@
     )
     y = run(
         mlp_body,
-        four,
+        partials,
         "mlp_forward",
         (*token_slots, *m_parts[0], vec, attn_out),
         [((lines, 192, D), BF)],
     )
 
     def residual(stream, blocks):
-        return call(residual_body, stream_pair, "residual", (stream, *exchange(blocks), vec))
-
-    stream, low = residual(tokens, y)
+        return run(residual_body, stream_pair, "residual", (stream, *sum_team(*blocks), vec))
+
+    stream, low = residual(tokens, (after(y[0], pieces[1][4]), *y[1:]))
     streams = [tokens, stream]
-    slots = [token_slots, exchange([low] * TEAM)]
+    slots = [token_slots, slots_of(gather_team(low, pieces[1][5], pieces[1][7]))]
 
     grad = cotangent
-    grad_slots = [load[TOK + 16 :] for load in loads]
+    grad_slots = slots_of(loads, TOK)
     outs = [None] * LAYERS
     block_m, block_a = shape((192, D), BF), shape((112, D), BF)
 
-    def mlp_back(depth, slots, grad_slots):
+    def mlp_back(depth, slots, grad_slots, grads):
         last = depth == LAYERS - 1
-        result = run(
+        return run(
             partial(mlp_both_body, depth, last),
-            [shape((4, 192, D), BF)] * 2
-            + [shape((tok_all, D), F32), shape((8, D), F32)]
-            + ([shape((tok_all, D), F32)] if last else []),
+            [shape((tok_all, D), F32), shape((8, D), F32)]
+            + ([shape((tok_all, D), F32)] if last else [])
+            + grads,
             "mlp_both",
             (*slots, *grad_slots, *m_parts[depth], vec),
             [((lines, 192, D), BF), ((lines, 192, D), BF), wide, wide, wide, wide],
         )
-        return result[0], line_flip(result[1]), result[2:]
-
-    def attend_back(depth, slots, grad_slots, rest):
+
+    def attend_back(depth, slots, grad_slots, rest, *others):
         last = depth == LAYERS - 1
         result = run(
             partial(attend_both_body, depth, last),
-            [shape((4, 112, D), BF)] * 2 + four + (four if last else []),
+            [shape((4, 112, D), BF)] * 2 + partials + (partials if last else []),
             "attend_both",
             (*slots, *grad_slots, *a_parts[depth], vec, cosine, sine, mask, *rest),
             [
@@ -1091,57 +1153,87 @@
                 wide,
             ],
         )
-        return result[0], line_flip(result[1]), result[2:6], result[6:]
+        return result[0], line_flip(after(result[1], *others)), result[2:5], result[5:]
 
     def norm_back(depth, grad, received):
-        return call(
+        return run(
             norm_back_body, stream_pair, "norm_backward", (streams[depth], grad, *received)
         )
 
-    def add(kind, keep, other, name):
-        return run(add_body, [kind] * 3, name, (keep, other))
+    def add(kind, keep, other, slots, places, name):
+        return run(partial(add_body, slots, places), [kind] * len(slots), name, (keep, other))
 
     def shifts(sums):
         return [line_shift(piece, s + 1) for s, piece in enumerate(sums)]
 
-    def hand_over(depth, m_keep, m_other, m_sums, a_keep, a_other, a_sums):
+    def split(attend, mlp, early=()):
+        keep, other, *sums = attend
+        m_keep, m_other, *m_sums = mlp
         mine = run(
-            split_body,
+            partial(split_body, bool(early)),
             [shape((64, D), BF)] * TEAM
             + [shape((96, D), F32), shape((24, D), BF), shape((8, 128), F32)],
             "split_gradients",
-            (
-                one_of(m_keep, 0), one_of(m_other, 0), *m_sums,
-                one_of(a_keep, 0), one_of(a_other, 0), *a_sums,
-            ),
+            (one_of(keep, 0), one_of(other, 0), *sums, one_of(m_keep, 0), m_other, *m_sums, *early),
         )
         attn_rows = lax.ppermute(mine[TEAM + 1], everywhere, gather_back)
-        outs[depth] = exchange(mine[:TEAM]) + [mine[TEAM + 2], attn_rows, mine[TEAM]]
-        return mine
-
-    m_keep1, m_other1, rest = mlp_back(1, slots[1], grad_slots)
-    a_keep1, a_other1, ns, ys = attend_back(1, slots[1], grad_slots, rest)
-    received = exchange(ns)
-    received[3] = after(received[3], m_other1)
-    grad, low = norm_back(1, grad, received)
-    m_added1 = add(block_m, m_keep1, after(m_other1, low), "add_mlp")
+        return exchange(mine[:TEAM]) + [mine[TEAM], mine[TEAM + 2], attn_rows]
+
+    early_block, late_four = shape((2, EARLY, D), BF), shape((4, 192 - EARLY, D), BF)
+    dn, sum_m, y_part, e0, e1, e2, e3, m_keep1, m_send1 = mlp_back(
+        1, slots[1], grad_slots, [early_block] * 4 + [late_four] * 2
+    )
+    early = shifts((e1, e2, e3))
+    m_other1 = line_flip(m_send1)
+    a_keep1, a_other1, ns, ys = attend_back(1, slots[1], grad_slots, (dn, sum_m, y_part))
+    ns = (ns[0], ns[1], after(ns[2], *early))
+    grad, low = norm_back(1, grad, sum_team(*ns, m_other1))
+    m_added1 = add(
+        shape((192 - EARLY, D), BF), m_keep1, after(m_other1, low), (1, 2, 3), (1, 2, 3), "add_mlp"
+    )
     m_sums1 = shifts(m_added1)
-    grad_slots = exchange([low] * TEAM)
-    _, activations = residual(streams[1], [ys[0]] + [after(y, grad_slots[3]) for y in ys[1:]])
-    grad_slots[0] = after(grad_slots[0], *m_added1)
-    m_keep0, m_other0, rest = mlp_back(0, slots[0], grad_slots)
-    a_added1 = add(block_a, a_keep1, after(a_other1, rest[0]), "add_attend")
+    gathered = gather_team(low)
+    grad_slots = slots_of((after(gathered[0], *m_added1), *gathered[1:]))
+    dn, sum_m, m_keep0, m_first0, m_second0 = mlp_back(
+        0, slots[0], grad_slots, [shape((4, 192, D), BF)] + [shape((2, 192, D), BF)] * 2
+    )
+    a_added1 = add(block_a, a_keep1, after(a_other1, dn, *m_sums1), (1, 2, 3), (1, 2, 3), "add_attend")
     a_sums1 = shifts(a_added1)
+    m_first0 = line_flip(after(m_first0, *a_added1))
+    m_second0 = line_flip(after(m_second0, *a_added1))
     a_keep0, a_other0, ns, _ = attend_back(
-        0, slots[0], grad_slots, [after(rest[0], *a_added1, *m_sums1), *rest[1:]]
-    )
-    grad, _ = norm_back(0, grad, exchange(ns))
-    mine = hand_over(1, m_keep1, m_other1, m_sums1, a_keep1, a_other1, a_sums1)
-    m_added0 = add(block_m, m_keep0, after(m_other0, mine[0]), "add_mlp")
-    m_sums0 = shifts(m_added0)
-    a_added0 = add(block_a, a_keep0, after(a_other0, *m_added0), "add_attend")
+        0, slots[0], grad_slots, (after(dn, *a_added1), sum_m), m_second0
+    )
+    m1, m3 = add(
+        block_m, m_keep0, after(m_first0, a_keep0, *a_sums1), HALVES[0], (0, 1), "add_first"
+    )
+    first_added = m1
+    m1, m3 = line_shift(m1, 1), line_shift(m3, 3)
+    (m2,) = add(block_m, m_keep0, after(m_second0, m1, m3), HALVES[1][:1], (0,), "add_second")
+    grad, _ = norm_back(0, grad, sum_team(*ns))
+    _, activations = residual(streams[1], (ys[0], ys[1], after(ys[2], first_added)))
+    e_keep, e_send = run(
+        line_sum_body,
+        [shape((EARLY, D), F32), shape((EARLY, D), BF)],
+        "line_sum",
+        (e0, after(early[0], first_added), early[1], early[2]),
+    )
+    outs[1] = split(
+        (a_keep1, a_other1, *a_sums1),
+        (m_keep1, one_of(m_other1, 0), *m_sums1),
+        (e_keep, line_flip(e_send)),
+    )
+    a_added0 = add(
+        block_a,
+        a_keep0,
+        after(a_other0, m2, grad, activations, outs[1][0]),
+        (1, 2, 3),
+        (1, 2, 3),
+        "add_attend",
+    )
+    m2 = line_shift(m2, 2)
     a_sums0 = shifts(a_added0)
-    hand_over(0, m_keep0, m_other0, m_sums0, a_keep0, a_other0, a_sums0)
+    outs[0] = split((a_keep0, a_other0, *a_sums0), (m_keep0, one_of(m_second0, 1), m1, m2, m3))
     row_24 = shape((LAYERS, 24), F32)
     final = run(
         unpack_body,

time: 349 us -> 323 us (0.926)
  waiting for transfers between devices: 157 us -> 130 us
  other arithmetic: 6.13 us -> 10.5 us
    ppermute x30 -> x23, waiting for transfers between devices: 48.6 us -> 9.11 us  [team_send(): return lax.ppermute(piece, TEAM_AXES, flips)]
    ppermute x12 -> x14, waiting for transfers between devices: 30.5 us -> 48.7 us  [line_flip(): return lax.ppermute(piece, 'y', [(0, 1), (1, 0)])]
    pallas_call x15 -> x21, Pallas kernels: 75 us -> 86.4 us  [run(): pl.pallas_call(body, grid=(1,), out_shape=out_shape, in_specs=[pl.BlockSp...]
    pallas_call x4 -> x0, Pallas kernels: 9.65 us -> none  [call(): pl.pallas_call(body, out_shape=out_shape, scratch_shapes=list(scratch), c...]
    ppermute x30 -> x23, starting transfers between devices: 32.5 us -> 25.4 us  [team_send(): return lax.ppermute(piece, TEAM_AXES, flips)]
    ppermute x18 -> x21, waiting for transfers between devices: 70.3 us -> 63.8 us  [line_shift(): lax.ppermute(piece, 'z', [(i, (i + shift) % size) for i in range(size)])]
    ppermute x1, waiting for transfers between devices: 0.01 us -> 4.92 us  [local_team(): attn_piece = lax.ppermute(attn_weight, everywhere, spread)]
    ppermute x2, starting transfers between devices: 8.4 us -> 13.3 us  [split(): attn_rows = lax.ppermute(mine[TEAM + 1], everywhere, gather_back)]
  transfers between devices with their start and end apart: 63 -> 61, of which waited for: 23 -> 21; matrix products, arithmetic and copies ran while one was open for 3% -> 2% of each run, Pallas kernels for 21% -> 21%
where the time goes in v1:
time: 323 us; the launch traced here: 319 us
  waiting for transfers between devices  130 us (40%)
  Pallas kernels  86.4 us (27%)
  starting transfers between devices  78.4 us (24%)
  local copies, waits for them, and re-layouts  11.6 us (4%)
  other arithmetic  10.5 us (3%)
    pallas_call x21, Pallas kernels, run(): pl.pallas_call(body, grid=(1,), out_shape=out_shape, in_specs=[pl.BlockSp...  86.4 us
    ppermute x21, waiting for transfers between devices, line_shift(): lax.ppermute(piece, 'z', [(i, (i + shift) % size) for i in range(size)])  63.8 us
    ppermute x14, waiting for transfers between devices, line_flip(): return lax.ppermute(piece, 'y', [(0, 1), (1, 0)])  48.7 us
    ppermute x21, starting transfers between devices, line_shift(): lax.ppermute(piece, 'z', [(i, (i + shift) % size) for i in range(size)])  27.3 us
    ppermute x23, starting transfers between devices, team_send(): return lax.ppermute(piece, TEAM_AXES, flips)  25.4 us
    ppermute x2, starting transfers between devices, split(): attn_rows = lax.ppermute(mine[TEAM + 1], everywhere, gather_back)  13.3 us
    unnamed x159, local copies, waits for them, and re-layouts  11.6 us
    ppermute x23, waiting for transfers between devices, team_send(): return lax.ppermute(piece, TEAM_AXES, flips)  9.11 us
  transfers between devices with their start and end apart: 61, of which 21 were waited for; matrix products, arithmetic and copies ran while one was open for 2% of the time, Pallas kernels for 21%

profile of v1, /device:TPU:5, one launch (start us, length us, event | category | flops | bytes accessed | tf_op | source)
XLA Modules:
  0.0 318.7 jit_solution(18161945074254887901)
XLA Ops:
  5.9 5.6 %collective-permute-start.3 = (bf16[2,24,768]{2,1,0:T(8,128)(2,1)}, bf16[2,24,768]{2,1,0:T(8,128)(2,1)S(1)}, u32[]{:S(2)}, u32[]{:S(2)}) collective-permute-start(bf16[2,24,768]{2,1,0:T(8,128)(2,1)} %param.20), channel_id=1, source_target_pairs={{0,0},{1,4},{2,8},{3,12},{4,16},{5,20},{6,24},{7,28},{8,1},{9,5},{... | collective-permute-start | bytes 221192 | tf_op jit(solution)/shard_map/ppermute | solution.py:1039
  11.5 4.9 %collective-permute-done.3.attn_ref = bf16[2,24,768]{2,1,0:T(8,128)(2,1)S(1)} collective-permute-done((bf16[2,24,768]{2,1,0:T(8,128)(2,1)}, bf16[2,24,768]{2,1,0:T(8,128)(2,1)S(1)}, u32[]{:S(2)}, u32[]{:S(2)}) %collective-permute-start.3) | collective-permute-done | bytes 73760 | tf_op jit(solution)/shard_map/ppermute | solution.py:1039
  21.8 9.8 %collective-permute-done.6.refs_4_.refs_12_ = bf16[304,768]{1,0:T(8,128)(2,1)S(1)} collective-permute-done((bf16[304,768]{1,0:T(8,128)(2,1)}, bf16[304,768]{1,0:T(8,128)(2,1)S(1)}, u32[]{:S(2)}, u32[]{:S(2)}) %collective-permute-start.6) | collective-permute-done | bytes 466976 | tf_op jit(solution)/shard_map/ppermute | solution.py:985
  31.8 10.7 %collective-permute-done.4.refs_1_.refs_9_ = bf16[304,768]{1,0:T(8,128)(2,1)S(1)} collective-permute-done((bf16[304,768]{1,0:T(8,128)(2,1)}, bf16[304,768]{1,0:T(8,128)(2,1)S(1)}, u32[]{:S(2)}, u32[]{:S(2)}) %collective-permute-start.4) | collective-permute-done | bytes 466976 | tf_op jit(solution)/shard_map/ppermute | solution.py:981
  44.7 7.7 %collective-permute-done.10.refs_7_.refs_15_ = bf16[304,768]{1,0:T(8,128)(2,1)S(1)} collective-permute-done((bf16[304,768]{1,0:T(8,128)(2,1)S(1)}, bf16[304,768]{1,0:T(8,128)(2,1)S(1)}, u32[]{:S(2)}, u32[]{:S(2)}) %collective-permute-start.10) | collective-permute-done | bytes 466976 | tf_op jit(solution)/shard_map/ppermute | solution.py:985
  52.5 14.4 %collective-permute-done.8.refs_2_.refs_10_ = bf16[304,768]{1,0:T(8,128)(2,1)S(1)} collective-permute-done((bf16[304,768]{1,0:T(8,128)(2,1)}, bf16[304,768]{1,0:T(8,128)(2,1)S(1)}, u32[]{:S(2)}, u32[]{:S(2)}) %collective-permute-start.8) | collective-permute-done | bytes 466976 | tf_op jit(solution)/shard_map/ppermute | solution.py:981
  76.5 7.3 %collective-permute-done.12.refs_6_.refs_14_ = bf16[304,768]{1,0:T(8,128)(2,1)S(1)} collective-permute-done((bf16[304,768]{1,0:T(8,128)(2,1)S(1)}, bf16[304,768]{1,0:T(8,128)(2,1)S(1)}, u32[]{:S(2)}, u32[]{:S(2)}) %collective-permute-start.12) | collective-permute-done | bytes 466976 | tf_op jit(solution)/shard_map/ppermute | solution.py:985
  84.6 6.2 %attend_forward.1 = (f32[512,768]{1,0:T(8,128)}, f32[2,8,768]{2,1,0:T(8,128)}) custom-call(s32[3]{0:T(128)} %pad_add_fusion.1.me_ref, bf16[384,768]{1,0:T(8,128)(2,1)} %copy-done.1, bf16[384,768]{1,0:T(8,128)(2,1)} %copy-done.2, bf16[768,768]{1,0:T(8,128)(2,1)} %copy-done, bf16[768,768]{1,0:T(8,128)(2,1)} %copy-done, ...), custom_call_target="tpu_custom_call" | custom-call | tf_op jit(solution)/shard_map/attend_forward/pallas_call | solution.py:1012
  90.8 5.2 %mlp_forward.1 = (f32[128,768]{1,0:T(8,128)}, f32[128,768]{1,0:T(8,128)}, bf16[256,768]{1,0:T(8,128)(2,1)}) custom-call(s32[3]{0:T(128)} %pad_add_fusion.1.me_ref, bf16[384,768]{1,0:T(8,128)(2,1)} %copy-done.1, bf16[384,768]{1,0:T(8,128)(2,1)} %copy-done.2, bf16[768,768]{1,0:T(8,128)(2,1)} %copy-done, bf16[768,768]{1,0:T(8,128)(2,1)} %copy-done, ...), custom_call_target="tpu_custom_call" | custom-call | tf_op jit(solution)/shard_map/mlp_forward/pallas_call | solution.py:1012
  101.5 7.6 %collective-permute-done.13.refs_4_ = bf16[288,768]{1,0:T(8,128)(2,1)S(1)} collective-permute-done((bf16[288,768]{1,0:T(8,128)(2,1)S(1)}, bf16[288,768]{1,0:T(8,128)(2,1)S(1)}, u32[]{:S(2)}, u32[]{:S(2)}) %collective-permute-start.13) | collective-permute-done | bytes 442400 | tf_op jit(solution)/shard_map/ppermute | solution.py:985
  113.1 6.3 %collective-permute-done.22.refs_2_ = bf16[288,768]{1,0:T(8,128)(2,1)S(1)} collective-permute-done((bf16[288,768]{1,0:T(8,128)(2,1)S(1)}, bf16[288,768]{1,0:T(8,128)(2,1)S(1)}, u32[]{:S(2)}, u32[]{:S(2)}) %collective-permute-start.22) | collective-permute-done | bytes 442400 | tf_op jit(solution)/shard_map/ppermute | solution.py:981
  120.8 7.2 %collective-permute-done.18.refs_5_ = bf16[288,768]{1,0:T(8,128)(2,1)S(1)} collective-permute-done((bf16[288,768]{1,0:T(8,128)(2,1)S(1)}, bf16[288,768]{1,0:T(8,128)(2,1)S(1)}, u32[]{:S(2)}, u32[]{:S(2)}) %collective-permute-start.18) | collective-permute-done | bytes 442400 | tf_op jit(solution)/shard_map/ppermute | solution.py:985
  130.6 6.9 %collective-permute-done.23.refs_6_ = bf16[288,768]{1,0:T(8,128)(2,1)S(1)} collective-permute-done((bf16[288,768]{1,0:T(8,128)(2,1)S(1)}, bf16[288,768]{1,0:T(8,128)(2,1)S(1)}, u32[]{:S(2)}, u32[]{:S(2)}) %collective-permute-start.23) | collective-permute-done | bytes 442400 | tf_op jit(solution)/shard_map/ppermute | solution.py:985
  139.0 8.1 %mlp_both.2 = (f32[512,768]{1,0:T(8,128)}, f32[8,768]{1,0:T(8,128)}, f32[512,768]{1,0:T(8,128)}, bf16[2,48,768]{2,1,0:T(8,128)(2,1)}, bf16[2,48,768]{2,1,0:T(8,1...) custom-call(s32[3]{0:T(128)} %pad_add_fusion.1.me_ref, ...), custom_call_target="tpu_custom_call" | custom-call | tf_op jit(solution)/shard_map/mlp_both/pallas_call | solution.py:1012
  150.6 11.7 %attend_both.2 = (bf16[4,112,768]{2,1,0:T(8,128)(2,1)}, bf16[4,112,768]{2,1,0:T(8,128)(2,1)}, f32[128,768]{1,0:T(8,128)}, f32[128,768]{1,0:T(8,128)}, bf16[256,7...) custom-call(s32[3]{0:T(128)} %pad_add_fusion.1.me_ref, ...), custom_call_target="tpu_custom_call" | custom-call | tf_op jit(solution)/shard_map/attend_both/pallas_call | solution.py:1012
  170.3 3.4 %collective-permute-done.29.n2 = bf16[128,768]{1,0:T(8,128)(2,1)S(1)} collective-permute-done((bf16[128,768]{1,0:T(8,128)(2,1)S(1)}, bf16[128,768]{1,0:T(8,128)(2,1)S(1)}, u32[]{:S(2)}, u32[]{:S(2)}) %collective-permute-start.29) | collective-permute-done | bytes 196640 | tf_op jit(solution)/shard_map/ppermute | solution.py:976
  178.0 3.6 %collective-permute-done.30.g1 = bf16[128,768]{1,0:T(8,128)(2,1)S(1)} collective-permute-done((bf16[128,768]{1,0:T(8,128)(2,1)}, bf16[128,768]{1,0:T(8,128)(2,1)S(1)}, u32[]{:S(2)}, u32[]{:S(2)}) %collective-permute-start.30) | collective-permute-done | bytes 196640 | tf_op jit(solution)/shard_map/ppermute | solution.py:976
  182.6 4.1 %collective-permute-start.31 = (bf16[256,768]{1,0:T(8,128)(2,1)S(1)}, bf16[256,768]{1,0:T(8,128)(2,1)S(1)}, u32[]{:S(2)}, u32[]{:S(2)}) collective-permute-start(bf16[256,768]{1,0:T(8,128)(2,1)S(1)} %pad_maximum_fusion.3), channel_id=1, source_target_pairs={{0,2},{1,3},{2,0},{3,1},{4,6},{5,7},{6,4},{7,5},{8,10},{9,11},{10,... | collective-permute-start | bytes 1179656 | tf_op jit(solution)/shard_map/ppermute | solution.py:976
  189.1 3.1 collective-permute-start.34
  193.3 7.6 %mlp_both.3 = (f32[512,768]{1,0:T(8,128)}, f32[8,768]{1,0:T(8,128)}, bf16[4,192,768]{2,1,0:T(8,128)(2,1)}, bf16[2,192,768]{2,1,0:T(8,128)(2,1)}, bf16[2,192,768]{2,1,0:T(8,128)(2,1)}) custom-call(s32[3]{0:T(128)} %pad_add_fusion.1.me_ref, bf16[384,768]{1,0:T(8,128)(2,1)} %copy-done.1, bf16[384,768]{1,0:T(8,128)(2,1)} %copy-done.2, bf16[768,768]{1,0:T(8,128)(2,1)} %copy-done, ...), custom_call_target="tpu_custom_call" | custom-call | tf_op jit(solution)/shard_map/mlp_both/pallas_call | solution.py:1012
  200.9 6.9 %collective-permute-done.34.refs_8_ = bf16[144,768]{1,0:T(8,128)(2,1)S(1)} collective-permute-done((bf16[144,768]{1,0:T(8,128)(2,1)}, bf16[144,768]{1,0:T(8,128)(2,1)S(1)}, u32[]{:S(2)}, u32[]{:S(2)}) %collective-permute-start.34) | collective-permute-done | bytes 221216 | tf_op jit(solution)/shard_map/ppermute | solution.py:981
  211.7 4.9 %collective-permute-start.37 = (bf16[112,768]{1,0:T(8,128)(2,1)}, bf16[112,768]{1,0:T(8,128)(2,1)S(1)}, u32[]{:S(2)}, u32[]{:S(2)}) collective-permute-start(bf16[112,768]{1,0:T(8,128)(2,1)} %get-tuple-element.164), channel_id=1, source_target_pairs={{0,8},{8,16},{16,24},{24,0},{1,9},{9,17},{17,25},{25,1},{2,10},{10... | collective-permute-start | bytes 516104 | tf_op jit(solution)/shard_map/ppermute | solution.py:981
  216.6 11.3 %attend_both.3 = (bf16[4,112,768]{2,1,0:T(8,128)(2,1)}, bf16[4,112,768]{2,1,0:T(8,128)(2,1)}, f32[128,768]{1,0:T(8,128)}, f32[128,768]{1,0:T(8,128)}, bf16[256,768]{1,0:T(8,128)(2,1)}) custom-call(s32[3]{0:T(128)} %pad_add_fusion.1.me_ref, bf16[384,768]{1,0:T(8,128)(2,1)} %copy-done.1, bf16[384,768]{1,0:T(8,128)(2,1)} %copy-done.2, ...), custom_call_target="tpu_custom_call" | custom-call | tf_op jit(solution)/shard_map/attend_both/pallas_call | solution.py:1012
  231.3 8.5 %collective-permute-done.38.refs_3_ = bf16[112,768]{1,0:T(8,128)(2,1)S(1)} collective-permute-done((bf16[112,768]{1,0:T(8,128)(2,1)S(1)}, bf16[112,768]{1,0:T(8,128)(2,1)S(1)}, u32[]{:S(2)}, u32[]{:S(2)}) %collective-permute-start.38) | collective-permute-done | bytes 172064 | tf_op jit(solution)/shard_map/ppermute | solution.py:981
  245.1 3.8 %collective-permute-start.46 = (bf16[192,768]{1,0:T(8,128)(2,1)}, bf16[192,768]{1,0:T(8,128)(2,1)S(1)}, u32[]{:S(2)}, u32[]{:S(2)}) collective-permute-start(bf16[192,768]{1,0:T(8,128)(2,1)} %get-tuple-element.172), channel_id=1, source_target_pairs={{0,8},{8,16},{16,24},{24,0},{1,9},{9,17},{17,25},{25,1},{2,10},{10... | collective-permute-start | bytes 884744 | tf_op jit(solution)/shard_map/ppermute | solution.py:981
  249.6 13.5 %collective-permute-done.47.refs_9_ = bf16[192,768]{1,0:T(8,128)(2,1)S(1)} collective-permute-done((bf16[192,768]{1,0:T(8,128)(2,1)}, bf16[192,768]{1,0:T(8,128)(2,1)S(1)}, u32[]{:S(2)}, u32[]{:S(2)}) %collective-permute-start.47) | collective-permute-done | bytes 294944 | tf_op jit(solution)/shard_map/ppermute | solution.py:981
  272.0 2.9 split_gradients.2
  286.2 6.4 %collective-permute-start.60 = (bf16[24,768]{1,0:T(8,128)(2,1)S(1)}, bf16[24,768]{1,0:T(8,128)(2,1)S(1)}, u32[]{:S(2)}, u32[]{:S(2)}) collective-permute-start(bf16[24,768]{1,0:T(8,128)(2,1)S(1)} %copy-done.77), channel_id=1, source_target_pairs={{0,0},{4,1},{8,2},{12,3},{16,4},{20,5},{24,6},{28,7},{1,8},{5,9},{... | collective-permute-start | bytes 110600 | tf_op jit(solution)/shard_map/ppermute | solution.py:1179
  293.2 3.3 %collective-permute-done.50.refs_3_ = bf16[112,768]{1,0:T(8,128)(2,1)S(1)} collective-permute-done((bf16[112,768]{1,0:T(8,128)(2,1)}, bf16[112,768]{1,0:T(8,128)(2,1)S(1)}, u32[]{:S(2)}, u32[]{:S(2)}) %collective-permute-start.50) | collective-permute-done | bytes 172064 | tf_op jit(solution)/shard_map/ppermute | solution.py:981
  298.2 3.0 split_gradients.3
  303.2 6.8 %collective-permute-start.56 = (bf16[24,768]{1,0:T(8,128)(2,1)}, bf16[24,768]{1,0:T(8,128)(2,1)S(1)}, u32[]{:S(2)}, u32[]{:S(2)}) collective-permute-start(bf16[24,768]{1,0:T(8,128)(2,1)} %get-tuple-element.202), channel_id=1, source_target_pairs={{0,0},{4,1},{8,2},{12,3},{16,4},{20,5},{24,6},{28,7},{1,8},{5,9},{... | collective-permute-start | bytes 110600 | tf_op jit(solution)/shard_map/ppermute | solution.py:1179
  310.1 3.5 %collective-permute-done.56.refs_6_ = bf16[24,768]{1,0:T(8,128)(2,1)S(1)} collective-permute-done((bf16[24,768]{1,0:T(8,128)(2,1)}, bf16[24,768]{1,0:T(8,128)(2,1)S(1)}, u32[]{:S(2)}, u32[]{:S(2)}) %collective-permute-start.56) | collective-permute-done | bytes 36896 | tf_op jit(solution)/shard_map/ppermute | solution.py:1179
  (295 shorter events, 100.7 us)
Async XLA Ops:
  21.7 20.8 %collective-permute-start.4 = (bf16[304,768]{1,0:T(8,128)(2,1)}, bf16[304,768]{1,0:T(8,128)(2,1)S(1)}, u32[]{:S(2)}, u32[]{:S(2)}) collective-permute-start(bf16[304,768]{1,0:T(8,128)(2,1)} %get-tuple-element.123.refs_0_.refs_8_), channel_id=1, source_target_pairs={{0,8},{8,16},{16,24},{24,0},{1,9},{9,17},{17,25},{25,1},{2,10},{10... | collective-permute-start | bytes 1400840 | tf_op jit(solution)/shard_map/ppermute | solution.py:981
  42.5 24.4 %collective-permute-start.7 = (bf16[384,768]{1,0:T(8,128)(2,1)S(1)}, bf16[384,768]{1,0:T(8,128)(2,1)S(1)}, u32[]{:S(2)}, u32[]{:S(2)}) collective-permute-start(bf16[384,768]{1,0:T(8,128)(2,1)S(1)} %fusion.1.x0.g0), channel_id=1, source_target_pairs={{0,1},{1,0},{2,3},{3,2},{4,5},{5,4},{6,7},{7,6},{8,9},{9,8},{10,11... | collective-permute-start | bytes 1769480 | tf_op jit(solution)/shard_map/ppermute | solution.py:976
  44.5 22.4 %collective-permute-start.8 = (bf16[304,768]{1,0:T(8,128)(2,1)}, bf16[304,768]{1,0:T(8,128)(2,1)S(1)}, u32[]{:S(2)}, u32[]{:S(2)}) collective-permute-start(bf16[304,768]{1,0:T(8,128)(2,1)} %get-tuple-element.123.refs_0_.refs_8_), channel_id=1, source_target_pairs={{0,16},{8,24},{16,0},{24,8},{1,17},{9,25},{17,1},{25,9},{2,18},{10... | collective-permute-start | bytes 1400840 | tf_op jit(solution)/shard_map/ppermute | solution.py:981
  44.7 22.2 %collective-permute-start.9 = (bf16[304,768]{1,0:T(8,128)(2,1)S(1)}, bf16[304,768]{1,0:T(8,128)(2,1)S(1)}, u32[]{:S(2)}, u32[]{:S(2)}) collective-permute-start(bf16[304,768]{1,0:T(8,128)(2,1)S(1)} %collective-permute-done.4.refs_1_.refs_9_), channel_id=1, source_target_pairs={{0,4},{4,0},{1,5},{5,1},{2,6},{6,2},{3,7},{7,3},{8,12},{12,8},{9,1... | collective-permute-start | bytes 1400840 | tf_op jit(solution)/shard_map/ppermute | solution.py:985
  70.1 27.3 %collective-permute-start.19 = (bf16[288,768]{1,0:T(8,128)(2,1)}, bf16[288,768]{1,0:T(8,128)(2,1)S(1)}, u32[]{:S(2)}, u32[]{:S(2)}) collective-permute-start(bf16[288,768]{1,0:T(8,128)(2,1)} %get-tuple-element.136.refs_0_), channel_id=1, source_target_pairs={{0,24},{8,0},{16,8},{24,16},{1,25},{9,1},{17,9},{25,17},{2,26},{10... | collective-permute-start | bytes 1327112 | tf_op jit(solution)/shard_map/ppermute | solution.py:981
  71.3 26.1 %collective-permute-start.17 = (bf16[288,768]{1,0:T(8,128)(2,1)}, bf16[288,768]{1,0:T(8,128)(2,1)S(1)}, u32[]{:S(2)}, u32[]{:S(2)}) collective-permute-start(bf16[288,768]{1,0:T(8,128)(2,1)} %get-tuple-element.136.refs_0_), channel_id=1, source_target_pairs={{0,8},{8,16},{16,24},{24,0},{1,9},{9,17},{17,25},{25,1},{2,10},{10... | collective-permute-start | bytes 1327112 | tf_op jit(solution)/shard_map/ppermute | solution.py:981
  97.4 22.0 %collective-permute-start.22 = (bf16[288,768]{1,0:T(8,128)(2,1)S(1)}, bf16[288,768]{1,0:T(8,128)(2,1)S(1)}, u32[]{:S(2)}, u32[]{:S(2)}) collective-permute-start(bf16[288,768]{1,0:T(8,128)(2,1)S(1)} %copy-done.17), channel_id=1, source_target_pairs={{0,16},{8,24},{16,0},{24,8},{1,17},{9,25},{17,1},{25,9},{2,18},{10... | collective-permute-start | bytes 1327112 | tf_op jit(solution)/shard_map/ppermute | solution.py:981
  97.6 23.2 %collective-permute-start.20 = (bf16[288,768]{1,0:T(8,128)(2,1)S(1)}, bf16[288,768]{1,0:T(8,128)(2,1)S(1)}, u32[]{:S(2)}, u32[]{:S(2)}) collective-permute-start(bf16[288,768]{1,0:T(8,128)(2,1)S(1)} %collective-permute-done.19.refs_3_), channel_id=1, source_target_pairs={{0,4},{4,0},{1,5},{5,1},{2,6},{6,2},{3,7},{7,3},{8,12},{12,8},{9,1... | collective-permute-start | bytes 1327112 | tf_op jit(solution)/shard_map/ppermute | solution.py:985
  99.0 29.1 %collective-permute-start.18 = (bf16[288,768]{1,0:T(8,128)(2,1)S(1)}, bf16[288,768]{1,0:T(8,128)(2,1)S(1)}, u32[]{:S(2)}, u32[]{:S(2)}) collective-permute-start(bf16[288,768]{1,0:T(8,128)(2,1)S(1)} %collective-permute-done.17.refs_1_), channel_id=1, source_target_pairs={{0,4},{4,0},{1,5},{5,1},{2,6},{6,2},{3,7},{7,3},{8,12},{12,8},{9,1... | collective-permute-start | bytes 1327112 | tf_op jit(solution)/shard_map/ppermute | solution.py:985
  111.9 16.1 %collective-permute-start.16 = (bf16[128,768]{1,0:T(8,128)(2,1)}, bf16[128,768]{1,0:T(8,128)(2,1)S(1)}, u32[]{:S(2)}, u32[]{:S(2)}) collective-permute-start(bf16[128,768]{1,0:T(8,128)(2,1)} %get-tuple-element.134.x0), channel_id=1, source_target_pairs={{0,1},{1,0},{2,3},{3,2},{4,5},{5,4},{6,7},{7,6},{8,9},{9,8},{10,11... | collective-permute-start | bytes 589832 | tf_op jit(solution)/shard_map/ppermute | solution.py:976
  119.4 18.2 %collective-permute-start.23 = (bf16[288,768]{1,0:T(8,128)(2,1)S(1)}, bf16[288,768]{1,0:T(8,128)(2,1)S(1)}, u32[]{:S(2)}, u32[]{:S(2)}) collective-permute-start(bf16[288,768]{1,0:T(8,128)(2,1)S(1)} %collective-permute-done.22.refs_2_), channel_id=1, source_target_pairs={{0,4},{4,0},{1,5},{5,1},{2,6},{6,2},{3,7},{7,3},{8,12},{12,8},{9,1... | collective-permute-start | bytes 1327112 | tf_op jit(solution)/shard_map/ppermute | solution.py:985
  147.1 20.5 %collective-permute-start.28 = (bf16[4,144,768]{2,1,0:T(8,128)(2,1)}, bf16[4,144,768]{2,1,0:T(8,128)(2,1)S(1)}, u32[]{:S(2)}, u32[]{:S(2)}) collective-permute-start(bf16[4,144,768]{2,1,0:T(8,128)(2,1)} %get-tuple-element.148), channel_id=1, source_target_pairs={{0,4},{4,0},{1,5},{5,1},{2,6},{6,2},{3,7},{7,3},{8,12},{12,8},{9,1... | collective-permute-start | bytes 2654216 | tf_op jit(solution)/shard_map/ppermute | solution.py:985
  147.1 15.2 %collective-permute-start.24 = (bf16[2,48,768]{2,1,0:T(8,128)(2,1)}, bf16[2,48,768]{2,1,0:T(8,128)(2,1)S(1)}, u32[]{:S(2)}, u32[]{:S(2)}) collective-permute-start(bf16[2,48,768]{2,1,0:T(8,128)(2,1)} %get-tuple-element.144), channel_id=1, source_target_pairs={{0,8},{8,16},{16,24},{24,0},{1,9},{9,17},{17,25},{25,1},{2,10},{10... | collective-permute-start | bytes 442376 | tf_op jit(solution)/shard_map/ppermute | solution.py:981
  147.5 14.8 %collective-permute-start.25 = (bf16[2,48,768]{2,1,0:T(8,128)(2,1)}, bf16[2,48,768]{2,1,0:T(8,128)(2,1)S(1)}, u32[]{:S(2)}, u32[]{:S(2)}) collective-permute-start(bf16[2,48,768]{2,1,0:T(8,128)(2,1)} %get-tuple-element.145), channel_id=1, source_target_pairs={{0,16},{8,24},{16,0},{24,8},{1,17},{9,25},{17,1},{25,9},{2,18},{10... | collective-permute-start | bytes 442376 | tf_op jit(solution)/shard_map/ppermute | solution.py:981
  178.0 22.9 %collective-permute-start.32 = (bf16[4,112,768]{2,1,0:T(8,128)(2,1)S(1)}, bf16[4,112,768]{2,1,0:T(8,128)(2,1)S(1)}, u32[]{:S(2)}, u32[]{:S(2)}) collective-permute-start(bf16[4,112,768]{2,1,0:T(8,128)(2,1)S(1)} %copy-done.68), channel_id=1, source_target_pairs={{0,4},{4,0},{1,5},{5,1},{2,6},{6,2},{3,7},{7,3},{8,12},{12,8},{9,1... | collective-permute-start | bytes 2064392 | tf_op jit(solution)/shard_map/ppermute | solution.py:985
  189.1 18.7 %collective-permute-start.34 = (bf16[144,768]{1,0:T(8,128)(2,1)}, bf16[144,768]{1,0:T(8,128)(2,1)S(1)}, u32[]{:S(2)}, u32[]{:S(2)}) collective-permute-start(bf16[144,768]{1,0:T(8,128)(2,1)} %get-tuple-element.155), channel_id=1, source_target_pairs={{0,16},{8,24},{16,0},{24,8},{1,17},{9,25},{17,1},{25,9},{2,18},{10... | collective-permute-start | bytes 663560 | tf_op jit(solution)/shard_map/ppermute | solution.py:981
  192.3 15.6 %collective-permute-start.35 = (bf16[144,768]{1,0:T(8,128)(2,1)}, bf16[144,768]{1,0:T(8,128)(2,1)S(1)}, u32[]{:S(2)}, u32[]{:S(2)}) collective-permute-start(bf16[144,768]{1,0:T(8,128)(2,1)} %get-tuple-element.156), channel_id=1, source_target_pairs={{0,24},{8,0},{16,8},{24,16},{1,25},{9,1},{17,9},{25,17},{2,26},{10... | collective-permute-start | bytes 663560 | tf_op jit(solution)/shard_map/ppermute | solution.py:981
  210.2 29.6 %collective-permute-start.36 = (bf16[2,192,768]{2,1,0:T(8,128)(2,1)S(1)}, bf16[2,192,768]{2,1,0:T(8,128)(2,1)S(1)}, u32[]{:S(2)}, u32[]{:S(2)}) collective-permute-start(bf16[2,192,768]{2,1,0:T(8,128)(2,1)S(1)} %copy-done.70), channel_id=1, source_target_pairs={{0,4},{4,0},{1,5},{5,1},{2,6},{6,2},{3,7},{7,3},{8,12},{12,8},{9,1... | collective-permute-start | bytes 1769480 | tf_op jit(solution)/shard_map/ppermute | solution.py:985
  210.3 33.2 %collective-permute-start.44 = (bf16[2,192,768]{2,1,0:T(8,128)(2,1)S(1)}, bf16[2,192,768]{2,1,0:T(8,128)(2,1)S(1)}, u32[]{:S(2)}, u32[]{:S(2)}) collective-permute-start(bf16[2,192,768]{2,1,0:T(8,128)(2,1)S(1)} %copy-done.69), channel_id=1, source_target_pairs={{0,4},{4,0},{1,5},{5,1},{2,6},{6,2},{3,7},{7,3},{8,12},{12,8},{9,1... | collective-permute-start | bytes 1769480 | tf_op jit(solution)/shard_map/ppermute | solution.py:985
  211.7 17.8 %collective-permute-start.37 = (bf16[112,768]{1,0:T(8,128)(2,1)}, bf16[112,768]{1,0:T(8,128)(2,1)S(1)}, u32[]{:S(2)}, u32[]{:S(2)}) collective-permute-start(bf16[112,768]{1,0:T(8,128)(2,1)} %get-tuple-element.164), channel_id=1, source_target_pairs={{0,8},{8,16},{16,24},{24,0},{1,9},{9,17},{17,25},{25,1},{2,10},{10... | collective-permute-start | bytes 516104 | tf_op jit(solution)/shard_map/ppermute | solution.py:981
  228.0 15.7 %collective-permute-start.42 = (bf16[256,768]{1,0:T(8,128)(2,1)}, bf16[256,768]{1,0:T(8,128)(2,1)S(1)}, u32[]{:S(2)}, u32[]{:S(2)}) collective-permute-start(bf16[256,768]{1,0:T(8,128)(2,1)} %get-tuple-element.178), channel_id=1, source_target_pairs={{0,2},{1,3},{2,0},{3,1},{4,6},{5,7},{6,4},{7,5},{8,10},{9,11},{10,... | collective-permute-start | bytes 1179656 | tf_op jit(solution)/shard_map/ppermute | solution.py:976
  243.6 34.3 %collective-permute-start.45 = (bf16[4,112,768]{2,1,0:T(8,128)(2,1)S(1)}, bf16[4,112,768]{2,1,0:T(8,128)(2,1)S(1)}, u32[]{:S(2)}, u32[]{:S(2)}) collective-permute-start(bf16[4,112,768]{2,1,0:T(8,128)(2,1)S(1)} %copy-done.67), channel_id=1, source_target_pairs={{0,4},{4,0},{1,5},{5,1},{2,6},{6,2},{3,7},{7,3},{8,12},{12,8},{9,1... | collective-permute-start | bytes 2064392 | tf_op jit(solution)/shard_map/ppermute | solution.py:985
  243.7 24.5 %collective-permute-start.43 = (bf16[128,768]{1,0:T(8,128)(2,1)S(1)}, bf16[128,768]{1,0:T(8,128)(2,1)S(1)}, u32[]{:S(2)}, u32[]{:S(2)}) collective-permute-start(bf16[128,768]{1,0:T(8,128)(2,1)S(1)} %add_convert_fusion), channel_id=1, source_target_pairs={{0,1},{1,0},{2,3},{3,2},{4,5},{5,4},{6,7},{7,6},{8,9},{9,8},{10,11... | collective-permute-start | bytes 589832 | tf_op jit(solution)/shard_map/ppermute | solution.py:976
  245.1 18.0 %collective-permute-start.46 = (bf16[192,768]{1,0:T(8,128)(2,1)}, bf16[192,768]{1,0:T(8,128)(2,1)S(1)}, u32[]{:S(2)}, u32[]{:S(2)}) collective-permute-start(bf16[192,768]{1,0:T(8,128)(2,1)} %get-tuple-element.172), channel_id=1, source_target_pairs={{0,8},{8,16},{16,24},{24,0},{1,9},{9,17},{17,25},{25,1},{2,10},{10... | collective-permute-start | bytes 884744 | tf_op jit(solution)/shard_map/ppermute | solution.py:981
  248.9 14.2 %collective-permute-start.47 = (bf16[192,768]{1,0:T(8,128)(2,1)}, bf16[192,768]{1,0:T(8,128)(2,1)S(1)}, u32[]{:S(2)}, u32[]{:S(2)}) collective-permute-start(bf16[192,768]{1,0:T(8,128)(2,1)} %get-tuple-element.185), channel_id=1, source_target_pairs={{0,24},{8,0},{16,8},{24,16},{1,25},{9,1},{17,9},{25,17},{2,26},{10... | collective-permute-start | bytes 884744 | tf_op jit(solution)/shard_map/ppermute | solution.py:981
  249.4 25.6 %collective-permute-start.41 = (bf16[128,768]{1,0:T(8,128)(2,1)S(1)}, bf16[128,768]{1,0:T(8,128)(2,1)S(1)}, u32[]{:S(2)}, u32[]{:S(2)}) collective-permute-start(bf16[128,768]{1,0:T(8,128)(2,1)S(1)} %add_convert_fusion.1), channel_id=1, source_target_pairs={{0,1},{1,0},{2,3},{3,2},{4,5},{5,4},{6,7},{7,6},{8,9},{9,8},{10,11... | collective-permute-start | bytes 589832 | tf_op jit(solution)/shard_map/ppermute | solution.py:976
  265.5 20.7 %collective-permute-start.52 = (bf16[192,768]{1,0:T(8,128)(2,1)}, bf16[192,768]{1,0:T(8,128)(2,1)S(1)}, u32[]{:S(2)}, u32[]{:S(2)}) collective-permute-start(bf16[192,768]{1,0:T(8,128)(2,1)} %add_second.1), channel_id=1, source_target_pairs={{0,16},{8,24},{16,0},{24,8},{1,17},{9,25},{17,1},{25,9},{2,18},{10... | collective-permute-start | bytes 884744 | tf_op jit(solution)/shard_map/ppermute | solution.py:981
  283.6 12.9 %collective-permute-start.50 = (bf16[112,768]{1,0:T(8,128)(2,1)}, bf16[112,768]{1,0:T(8,128)(2,1)S(1)}, u32[]{:S(2)}, u32[]{:S(2)}) collective-permute-start(bf16[112,768]{1,0:T(8,128)(2,1)} %get-tuple-element.194), channel_id=1, source_target_pairs={{0,16},{8,24},{16,0},{24,8},{1,17},{9,25},{17,1},{25,9},{2,18},{10... | collective-permute-start | bytes 516104 | tf_op jit(solution)/shard_map/ppermute | solution.py:981
  283.6 13.9 %collective-permute-start.51 = (bf16[112,768]{1,0:T(8,128)(2,1)}, bf16[112,768]{1,0:T(8,128)(2,1)S(1)}, u32[]{:S(2)}, u32[]{:S(2)}) collective-permute-start(bf16[112,768]{1,0:T(8,128)(2,1)} %get-tuple-element.195), channel_id=1, source_target_pairs={{0,24},{8,0},{16,8},{24,16},{1,25},{9,1},{17,9},{25,17},{2,26},{10... | collective-permute-start | bytes 516104 | tf_op jit(solution)/shard_map/ppermute | solution.py:981
  285.7 16.7 %collective-permute-start.57 = (bf16[64,768]{1,0:T(8,128)(2,1)S(1)}, bf16[64,768]{1,0:T(8,128)(2,1)S(1)}, u32[]{:S(2)}, u32[]{:S(2)}) collective-permute-start(bf16[64,768]{1,0:T(8,128)(2,1)S(1)} %copy-done.76), channel_id=1, source_target_pairs={{0,1},{1,0},{2,3},{3,2},{4,5},{5,4},{6,7},{7,6},{8,9},{9,8},{10,11... | collective-permute-start | bytes 294920 | tf_op jit(solution)/shard_map/ppermute | solution.py:976
  286.2 16.0 %collective-permute-start.60 = (bf16[24,768]{1,0:T(8,128)(2,1)S(1)}, bf16[24,768]{1,0:T(8,128)(2,1)S(1)}, u32[]{:S(2)}, u32[]{:S(2)}) collective-permute-start(bf16[24,768]{1,0:T(8,128)(2,1)S(1)} %copy-done.77), channel_id=1, source_target_pairs={{0,0},{4,1},{8,2},{12,3},{16,4},{20,5},{24,6},{28,7},{1,8},{5,9},{... | collective-permute-start | bytes 110600 | tf_op jit(solution)/shard_map/ppermute | solution.py:1179
  296.5 13.6 %collective-permute-start.59 = (bf16[64,768]{1,0:T(8,128)(2,1)S(1)}, bf16[64,768]{1,0:T(8,128)(2,1)S(1)}, u32[]{:S(2)}, u32[]{:S(2)}) collective-permute-start(bf16[64,768]{1,0:T(8,128)(2,1)S(1)} %copy-done.74), channel_id=1, source_target_pairs={{0,3},{1,2},{2,1},{3,0},{4,7},{5,6},{6,5},{7,4},{8,11},{9,10},{10,... | collective-permute-start | bytes 294920 | tf_op jit(solution)/shard_map/ppermute | solution.py:976
  (108 other events, 1322.5 us)

commit v2 on v1

--- a/solution.py
+++ b/solution.py
@@ -1046,7 +1046,7 @@
     near = line_near(chunks[0])
     pieces = [near + [line_flip(p) for p in near]]
     near = line_near(after(chunks[1], near[2], pieces[0][5], pieces[0][7]))
-    pieces.append(near + [line_flip(p) for p in near])
+    pieces.append(near + [line_flip(p) for p in (chunks[1], *near[1:])])
     m_parts = [[(p, part(192, 0)) for p in group] for group in pieces]
     a_parts = [[(p, part(96, 192)) for p in group] for group in pieces]
     small_parts = [(p, part(16, 288)) for p in pieces[0]]
@@ -1070,7 +1070,7 @@
 
     ids_rows = jnp.pad(segment_ids.astype(BF)[None, :], ((0, TOK - 1), (0, D - TOK)))
     load = jnp.concatenate([tokens, cotangent, ids_rows], axis=0)
-    loads = gather_team(after(load, pieces[0][1], pieces[0][3], pieces[0][4]), pieces[0][2], pieces[0][5], pieces[0][7])
+    loads = gather_team(after(load, pieces[0][1], pieces[0][3], pieces[0][4], pieces[1][4]), pieces[0][2], pieces[0][5], pieces[0][7])
     token_slots = slots_of(loads)
     here = lax.axis_index("x")
     rows = jnp.arange(TOK, dtype=jnp.int32)
@@ -1197,29 +1197,34 @@
     dn, sum_m, m_keep0, m_first0, m_second0 = mlp_back(
         0, slots[0], grad_slots, [shape((4, 192, D), BF)] + [shape((2, 192, D), BF)] * 2
     )
-    a_added1 = add(block_a, a_keep1, after(a_other1, dn, *m_sums1), (1, 2, 3), (1, 2, 3), "add_attend")
+    m_first0 = line_flip(after(m_first0, m_sums1[0]))
+    m_second0 = line_flip(after(m_second0, m_sums1[0]))
+    a_keep0, a_other0, ns, _ = attend_back(
+        0, slots[0], grad_slots, (after(dn, m_sums1[0]), sum_m), m_second0
+    )
+    a_added1 = add(
+        block_a,
+        a_keep1,
+        after(a_other1, a_keep0, m_first0, *m_sums1),
+        (1, 2, 3),
+        (1, 2, 3),
+        "add_attend",
+    )
     a_sums1 = shifts(a_added1)
-    m_first0 = line_flip(after(m_first0, *a_added1))
-    m_second0 = line_flip(after(m_second0, *a_added1))
-    a_keep0, a_other0, ns, _ = attend_back(
-        0, slots[0], grad_slots, (after(dn, *a_added1), sum_m), m_second0
-    )
-    m1, m3 = add(
-        block_m, m_keep0, after(m_first0, a_keep0, *a_sums1), HALVES[0], (0, 1), "add_first"
-    )
+    m1, m3 = add(block_m, m_keep0, after(m_first0, *a_sums1), HALVES[0], (0, 1), "add_first")
     first_added = m1
     m1, m3 = line_shift(m1, 1), line_shift(m3, 3)
     (m2,) = add(block_m, m_keep0, after(m_second0, m1, m3), HALVES[1][:1], (0,), "add_second")
-    grad, _ = norm_back(0, grad, sum_team(*ns))
-    _, activations = residual(streams[1], (ys[0], ys[1], after(ys[2], first_added)))
+    grad, _ = norm_back(0, grad, sum_team(ns[0], ns[1], after(ns[2], a_added1[0])))
+    _, activations = residual(streams[1], (ys[0], ys[1], after(ys[2], a_added1[0])))
     e_keep, e_send = run(
         line_sum_body,
         [shape((EARLY, D), F32), shape((EARLY, D), BF)],
         "line_sum",
-        (e0, after(early[0], first_added), early[1], early[2]),
+        (e0, after(early[0], a_added1[0]), early[1], early[2]),
     )
     outs[1] = split(
-        (a_keep1, a_other1, *a_sums1),
+        (after(a_keep1, first_added), a_other1, *a_sums1),
         (m_keep1, one_of(m_other1, 0), *m_sums1),
         (e_keep, line_flip(e_send)),
     )

time: 323 us -> 315 us (0.975)
  waiting for transfers between devices: 130 us -> 121 us
    ppermute x21, waiting for transfers between devices: 63.8 us -> 47.5 us  [line_shift(): lax.ppermute(piece, 'z', [(i, (i + shift) % size) for i in range(size)])]
    ppermute x23, starting transfers between devices: 25.4 us -> 30 us  [team_send(): return lax.ppermute(piece, TEAM_AXES, flips)]
    ppermute x23, waiting for transfers between devices: 9.11 us -> 13.5 us  [team_send(): return lax.ppermute(piece, TEAM_AXES, flips)]
    ppermute x21, starting transfers between devices: 27.3 us -> 23.2 us  [line_shift(): lax.ppermute(piece, 'z', [(i, (i + shift) % size) for i in range(size)])]
    unnamed x159 -> x155, local copies, waits for them, and re-layouts: 11.6 us -> 10.7 us
  transfers between devices with their start and end apart: 61 -> 61, of which waited for: 21 -> 22; matrix products, arithmetic and copies ran while one was open for 2% -> 2% of each run, Pallas kernels for 21% -> 22%
where the time goes in v2:
time: 315 us; the launch traced here: 311 us
  waiting for transfers between devices  121 us (38%)
  Pallas kernels  86.4 us (27%)
  starting transfers between devices  80.3 us (25%)
  local copies, waits for them, and re-layouts  10.7 us (3%)
  other arithmetic  10.4 us (3%)
    pallas_call x21, Pallas kernels, run(): pl.pallas_call(body, grid=(1,), out_shape=out_shape, in_specs=[pl.BlockSp...  86.4 us
    ppermute x14, waiting for transfers between devices, line_flip(): return lax.ppermute(piece, 'y', [(0, 1), (1, 0)])  51.9 us
    ppermute x21, waiting for transfers between devices, line_shift(): lax.ppermute(piece, 'z', [(i, (i + shift) % size) for i in range(size)])  47.5 us
    ppermute x23, starting transfers between devices, team_send(): return lax.ppermute(piece, TEAM_AXES, flips)  30 us
    ppermute x21, starting transfers between devices, line_shift(): lax.ppermute(piece, 'z', [(i, (i + shift) % size) for i in range(size)])  23.2 us
    ppermute x23, waiting for transfers between devices, team_send(): return lax.ppermute(piece, TEAM_AXES, flips)  13.5 us
    ppermute x2, starting transfers between devices, split(): attn_rows = lax.ppermute(mine[TEAM + 1], everywhere, gather_back)  11.7 us
    unnamed x155, local copies, waits for them, and re-layouts  10.7 us
  transfers between devices with their start and end apart: 61, of which 22 were waited for; matrix products, arithmetic and copies ran while one was open for 2% of the time, Pallas kernels for 22%

profile of v2, /device:TPU:5, one launch (start us, length us, event | category | flops | bytes accessed | tf_op | source)
XLA Modules:
  0.0 311.1 jit_solution(16703936753168312382)
XLA Ops:
  5.9 5.6 %collective-permute-start.3 = (bf16[2,24,768]{2,1,0:T(8,128)(2,1)}, bf16[2,24,768]{2,1,0:T(8,128)(2,1)S(1)}, u32[]{:S(2)}, u32[]{:S(2)}) collective-permute-start(bf16[2,24,768]{2,1,0:T(8,128)(2,1)} %param.20), channel_id=1, source_target_pairs={{0,0},{1,4},{2,8},{3,12},{4,16},{5,20},{6,24},{7,28},{8,1},{9,5},{... | collective-permute-start | bytes 221192 | tf_op jit(solution)/shard_map/ppermute | solution.py:1039
  11.4 4.9 %collective-permute-done.3.attn_ref = bf16[2,24,768]{2,1,0:T(8,128)(2,1)S(1)} collective-permute-done((bf16[2,24,768]{2,1,0:T(8,128)(2,1)}, bf16[2,24,768]{2,1,0:T(8,128)(2,1)S(1)}, u32[]{:S(2)}, u32[]{:S(2)}) %collective-permute-start.3) | collective-permute-done | bytes 73760 | tf_op jit(solution)/shard_map/ppermute | solution.py:1039
  23.2 18.0 %collective-permute-done.7.refs_4_ = bf16[288,768]{1,0:T(8,128)(2,1)S(1)} collective-permute-done((bf16[288,768]{1,0:T(8,128)(2,1)}, bf16[288,768]{1,0:T(8,128)(2,1)S(1)}, u32[]{:S(2)}, u32[]{:S(2)}) %collective-permute-start.7) | collective-permute-done | bytes 442400 | tf_op jit(solution)/shard_map/ppermute | solution.py:985
  45.3 7.1 %collective-permute-done.11.refs_7_.refs_15_ = bf16[304,768]{1,0:T(8,128)(2,1)S(1)} collective-permute-done((bf16[304,768]{1,0:T(8,128)(2,1)S(1)}, bf16[304,768]{1,0:T(8,128)(2,1)S(1)}, u32[]{:S(2)}, u32[]{:S(2)}) %collective-permute-start.11) | collective-permute-done | bytes 466976 | tf_op jit(solution)/shard_map/ppermute | solution.py:985
  52.4 14.4 %collective-permute-done.9.refs_2_.refs_10_ = bf16[304,768]{1,0:T(8,128)(2,1)S(1)} collective-permute-done((bf16[304,768]{1,0:T(8,128)(2,1)}, bf16[304,768]{1,0:T(8,128)(2,1)S(1)}, u32[]{:S(2)}, u32[]{:S(2)}) %collective-permute-start.9) | collective-permute-done | bytes 466976 | tf_op jit(solution)/shard_map/ppermute | solution.py:981
  76.4 7.0 %collective-permute-done.13.refs_6_.refs_14_ = bf16[304,768]{1,0:T(8,128)(2,1)S(1)} collective-permute-done((bf16[304,768]{1,0:T(8,128)(2,1)S(1)}, bf16[304,768]{1,0:T(8,128)(2,1)S(1)}, u32[]{:S(2)}, u32[]{:S(2)}) %collective-permute-start.13) | collective-permute-done | bytes 466976 | tf_op jit(solution)/shard_map/ppermute | solution.py:985
  84.1 6.2 %attend_forward.1 = (f32[512,768]{1,0:T(8,128)}, f32[2,8,768]{2,1,0:T(8,128)}) custom-call(s32[3]{0:T(128)} %pad_add_fusion.1.me_ref, bf16[384,768]{1,0:T(8,128)(2,1)} %copy-done.1, bf16[384,768]{1,0:T(8,128)(2,1)} %copy-done.2, bf16[768,768]{1,0:T(8,128)(2,1)} %copy-done, bf16[768,768]{1,0:T(8,128)(2,1)} %copy-done, ...), custom_call_target="tpu_custom_call" | custom-call | tf_op jit(solution)/shard_map/attend_forward/pallas_call | solution.py:1012
  90.3 5.2 %mlp_forward.1 = (f32[128,768]{1,0:T(8,128)}, f32[128,768]{1,0:T(8,128)}, bf16[256,768]{1,0:T(8,128)(2,1)}) custom-call(s32[3]{0:T(128)} %pad_add_fusion.1.me_ref, bf16[384,768]{1,0:T(8,128)(2,1)} %copy-done.1, bf16[384,768]{1,0:T(8,128)(2,1)} %copy-done.2, bf16[768,768]{1,0:T(8,128)(2,1)} %copy-done, bf16[768,768]{1,0:T(8,128)(2,1)} %copy-done, ...), custom_call_target="tpu_custom_call" | custom-call | tf_op jit(solution)/shard_map/mlp_forward/pallas_call | solution.py:1012
  101.0 4.5 %collective-permute-done.15.y2 = bf16[128,768]{1,0:T(8,128)(2,1)S(1)} collective-permute-done((bf16[128,768]{1,0:T(8,128)(2,1)S(1)}, bf16[128,768]{1,0:T(8,128)(2,1)S(1)}, u32[]{:S(2)}, u32[]{:S(2)}) %collective-permute-start.15) | collective-permute-done | bytes 196640 | tf_op jit(solution)/shard_map/ppermute | solution.py:976
  109.7 9.5 %collective-permute-done.22.refs_2_ = bf16[288,768]{1,0:T(8,128)(2,1)S(1)} collective-permute-done((bf16[288,768]{1,0:T(8,128)(2,1)S(1)}, bf16[288,768]{1,0:T(8,128)(2,1)S(1)}, u32[]{:S(2)}, u32[]{:S(2)}) %collective-permute-start.22) | collective-permute-done | bytes 442400 | tf_op jit(solution)/shard_map/ppermute | solution.py:981
  121.9 8.2 %collective-permute-done.23.refs_6_ = bf16[288,768]{1,0:T(8,128)(2,1)S(1)} collective-permute-done((bf16[288,768]{1,0:T(8,128)(2,1)S(1)}, bf16[288,768]{1,0:T(8,128)(2,1)S(1)}, u32[]{:S(2)}, u32[]{:S(2)}) %collective-permute-start.23) | collective-permute-done | bytes 442400 | tf_op jit(solution)/shard_map/ppermute | solution.py:985
  131.6 8.0 %mlp_both.2 = (f32[512,768]{1,0:T(8,128)}, f32[8,768]{1,0:T(8,128)}, f32[512,768]{1,0:T(8,128)}, bf16[2,48,768]{2,1,0:T(8,128)(2,1)}, bf16[2,48,768]{2,1,0:T(8,1...) custom-call(s32[3]{0:T(128)} %pad_add_fusion.1.me_ref, ...), custom_call_target="tpu_custom_call" | custom-call | tf_op jit(solution)/shard_map/mlp_both/pallas_call | solution.py:1012
  143.4 11.7 %attend_both.2 = (bf16[4,112,768]{2,1,0:T(8,128)(2,1)}, bf16[4,112,768]{2,1,0:T(8,128)(2,1)}, f32[128,768]{1,0:T(8,128)}, f32[128,768]{1,0:T(8,128)}, bf16[256,7...) custom-call(s32[3]{0:T(128)} %pad_add_fusion.1.me_ref, ...), custom_call_target="tpu_custom_call" | custom-call | tf_op jit(solution)/shard_map/attend_both/pallas_call | solution.py:1012
  161.9 3.3 %collective-permute-done.30.n2 = bf16[128,768]{1,0:T(8,128)(2,1)S(1)} collective-permute-done((bf16[128,768]{1,0:T(8,128)(2,1)S(1)}, bf16[128,768]{1,0:T(8,128)(2,1)S(1)}, u32[]{:S(2)}, u32[]{:S(2)}) %collective-permute-start.30) | collective-permute-done | bytes 196640 | tf_op jit(solution)/shard_map/ppermute | solution.py:976
  169.8 3.5 %collective-permute-done.31.g1 = bf16[128,768]{1,0:T(8,128)(2,1)S(1)} collective-permute-done((bf16[128,768]{1,0:T(8,128)(2,1)}, bf16[128,768]{1,0:T(8,128)(2,1)S(1)}, u32[]{:S(2)}, u32[]{:S(2)}) %collective-permute-start.31) | collective-permute-done | bytes 196640 | tf_op jit(solution)/shard_map/ppermute | solution.py:976
  174.3 4.9 %collective-permute-start.32 = (bf16[256,768]{1,0:T(8,128)(2,1)S(1)}, bf16[256,768]{1,0:T(8,128)(2,1)S(1)}, u32[]{:S(2)}, u32[]{:S(2)}) collective-permute-start(bf16[256,768]{1,0:T(8,128)(2,1)S(1)} %pad_maximum_fusion.3), channel_id=1, source_target_pairs={{0,2},{1,3},{2,0},{3,1},{4,6},{5,7},{6,4},{7,5},{8,10},{9,11},{10,... | collective-permute-start | bytes 1179656 | tf_op jit(solution)/shard_map/ppermute | solution.py:976
  183.5 7.6 %mlp_both.3 = (f32[512,768]{1,0:T(8,128)}, f32[8,768]{1,0:T(8,128)}, bf16[4,192,768]{2,1,0:T(8,128)(2,1)}, bf16[2,192,768]{2,1,0:T(8,128)(2,1)}, bf16[2,192,768]{2,1,0:T(8,128)(2,1)}) custom-call(s32[3]{0:T(128)} %pad_add_fusion.1.me_ref, bf16[384,768]{1,0:T(8,128)(2,1)} %copy-done.1, bf16[384,768]{1,0:T(8,128)(2,1)} %copy-done.2, bf16[768,768]{1,0:T(8,128)(2,1)} %copy-done, ...), custom_call_target="tpu_custom_call" | custom-call | tf_op jit(solution)/shard_map/mlp_both/pallas_call | solution.py:1012
  196.5 11.3 %attend_both.3 = (bf16[4,112,768]{2,1,0:T(8,128)(2,1)}, bf16[4,112,768]{2,1,0:T(8,128)(2,1)}, f32[128,768]{1,0:T(8,128)}, f32[128,768]{1,0:T(8,128)}, bf16[256,768]{1,0:T(8,128)(2,1)}) custom-call(s32[3]{0:T(128)} %pad_add_fusion.1.me_ref, bf16[384,768]{1,0:T(8,128)(2,1)} %copy-done.1, bf16[384,768]{1,0:T(8,128)(2,1)} %copy-done.2, ...), custom_call_target="tpu_custom_call" | custom-call | tf_op jit(solution)/shard_map/attend_both/pallas_call | solution.py:1012
  207.9 3.6 %collective-permute-done.34.received = bf16[2,192,768]{2,1,0:T(8,128)(2,1)S(1)} collective-permute-done((bf16[2,192,768]{2,1,0:T(8,128)(2,1)}, bf16[2,192,768]{2,1,0:T(8,128)(2,1)S(1)}, u32[]{:S(2)}, u32[]{:S(2)}) %collective-permute-start.34) | collective-permute-done | bytes 589856 | tf_op jit(solution)/shard_map/ppermute | solution.py:985
  218.8 5.3 %collective-permute-done.41.received.refs_6_ = bf16[2,192,768]{2,1,0:T(8,128)(2,1)S(1)} collective-permute-done((bf16[2,192,768]{2,1,0:T(8,128)(2,1)}, bf16[2,192,768]{2,1,0:T(8,128)(2,1)S(1)}, u32[]{:S(2)}, u32[]{:S(2)}) %collective-permute-start.41) | collective-permute-done | bytes 589856 | tf_op jit(solution)/shard_map/ppermute | solution.py:985
  227.1 3.9 %collective-permute-done.43.refs_2_ = bf16[112,768]{1,0:T(8,128)(2,1)S(1)} collective-permute-done((bf16[112,768]{1,0:T(8,128)(2,1)}, bf16[112,768]{1,0:T(8,128)(2,1)S(1)}, u32[]{:S(2)}, u32[]{:S(2)}) %collective-permute-start.43) | collective-permute-done | bytes 172064 | tf_op jit(solution)/shard_map/ppermute | solution.py:981
  233.4 2.7 collective-permute-start.47
  238.4 4.9 %collective-permute-done.47.refs_9_ = bf16[192,768]{1,0:T(8,128)(2,1)S(1)} collective-permute-done((bf16[192,768]{1,0:T(8,128)(2,1)}, bf16[192,768]{1,0:T(8,128)(2,1)S(1)}, u32[]{:S(2)}, u32[]{:S(2)}) %collective-permute-start.47) | collective-permute-done | bytes 294944 | tf_op jit(solution)/shard_map/ppermute | solution.py:981
  243.4 9.2 %collective-permute-done.46.refs_7_ = bf16[192,768]{1,0:T(8,128)(2,1)S(1)} collective-permute-done((bf16[192,768]{1,0:T(8,128)(2,1)}, bf16[192,768]{1,0:T(8,128)(2,1)S(1)}, u32[]{:S(2)}, u32[]{:S(2)}) %collective-permute-start.46) | collective-permute-done | bytes 294944 | tf_op jit(solution)/shard_map/ppermute | solution.py:981
  257.5 2.7 collective-permute-done.48.refs_11_
  260.8 3.0 split_gradients.2
  279.0 5.4 %collective-permute-start.60 = (bf16[24,768]{1,0:T(8,128)(2,1)S(1)}, bf16[24,768]{1,0:T(8,128)(2,1)S(1)}, u32[]{:S(2)}, u32[]{:S(2)}) collective-permute-start(bf16[24,768]{1,0:T(8,128)(2,1)S(1)} %copy-done.75), channel_id=1, source_target_pairs={{0,0},{4,1},{8,2},{12,3},{16,4},{20,5},{24,6},{28,7},{1,8},{5,9},{... | collective-permute-start | bytes 110600 | tf_op jit(solution)/shard_map/ppermute | solution.py:1179
  285.5 3.1 %collective-permute-done.50.refs_3_ = bf16[112,768]{1,0:T(8,128)(2,1)S(1)} collective-permute-done((bf16[112,768]{1,0:T(8,128)(2,1)}, bf16[112,768]{1,0:T(8,128)(2,1)S(1)}, u32[]{:S(2)}, u32[]{:S(2)}) %collective-permute-start.50) | collective-permute-done | bytes 172064 | tf_op jit(solution)/shard_map/ppermute | solution.py:981
  290.9 3.0 split_gradients.3
  295.8 6.3 %collective-permute-start.56 = (bf16[24,768]{1,0:T(8,128)(2,1)}, bf16[24,768]{1,0:T(8,128)(2,1)S(1)}, u32[]{:S(2)}, u32[]{:S(2)}) collective-permute-start(bf16[24,768]{1,0:T(8,128)(2,1)} %get-tuple-element.206), channel_id=1, source_target_pairs={{0,0},{4,1},{8,2},{12,3},{16,4},{20,5},{24,6},{28,7},{1,8},{5,9},{... | collective-permute-start | bytes 110600 | tf_op jit(solution)/shard_map/ppermute | solution.py:1179
  302.1 3.6 %collective-permute-done.56.refs_6_ = bf16[24,768]{1,0:T(8,128)(2,1)S(1)} collective-permute-done((bf16[24,768]{1,0:T(8,128)(2,1)}, bf16[24,768]{1,0:T(8,128)(2,1)S(1)}, u32[]{:S(2)}, u32[]{:S(2)}) %collective-permute-start.56) | collective-permute-done | bytes 36896 | tf_op jit(solution)/shard_map/ppermute | solution.py:1179
  306.5 2.9 unpack_gradients.1
  (291 shorter events, 108.8 us)
Async XLA Ops:
  19.6 21.6 %collective-permute-start.6 = (bf16[304,768]{1,0:T(8,128)(2,1)}, bf16[304,768]{1,0:T(8,128)(2,1)S(1)}, u32[]{:S(2)}, u32[]{:S(2)}) collective-permute-start(bf16[304,768]{1,0:T(8,128)(2,1)} %get-tuple-element.126.refs_0_.refs_8_), channel_id=1, source_target_pairs={{0,4},{4,0},{1,5},{5,1},{2,6},{6,2},{3,7},{7,3},{8,12},{12,8},{9,1... | collective-permute-start | bytes 1400840 | tf_op jit(solution)/shard_map/ppermute | solution.py:985
  19.6 21.6 %collective-permute-start.5 = (bf16[304,768]{1,0:T(8,128)(2,1)}, bf16[304,768]{1,0:T(8,128)(2,1)S(1)}, u32[]{:S(2)}, u32[]{:S(2)}) collective-permute-start(bf16[304,768]{1,0:T(8,128)(2,1)} %get-tuple-element.126.refs_0_.refs_8_), channel_id=1, source_target_pairs={{0,24},{8,0},{16,8},{24,16},{1,25},{9,1},{17,9},{25,17},{2,26},{10... | collective-permute-start | bytes 1400840 | tf_op jit(solution)/shard_map/ppermute | solution.py:981
  21.6 20.8 %collective-permute-start.4 = (bf16[304,768]{1,0:T(8,128)(2,1)}, bf16[304,768]{1,0:T(8,128)(2,1)S(1)}, u32[]{:S(2)}, u32[]{:S(2)}) collective-permute-start(bf16[304,768]{1,0:T(8,128)(2,1)} %get-tuple-element.126.refs_0_.refs_8_), channel_id=1, source_target_pairs={{0,8},{8,16},{16,24},{24,0},{1,9},{9,17},{17,25},{25,1},{2,10},{10... | collective-permute-start | bytes 1400840 | tf_op jit(solution)/shard_map/ppermute | solution.py:981
  21.6 19.6 %collective-permute-start.7 = (bf16[288,768]{1,0:T(8,128)(2,1)}, bf16[288,768]{1,0:T(8,128)(2,1)S(1)}, u32[]{:S(2)}, u32[]{:S(2)}) collective-permute-start(bf16[288,768]{1,0:T(8,128)(2,1)} %get-tuple-element.138.refs_0_), channel_id=1, source_target_pairs={{0,4},{4,0},{1,5},{5,1},{2,6},{6,2},{3,7},{7,3},{8,12},{12,8},{9,1... | collective-permute-start | bytes 1327112 | tf_op jit(solution)/shard_map/ppermute | solution.py:985
  42.4 24.4 %collective-permute-start.8 = (bf16[384,768]{1,0:T(8,128)(2,1)S(1)}, bf16[384,768]{1,0:T(8,128)(2,1)S(1)}, u32[]{:S(2)}, u32[]{:S(2)}) collective-permute-start(bf16[384,768]{1,0:T(8,128)(2,1)S(1)} %fusion.1.x0.g0), channel_id=1, source_target_pairs={{0,1},{1,0},{2,3},{3,2},{4,5},{5,4},{6,7},{7,6},{8,9},{9,8},{10,11... | collective-permute-start | bytes 1769480 | tf_op jit(solution)/shard_map/ppermute | solution.py:976
  44.4 22.4 %collective-permute-start.9 = (bf16[304,768]{1,0:T(8,128)(2,1)}, bf16[304,768]{1,0:T(8,128)(2,1)S(1)}, u32[]{:S(2)}, u32[]{:S(2)}) collective-permute-start(bf16[304,768]{1,0:T(8,128)(2,1)} %get-tuple-element.126.refs_0_.refs_8_), channel_id=1, source_target_pairs={{0,16},{8,24},{16,0},{24,8},{1,17},{9,25},{17,1},{25,9},{2,18},{10... | collective-permute-start | bytes 1400840 | tf_op jit(solution)/shard_map/ppermute | solution.py:981
  44.7 22.2 %collective-permute-start.10 = (bf16[304,768]{1,0:T(8,128)(2,1)S(1)}, bf16[304,768]{1,0:T(8,128)(2,1)S(1)}, u32[]{:S(2)}, u32[]{:S(2)}) collective-permute-start(bf16[304,768]{1,0:T(8,128)(2,1)S(1)} %collective-permute-done.4.refs_1_.refs_9_), channel_id=1, source_target_pairs={{0,4},{4,0},{1,5},{5,1},{2,6},{6,2},{3,7},{7,3},{8,12},{12,8},{9,1... | collective-permute-start | bytes 1400840 | tf_op jit(solution)/shard_map/ppermute | solution.py:985
  70.0 26.9 %collective-permute-start.19 = (bf16[288,768]{1,0:T(8,128)(2,1)}, bf16[288,768]{1,0:T(8,128)(2,1)S(1)}, u32[]{:S(2)}, u32[]{:S(2)}) collective-permute-start(bf16[288,768]{1,0:T(8,128)(2,1)} %get-tuple-element.138.refs_0_), channel_id=1, source_target_pairs={{0,24},{8,0},{16,8},{24,16},{1,25},{9,1},{17,9},{25,17},{2,26},{10... | collective-permute-start | bytes 1327112 | tf_op jit(solution)/shard_map/ppermute | solution.py:981
  71.2 25.8 %collective-permute-start.17 = (bf16[288,768]{1,0:T(8,128)(2,1)}, bf16[288,768]{1,0:T(8,128)(2,1)S(1)}, u32[]{:S(2)}, u32[]{:S(2)}) collective-permute-start(bf16[288,768]{1,0:T(8,128)(2,1)} %get-tuple-element.138.refs_0_), channel_id=1, source_target_pairs={{0,8},{8,16},{16,24},{24,0},{1,9},{9,17},{17,25},{25,1},{2,10},{10... | collective-permute-start | bytes 1327112 | tf_op jit(solution)/shard_map/ppermute | solution.py:981
  97.0 22.2 %collective-permute-start.22 = (bf16[288,768]{1,0:T(8,128)(2,1)S(1)}, bf16[288,768]{1,0:T(8,128)(2,1)S(1)}, u32[]{:S(2)}, u32[]{:S(2)}) collective-permute-start(bf16[288,768]{1,0:T(8,128)(2,1)S(1)} %copy-done.17), channel_id=1, source_target_pairs={{0,16},{8,24},{16,0},{24,8},{1,17},{9,25},{17,1},{25,9},{2,18},{10... | collective-permute-start | bytes 1327112 | tf_op jit(solution)/shard_map/ppermute | solution.py:981
  97.1 22.5 %collective-permute-start.20 = (bf16[288,768]{1,0:T(8,128)(2,1)S(1)}, bf16[288,768]{1,0:T(8,128)(2,1)S(1)}, u32[]{:S(2)}, u32[]{:S(2)}) collective-permute-start(bf16[288,768]{1,0:T(8,128)(2,1)S(1)} %collective-permute-done.19.refs_3_), channel_id=1, source_target_pairs={{0,4},{4,0},{1,5},{5,1},{2,6},{6,2},{3,7},{7,3},{8,12},{12,8},{9,1... | collective-permute-start | bytes 1327112 | tf_op jit(solution)/shard_map/ppermute | solution.py:985
  97.7 21.9 %collective-permute-start.18 = (bf16[288,768]{1,0:T(8,128)(2,1)S(1)}, bf16[288,768]{1,0:T(8,128)(2,1)S(1)}, u32[]{:S(2)}, u32[]{:S(2)}) collective-permute-start(bf16[288,768]{1,0:T(8,128)(2,1)S(1)} %collective-permute-done.17.refs_1_), channel_id=1, source_target_pairs={{0,4},{4,0},{1,5},{5,1},{2,6},{6,2},{3,7},{7,3},{8,12},{12,8},{9,1... | collective-permute-start | bytes 1327112 | tf_op jit(solution)/shard_map/ppermute | solution.py:985
  139.6 19.7 %collective-permute-start.29 = (bf16[4,144,768]{2,1,0:T(8,128)(2,1)}, bf16[4,144,768]{2,1,0:T(8,128)(2,1)S(1)}, u32[]{:S(2)}, u32[]{:S(2)}) collective-permute-start(bf16[4,144,768]{2,1,0:T(8,128)(2,1)} %get-tuple-element.152), channel_id=1, source_target_pairs={{0,4},{4,0},{1,5},{5,1},{2,6},{6,2},{3,7},{7,3},{8,12},{12,8},{9,1... | collective-permute-start | bytes 2654216 | tf_op jit(solution)/shard_map/ppermute | solution.py:985
  140.0 15.1 %collective-permute-start.25 = (bf16[2,48,768]{2,1,0:T(8,128)(2,1)}, bf16[2,48,768]{2,1,0:T(8,128)(2,1)S(1)}, u32[]{:S(2)}, u32[]{:S(2)}) collective-permute-start(bf16[2,48,768]{2,1,0:T(8,128)(2,1)} %get-tuple-element.148), channel_id=1, source_target_pairs={{0,8},{8,16},{16,24},{24,0},{1,9},{9,17},{17,25},{25,1},{2,10},{10... | collective-permute-start | bytes 442376 | tf_op jit(solution)/shard_map/ppermute | solution.py:981
  140.8 14.3 %collective-permute-start.26 = (bf16[2,48,768]{2,1,0:T(8,128)(2,1)}, bf16[2,48,768]{2,1,0:T(8,128)(2,1)S(1)}, u32[]{:S(2)}, u32[]{:S(2)}) collective-permute-start(bf16[2,48,768]{2,1,0:T(8,128)(2,1)} %get-tuple-element.149), channel_id=1, source_target_pairs={{0,16},{8,24},{16,0},{24,8},{1,17},{9,25},{17,1},{25,9},{2,18},{10... | collective-permute-start | bytes 442376 | tf_op jit(solution)/shard_map/ppermute | solution.py:981
  182.1 25.7 %collective-permute-start.24 = (bf16[4,112,768]{2,1,0:T(8,128)(2,1)S(1)}, bf16[4,112,768]{2,1,0:T(8,128)(2,1)S(1)}, u32[]{:S(2)}, u32[]{:S(2)}) collective-permute-start(bf16[4,112,768]{2,1,0:T(8,128)(2,1)S(1)} %copy-done.68), channel_id=1, source_target_pairs={{0,4},{4,0},{1,5},{5,1},{2,6},{6,2},{3,7},{7,3},{8,12},{12,8},{9,1... | collective-permute-start | bytes 2064392 | tf_op jit(solution)/shard_map/ppermute | solution.py:985
  191.1 20.3 %collective-permute-start.34 = (bf16[2,192,768]{2,1,0:T(8,128)(2,1)}, bf16[2,192,768]{2,1,0:T(8,128)(2,1)S(1)}, u32[]{:S(2)}, u32[]{:S(2)}) collective-permute-start(bf16[2,192,768]{2,1,0:T(8,128)(2,1)} %get-tuple-element.167), channel_id=1, source_target_pairs={{0,4},{4,0},{1,5},{5,1},{2,6},{6,2},{3,7},{7,3},{8,12},{12,8},{9,1... | collective-permute-start | bytes 1769480 | tf_op jit(solution)/shard_map/ppermute | solution.py:985
  192.1 32.1 %collective-permute-start.41 = (bf16[2,192,768]{2,1,0:T(8,128)(2,1)}, bf16[2,192,768]{2,1,0:T(8,128)(2,1)S(1)}, u32[]{:S(2)}, u32[]{:S(2)}) collective-permute-start(bf16[2,192,768]{2,1,0:T(8,128)(2,1)} %get-tuple-element.181), channel_id=1, source_target_pairs={{0,4},{4,0},{1,5},{5,1},{2,6},{6,2},{3,7},{7,3},{8,12},{12,8},{9,1... | collective-permute-start | bytes 1769480 | tf_op jit(solution)/shard_map/ppermute | solution.py:985
  192.7 15.2 %collective-permute-start.35 = (bf16[144,768]{1,0:T(8,128)(2,1)S(1)}, bf16[144,768]{1,0:T(8,128)(2,1)S(1)}, u32[]{:S(2)}, u32[]{:S(2)}) collective-permute-start(bf16[144,768]{1,0:T(8,128)(2,1)S(1)} %copy-done.71), channel_id=1, source_target_pairs={{0,16},{8,24},{16,0},{24,8},{1,17},{9,25},{17,1},{25,9},{2,18},{10... | collective-permute-start | bytes 663560 | tf_op jit(solution)/shard_map/ppermute | solution.py:981
  194.1 13.8 %collective-permute-start.36 = (bf16[144,768]{1,0:T(8,128)(2,1)S(1)}, bf16[144,768]{1,0:T(8,128)(2,1)S(1)}, u32[]{:S(2)}, u32[]{:S(2)}) collective-permute-start(bf16[144,768]{1,0:T(8,128)(2,1)S(1)} %copy-done.70), channel_id=1, source_target_pairs={{0,24},{8,0},{16,8},{24,16},{1,25},{9,1},{17,9},{25,17},{2,26},{10... | collective-permute-start | bytes 663560 | tf_op jit(solution)/shard_map/ppermute | solution.py:981
  213.8 22.8 %collective-permute-start.37 = (bf16[256,768]{1,0:T(8,128)(2,1)S(1)}, bf16[256,768]{1,0:T(8,128)(2,1)S(1)}, u32[]{:S(2)}, u32[]{:S(2)}) collective-permute-start(bf16[256,768]{1,0:T(8,128)(2,1)S(1)} %copy-done.69), channel_id=1, source_target_pairs={{0,2},{1,3},{2,0},{3,1},{4,6},{5,7},{6,4},{7,5},{8,10},{9,11},{10,... | collective-permute-start | bytes 1179656 | tf_op jit(solution)/shard_map/ppermute | solution.py:976
  224.1 13.7 %collective-permute-start.39 = (bf16[256,768]{1,0:T(8,128)(2,1)}, bf16[256,768]{1,0:T(8,128)(2,1)S(1)}, u32[]{:S(2)}, u32[]{:S(2)}) collective-permute-start(bf16[256,768]{1,0:T(8,128)(2,1)} %get-tuple-element.176), channel_id=1, source_target_pairs={{0,2},{1,3},{2,0},{3,1},{4,6},{5,7},{6,4},{7,5},{8,10},{9,11},{10,... | collective-permute-start | bytes 1179656 | tf_op jit(solution)/shard_map/ppermute | solution.py:976
  226.4 43.4 %collective-permute-start.42 = (bf16[4,112,768]{2,1,0:T(8,128)(2,1)S(1)}, bf16[4,112,768]{2,1,0:T(8,128)(2,1)S(1)}, u32[]{:S(2)}, u32[]{:S(2)}) collective-permute-start(bf16[4,112,768]{2,1,0:T(8,128)(2,1)S(1)} %copy-done.67), channel_id=1, source_target_pairs={{0,4},{4,0},{1,5},{5,1},{2,6},{6,2},{3,7},{7,3},{8,12},{12,8},{9,1... | collective-permute-start | bytes 2064392 | tf_op jit(solution)/shard_map/ppermute | solution.py:985
  236.1 16.5 %collective-permute-start.46 = (bf16[192,768]{1,0:T(8,128)(2,1)}, bf16[192,768]{1,0:T(8,128)(2,1)S(1)}, u32[]{:S(2)}, u32[]{:S(2)}) collective-permute-start(bf16[192,768]{1,0:T(8,128)(2,1)} %get-tuple-element.187), channel_id=1, source_target_pairs={{0,8},{8,16},{16,24},{24,0},{1,9},{9,17},{17,25},{25,1},{2,10},{10... | collective-permute-start | bytes 884744 | tf_op jit(solution)/shard_map/ppermute | solution.py:981
  236.8 27.0 %collective-permute-start.38 = (bf16[128,768]{1,0:T(8,128)(2,1)S(1)}, bf16[128,768]{1,0:T(8,128)(2,1)S(1)}, u32[]{:S(2)}, u32[]{:S(2)}) collective-permute-start(bf16[128,768]{1,0:T(8,128)(2,1)S(1)} %add_convert_fusion.1), channel_id=1, source_target_pairs={{0,1},{1,0},{2,3},{3,2},{4,5},{5,4},{6,7},{7,6},{8,9},{9,8},{10,11... | collective-permute-start | bytes 589832 | tf_op jit(solution)/shard_map/ppermute | solution.py:976
  237.9 28.8 %collective-permute-start.40 = (bf16[128,768]{1,0:T(8,128)(2,1)S(1)}, bf16[128,768]{1,0:T(8,128)(2,1)S(1)}, u32[]{:S(2)}, u32[]{:S(2)}) collective-permute-start(bf16[128,768]{1,0:T(8,128)(2,1)S(1)} %add_convert_fusion), channel_id=1, source_target_pairs={{0,1},{1,0},{2,3},{3,2},{4,5},{5,4},{6,7},{7,6},{8,9},{9,8},{10,11... | collective-permute-start | bytes 589832 | tf_op jit(solution)/shard_map/ppermute | solution.py:976
  254.9 24.2 %collective-permute-start.52 = (bf16[192,768]{1,0:T(8,128)(2,1)}, bf16[192,768]{1,0:T(8,128)(2,1)S(1)}, u32[]{:S(2)}, u32[]{:S(2)}) collective-permute-start(bf16[192,768]{1,0:T(8,128)(2,1)} %add_second.1), channel_id=1, source_target_pairs={{0,16},{8,24},{16,0},{24,8},{1,17},{9,25},{17,1},{25,9},{2,18},{10... | collective-permute-start | bytes 884744 | tf_op jit(solution)/shard_map/ppermute | solution.py:981
  274.2 14.4 %collective-permute-start.50 = (bf16[112,768]{1,0:T(8,128)(2,1)}, bf16[112,768]{1,0:T(8,128)(2,1)S(1)}, u32[]{:S(2)}, u32[]{:S(2)}) collective-permute-start(bf16[112,768]{1,0:T(8,128)(2,1)} %get-tuple-element.198), channel_id=1, source_target_pairs={{0,16},{8,24},{16,0},{24,8},{1,17},{9,25},{17,1},{25,9},{2,18},{10... | collective-permute-start | bytes 516104 | tf_op jit(solution)/shard_map/ppermute | solution.py:981
  275.5 14.7 %collective-permute-start.51 = (bf16[112,768]{1,0:T(8,128)(2,1)}, bf16[112,768]{1,0:T(8,128)(2,1)S(1)}, u32[]{:S(2)}, u32[]{:S(2)}) collective-permute-start(bf16[112,768]{1,0:T(8,128)(2,1)} %get-tuple-element.199), channel_id=1, source_target_pairs={{0,24},{8,0},{16,8},{24,16},{1,25},{9,1},{17,9},{25,17},{2,26},{10... | collective-permute-start | bytes 516104 | tf_op jit(solution)/shard_map/ppermute | solution.py:981
  277.9 17.1 %collective-permute-start.57 = (bf16[64,768]{1,0:T(8,128)(2,1)S(1)}, bf16[64,768]{1,0:T(8,128)(2,1)S(1)}, u32[]{:S(2)}, u32[]{:S(2)}) collective-permute-start(bf16[64,768]{1,0:T(8,128)(2,1)S(1)} %copy-done.74), channel_id=1, source_target_pairs={{0,1},{1,0},{2,3},{3,2},{4,5},{5,4},{6,7},{7,6},{8,9},{9,8},{10,11... | collective-permute-start | bytes 294920 | tf_op jit(solution)/shard_map/ppermute | solution.py:976
  279.0 15.3 %collective-permute-start.60 = (bf16[24,768]{1,0:T(8,128)(2,1)S(1)}, bf16[24,768]{1,0:T(8,128)(2,1)S(1)}, u32[]{:S(2)}, u32[]{:S(2)}) collective-permute-start(bf16[24,768]{1,0:T(8,128)(2,1)S(1)} %copy-done.75), channel_id=1, source_target_pairs={{0,0},{4,1},{8,2},{12,3},{16,4},{20,5},{24,6},{28,7},{1,8},{5,9},{... | collective-permute-start | bytes 110600 | tf_op jit(solution)/shard_map/ppermute | solution.py:1179
  288.6 13.5 %collective-permute-start.59 = (bf16[64,768]{1,0:T(8,128)(2,1)S(1)}, bf16[64,768]{1,0:T(8,128)(2,1)S(1)}, u32[]{:S(2)}, u32[]{:S(2)}) collective-permute-start(bf16[64,768]{1,0:T(8,128)(2,1)S(1)} %copy-done.72), channel_id=1, source_target_pairs={{0,3},{1,2},{2,1},{3,0},{4,7},{5,6},{6,5},{7,4},{8,11},{9,10},{10,... | collective-permute-start | bytes 294920 | tf_op jit(solution)/shard_map/ppermute | solution.py:976
  (106 other events, 1153.4 us)

commit v3 on v1

--- a/solution.py
+++ b/solution.py
@@ -585,6 +585,12 @@
 def add_body(slots, places, me_ref, keep, received, *outs):
     for s, n, out in zip(slots, places, outs):
         out[...] = (keep[s].astype(F32) + received[n].astype(F32)).astype(BF)
+
+
+def add_both_body(slots, places, me_ref, m_keep, m_received, a_keep, a_received, *outs):
+    for s, n, out in zip(slots, places, outs):
+        out[0:192] = (m_keep[s].astype(F32) + m_received[n].astype(F32)).astype(BF)
+        out[192:304] = (a_keep[s].astype(F32) + a_received[s].astype(F32)).astype(BF)
 
 
 def line_sum_body(me_ref, own, r1, r2, r3, keep_ref, send_ref):
@@ -895,7 +901,8 @@
     outs, (down_ref, attn_ref, small_ref), refs = refs[-7:-3], refs[-3:], refs[:-7]
     split_attend(me_ref, refs[:5], outs, attn_ref, small_ref)
     refs = refs[5:]
-    rest = total([refs[0][0], refs[1][0], refs[2][...], refs[3][...], refs[4][...]])
+    size = refs[0].shape[1]
+    rest = total([refs[0][0], refs[1][0]] + [ref[0:size, :] for ref in refs[2:5]])
     if early:
         rest = jnp.concatenate([total([refs[5][...], refs[6][...]]), rest], axis=0)
     down_ref[...] = rest[96:192]
@@ -908,7 +915,7 @@
 
 def split_attend(me_ref, refs, outs, attn_ref, small_ref):
     me = me_ref[0]
-    attn = total([refs[0][0], refs[1][0], refs[2][...], refs[3][...], refs[4][...]])
+    attn = total([refs[0][0], refs[1][0]] + [ref[-112:, :] for ref in refs[2:]])
     side = attn[0:96, MINE:]
     attn_ref[...] = jnp.concatenate(
         [side[24 * n : 24 * (n + 1)] for n in range(4)], axis=1
@@ -1046,7 +1053,7 @@
     near = line_near(chunks[0])
     pieces = [near + [line_flip(p) for p in near]]
     near = line_near(after(chunks[1], near[2], pieces[0][5], pieces[0][7]))
-    pieces.append(near + [line_flip(p) for p in near])
+    pieces.append(near + [line_flip(p) for p in (chunks[1], *near[1:])])
     m_parts = [[(p, part(192, 0)) for p in group] for group in pieces]
     a_parts = [[(p, part(96, 192)) for p in group] for group in pieces]
     small_parts = [(p, part(16, 288)) for p in pieces[0]]
@@ -1070,7 +1077,7 @@
 
     ids_rows = jnp.pad(segment_ids.astype(BF)[None, :], ((0, TOK - 1), (0, D - TOK)))
     load = jnp.concatenate([tokens, cotangent, ids_rows], axis=0)
-    loads = gather_team(after(load, pieces[0][1], pieces[0][3], pieces[0][4]), pieces[0][2], pieces[0][5], pieces[0][7])
+    loads = gather_team(after(load, pieces[0][1], pieces[0][3], pieces[0][4], pieces[1][4]), pieces[0][2], pieces[0][5], pieces[0][7])
     token_slots = slots_of(loads)
     here = lax.axis_index("x")
     rows = jnp.arange(TOK, dtype=jnp.int32)
@@ -1197,20 +1204,25 @@
     dn, sum_m, m_keep0, m_first0, m_second0 = mlp_back(
         0, slots[0], grad_slots, [shape((4, 192, D), BF)] + [shape((2, 192, D), BF)] * 2
     )
-    a_added1 = add(block_a, a_keep1, after(a_other1, dn, *m_sums1), (1, 2, 3), (1, 2, 3), "add_attend")
-    a_sums1 = shifts(a_added1)
-    m_first0 = line_flip(after(m_first0, *a_added1))
-    m_second0 = line_flip(after(m_second0, *a_added1))
+    m_first0 = line_flip(after(m_first0, m_sums1[0]))
+    m_second0 = line_flip(after(m_second0, m_sums1[0]))
     a_keep0, a_other0, ns, _ = attend_back(
-        0, slots[0], grad_slots, (after(dn, *a_added1), sum_m), m_second0
-    )
-    m1, m3 = add(
-        block_m, m_keep0, after(m_first0, a_keep0, *a_sums1), HALVES[0], (0, 1), "add_first"
-    )
-    first_added = m1
-    m1, m3 = line_shift(m1, 1), line_shift(m3, 3)
-    (m2,) = add(block_m, m_keep0, after(m_second0, m1, m3), HALVES[1][:1], (0,), "add_second")
-    grad, _ = norm_back(0, grad, sum_team(*ns))
+        0, slots[0], grad_slots, (after(dn, m_sums1[0]), sum_m)
+    )
+    block_both = shape((304, D), BF)
+
+    def add_both(other, slots, places, name):
+        return run(
+            partial(add_both_body, slots, places),
+            [block_both] * len(slots),
+            name,
+            (m_keep0, other, a_keep1, a_other1),
+        )
+
+    both1, both3 = add_both(after(m_first0, a_keep0, a_other1, *m_sums1), HALVES[0], (0, 1), "add_first")
+    first_added = both1
+    both1, both3 = line_shift(both1, 1), line_shift(both3, 3)
+    grad, _ = norm_back(0, grad, sum_team(ns[0], ns[1], after(ns[2], first_added)))
     _, activations = residual(streams[1], (ys[0], ys[1], after(ys[2], first_added)))
     e_keep, e_send = run(
         line_sum_body,
@@ -1218,22 +1230,22 @@
         "line_sum",
         (e0, after(early[0], first_added), early[1], early[2]),
     )
+    e_other = line_flip(e_send)
+    (both2,) = add_both(
+        after(m_second0, both1, both3, grad, activations, e_other), HALVES[1][:1], (0,), "add_second"
+    )
+    a_added0 = add(
+        block_a, a_keep0, after(a_other0, both2), (1, 2, 3), (1, 2, 3), "add_attend"
+    )
+    both2 = line_shift(both2, 2)
+    a_sums0 = shifts([after(piece, both2) for piece in a_added0])
+    both = (both1, both2, both3)
     outs[1] = split(
-        (a_keep1, a_other1, *a_sums1),
-        (m_keep1, one_of(m_other1, 0), *m_sums1),
-        (e_keep, line_flip(e_send)),
-    )
-    a_added0 = add(
-        block_a,
-        a_keep0,
-        after(a_other0, m2, grad, activations, outs[1][0]),
-        (1, 2, 3),
-        (1, 2, 3),
-        "add_attend",
-    )
-    m2 = line_shift(m2, 2)
-    a_sums0 = shifts(a_added0)
-    outs[0] = split((a_keep0, a_other0, *a_sums0), (m_keep0, one_of(m_second0, 1), m1, m2, m3))
+        (a_keep1, a_other1, *both), (m_keep1, one_of(m_other1, 0), *m_sums1), (e_keep, e_other)
+    )
+    outs[0] = split(
+        (a_keep0, after(a_other0, outs[1][0]), *a_sums0), (m_keep0, one_of(m_second0, 1), *both)
+    )
     row_24 = shape((LAYERS, 24), F32)
     final = run(
         unpack_body,

time: 323 us -> 316 us (0.978)
  starting transfers between devices: 78.4 us -> 74.8 us
    ppermute x21 -> x18, waiting for transfers between devices: 63.8 us -> 47.4 us  [line_shift(): lax.ppermute(piece, 'z', [(i, (i + shift) % size) for i in range(size)])]
    ppermute x23, waiting for transfers between devices: 9.11 us -> 18.5 us  [team_send(): return lax.ppermute(piece, TEAM_AXES, flips)]
    ppermute x14, waiting for transfers between devices: 48.7 us -> 56.9 us  [line_flip(): return lax.ppermute(piece, 'y', [(0, 1), (1, 0)])]
    ppermute x21 -> x18, starting transfers between devices: 27.3 us -> 19.9 us  [line_shift(): lax.ppermute(piece, 'z', [(i, (i + shift) % size) for i in range(size)])]
    unnamed x159 -> x145, local copies, waits for them, and re-layouts: 11.6 us -> 9.59 us
    pallas_call x21 -> x20, Pallas kernels: 86.4 us -> 85.7 us  [run(): pl.pallas_call(body, grid=(1,), out_shape=out_shape, in_specs=[pl.BlockSp...]
  transfers between devices with their start and end apart: 61 -> 58, of which waited for: 21 -> 20; matrix products, arithmetic and copies ran while one was open for 2% -> 2% of each run, Pallas kernels for 21% -> 21%
where the time goes in v3:
time: 316 us; the launch traced here: 313 us
  waiting for transfers between devices  130 us (41%)
  Pallas kernels  85.7 us (27%)
  starting transfers between devices  74.8 us (24%)
  other arithmetic  10.3 us (3%)
  local copies, waits for them, and re-layouts  9.6 us (3%)
    pallas_call x20, Pallas kernels, run(): pl.pallas_call(body, grid=(1,), out_shape=out_shape, in_specs=[pl.BlockSp...  85.7 us
    ppermute x14, waiting for transfers between devices, line_flip(): return lax.ppermute(piece, 'y', [(0, 1), (1, 0)])  56.9 us
    ppermute x18, waiting for transfers between devices, line_shift(): lax.ppermute(piece, 'z', [(i, (i + shift) % size) for i in range(size)])  47.4 us
    ppermute x23, starting transfers between devices, team_send(): return lax.ppermute(piece, TEAM_AXES, flips)  28.3 us
    ppermute x18, starting transfers between devices, line_shift(): lax.ppermute(piece, 'z', [(i, (i + shift) % size) for i in range(size)])  19.9 us
    ppermute x23, waiting for transfers between devices, team_send(): return lax.ppermute(piece, TEAM_AXES, flips)  18.5 us
    ppermute x2, starting transfers between devices, split(): attn_rows = lax.ppermute(mine[TEAM + 1], everywhere, gather_back)  11 us
    ppermute x14, starting transfers between devices, line_flip(): return lax.ppermute(piece, 'y', [(0, 1), (1, 0)])  10.1 us
  transfers between devices with their start and end apart: 58, of which 20 were waited for; matrix products, arithmetic and copies ran while one was open for 2% of the time, Pallas kernels for 21%

profile of v3, /device:TPU:5, one launch (start us, length us, event | category | flops | bytes accessed | tf_op | source)
XLA Modules:
  0.0 312.6 jit_solution(3788189858108121654)
XLA Ops:
  5.9 5.6 %collective-permute-start.3 = (bf16[2,24,768]{2,1,0:T(8,128)(2,1)}, bf16[2,24,768]{2,1,0:T(8,128)(2,1)S(1)}, u32[]{:S(2)}, u32[]{:S(2)}) collective-permute-start(bf16[2,24,768]{2,1,0:T(8,128)(2,1)} %param.20), channel_id=1, source_target_pairs={{0,0},{1,4},{2,8},{3,12},{4,16},{5,20},{6,24},{7,28},{8,1},{9,5},{... | collective-permute-start | bytes 221192 | tf_op jit(solution)/shard_map/ppermute | solution.py:1046
  11.4 4.9 %collective-permute-done.3.attn_ref = bf16[2,24,768]{2,1,0:T(8,128)(2,1)S(1)} collective-permute-done((bf16[2,24,768]{2,1,0:T(8,128)(2,1)}, bf16[2,24,768]{2,1,0:T(8,128)(2,1)S(1)}, u32[]{:S(2)}, u32[]{:S(2)}) %collective-permute-start.3) | collective-permute-done | bytes 73760 | tf_op jit(solution)/shard_map/ppermute | solution.py:1046
  23.2 18.0 %collective-permute-done.7.refs_4_ = bf16[288,768]{1,0:T(8,128)(2,1)S(1)} collective-permute-done((bf16[288,768]{1,0:T(8,128)(2,1)}, bf16[288,768]{1,0:T(8,128)(2,1)S(1)}, u32[]{:S(2)}, u32[]{:S(2)}) %collective-permute-start.7) | collective-permute-done | bytes 442400 | tf_op jit(solution)/shard_map/ppermute | solution.py:992
  45.3 7.1 %collective-permute-done.11.refs_7_.refs_15_ = bf16[304,768]{1,0:T(8,128)(2,1)S(1)} collective-permute-done((bf16[304,768]{1,0:T(8,128)(2,1)S(1)}, bf16[304,768]{1,0:T(8,128)(2,1)S(1)}, u32[]{:S(2)}, u32[]{:S(2)}) %collective-permute-start.11) | collective-permute-done | bytes 466976 | tf_op jit(solution)/shard_map/ppermute | solution.py:992
  52.4 14.4 %collective-permute-done.9.refs_2_.refs_10_ = bf16[304,768]{1,0:T(8,128)(2,1)S(1)} collective-permute-done((bf16[304,768]{1,0:T(8,128)(2,1)}, bf16[304,768]{1,0:T(8,128)(2,1)S(1)}, u32[]{:S(2)}, u32[]{:S(2)}) %collective-permute-start.9) | collective-permute-done | bytes 466976 | tf_op jit(solution)/shard_map/ppermute | solution.py:988
  76.4 6.9 %collective-permute-done.13.refs_6_.refs_14_ = bf16[304,768]{1,0:T(8,128)(2,1)S(1)} collective-permute-done((bf16[304,768]{1,0:T(8,128)(2,1)S(1)}, bf16[304,768]{1,0:T(8,128)(2,1)S(1)}, u32[]{:S(2)}, u32[]{:S(2)}) %collective-permute-start.13) | collective-permute-done | bytes 466976 | tf_op jit(solution)/shard_map/ppermute | solution.py:992
  84.1 6.2 %attend_forward.1 = (f32[512,768]{1,0:T(8,128)}, f32[2,8,768]{2,1,0:T(8,128)}) custom-call(s32[3]{0:T(128)} %pad_add_fusion.1.me_ref, bf16[384,768]{1,0:T(8,128)(2,1)} %copy-done.1, bf16[384,768]{1,0:T(8,128)(2,1)} %copy-done.2, bf16[768,768]{1,0:T(8,128)(2,1)} %copy-done, bf16[768,768]{1,0:T(8,128)(2,1)} %copy-done, ...), custom_call_target="tpu_custom_call" | custom-call | tf_op jit(solution)/shard_map/attend_forward/pallas_call | solution.py:1019
  90.3 5.1 %mlp_forward.1 = (f32[128,768]{1,0:T(8,128)}, f32[128,768]{1,0:T(8,128)}, bf16[256,768]{1,0:T(8,128)(2,1)}) custom-call(s32[3]{0:T(128)} %pad_add_fusion.1.me_ref, bf16[384,768]{1,0:T(8,128)(2,1)} %copy-done.1, bf16[384,768]{1,0:T(8,128)(2,1)} %copy-done.2, bf16[768,768]{1,0:T(8,128)(2,1)} %copy-done, bf16[768,768]{1,0:T(8,128)(2,1)} %copy-done, ...), custom_call_target="tpu_custom_call" | custom-call | tf_op jit(solution)/shard_map/mlp_forward/pallas_call | solution.py:1019
  100.9 4.5 %collective-permute-done.15.y2 = bf16[128,768]{1,0:T(8,128)(2,1)S(1)} collective-permute-done((bf16[128,768]{1,0:T(8,128)(2,1)S(1)}, bf16[128,768]{1,0:T(8,128)(2,1)S(1)}, u32[]{:S(2)}, u32[]{:S(2)}) %collective-permute-start.15) | collective-permute-done | bytes 196640 | tf_op jit(solution)/shard_map/ppermute | solution.py:983
  109.6 9.5 %collective-permute-done.22.refs_2_ = bf16[288,768]{1,0:T(8,128)(2,1)S(1)} collective-permute-done((bf16[288,768]{1,0:T(8,128)(2,1)S(1)}, bf16[288,768]{1,0:T(8,128)(2,1)S(1)}, u32[]{:S(2)}, u32[]{:S(2)}) %collective-permute-start.22) | collective-permute-done | bytes 442400 | tf_op jit(solution)/shard_map/ppermute | solution.py:988
  121.9 8.2 %collective-permute-done.23.refs_6_ = bf16[288,768]{1,0:T(8,128)(2,1)S(1)} collective-permute-done((bf16[288,768]{1,0:T(8,128)(2,1)S(1)}, bf16[288,768]{1,0:T(8,128)(2,1)S(1)}, u32[]{:S(2)}, u32[]{:S(2)}) %collective-permute-start.23) | collective-permute-done | bytes 442400 | tf_op jit(solution)/shard_map/ppermute | solution.py:992
  131.6 8.0 %mlp_both.2 = (f32[512,768]{1,0:T(8,128)}, f32[8,768]{1,0:T(8,128)}, f32[512,768]{1,0:T(8,128)}, bf16[2,48,768]{2,1,0:T(8,128)(2,1)}, bf16[2,48,768]{2,1,0:T(8,1...) custom-call(s32[3]{0:T(128)} %pad_add_fusion.1.me_ref, ...), custom_call_target="tpu_custom_call" | custom-call | tf_op jit(solution)/shard_map/mlp_both/pallas_call | solution.py:1019
  143.4 11.7 %attend_both.2 = (bf16[4,112,768]{2,1,0:T(8,128)(2,1)}, bf16[4,112,768]{2,1,0:T(8,128)(2,1)}, f32[128,768]{1,0:T(8,128)}, f32[128,768]{1,0:T(8,128)}, bf16[256,7...) custom-call(s32[3]{0:T(128)} %pad_add_fusion.1.me_ref, ...), custom_call_target="tpu_custom_call" | custom-call | tf_op jit(solution)/shard_map/attend_both/pallas_call | solution.py:1019
  162.0 3.3 %collective-permute-done.29.n2 = bf16[128,768]{1,0:T(8,128)(2,1)S(1)} collective-permute-done((bf16[128,768]{1,0:T(8,128)(2,1)S(1)}, bf16[128,768]{1,0:T(8,128)(2,1)S(1)}, u32[]{:S(2)}, u32[]{:S(2)}) %collective-permute-start.29) | collective-permute-done | bytes 196640 | tf_op jit(solution)/shard_map/ppermute | solution.py:983
  169.8 3.5 %collective-permute-done.30.g1 = bf16[128,768]{1,0:T(8,128)(2,1)S(1)} collective-permute-done((bf16[128,768]{1,0:T(8,128)(2,1)}, bf16[128,768]{1,0:T(8,128)(2,1)S(1)}, u32[]{:S(2)}, u32[]{:S(2)}) %collective-permute-start.30) | collective-permute-done | bytes 196640 | tf_op jit(solution)/shard_map/ppermute | solution.py:983
  174.3 4.9 %collective-permute-start.31 = (bf16[256,768]{1,0:T(8,128)(2,1)S(1)}, bf16[256,768]{1,0:T(8,128)(2,1)S(1)}, u32[]{:S(2)}, u32[]{:S(2)}) collective-permute-start(bf16[256,768]{1,0:T(8,128)(2,1)S(1)} %pad_maximum_fusion.3), channel_id=1, source_target_pairs={{0,2},{1,3},{2,0},{3,1},{4,6},{5,7},{6,4},{7,5},{8,10},{9,11},{10,... | collective-permute-start | bytes 1179656 | tf_op jit(solution)/shard_map/ppermute | solution.py:983
  183.4 7.6 %mlp_both.3 = (f32[512,768]{1,0:T(8,128)}, f32[8,768]{1,0:T(8,128)}, bf16[4,192,768]{2,1,0:T(8,128)(2,1)}, bf16[2,192,768]{2,1,0:T(8,128)(2,1)}, bf16[2,192,768]{2,1,0:T(8,128)(2,1)}) custom-call(s32[3]{0:T(128)} %pad_add_fusion.1.me_ref, bf16[384,768]{1,0:T(8,128)(2,1)} %copy-done.1, bf16[384,768]{1,0:T(8,128)(2,1)} %copy-done.2, bf16[768,768]{1,0:T(8,128)(2,1)} %copy-done, ...), custom_call_target="tpu_custom_call" | custom-call | tf_op jit(solution)/shard_map/mlp_both/pallas_call | solution.py:1019
  195.4 11.3 %attend_both.3 = (bf16[4,112,768]{2,1,0:T(8,128)(2,1)}, bf16[4,112,768]{2,1,0:T(8,128)(2,1)}, f32[128,768]{1,0:T(8,128)}, f32[128,768]{1,0:T(8,128)}, bf16[256,768]{1,0:T(8,128)(2,1)}) custom-call(s32[3]{0:T(128)} %pad_add_fusion.1.me_ref, bf16[384,768]{1,0:T(8,128)(2,1)} %copy-done.1, bf16[384,768]{1,0:T(8,128)(2,1)} %copy-done.2, ...), custom_call_target="tpu_custom_call" | custom-call | tf_op jit(solution)/shard_map/attend_both/pallas_call | solution.py:1019
  206.7 4.7 %collective-permute-done.33.m_received = bf16[2,192,768]{2,1,0:T(8,128)(2,1)S(1)} collective-permute-done((bf16[2,192,768]{2,1,0:T(8,128)(2,1)}, bf16[2,192,768]{2,1,0:T(8,128)(2,1)S(1)}, u32[]{:S(2)}, u32[]{:S(2)}) %collective-permute-start.33) | collective-permute-done | bytes 589856 | tf_op jit(solution)/shard_map/ppermute | solution.py:992
  212.3 3.0 add_first.1
  222.1 3.5 %collective-permute-done.38.y2 = bf16[128,768]{1,0:T(8,128)(2,1)S(1)} collective-permute-done((bf16[128,768]{1,0:T(8,128)(2,1)S(1)}, bf16[128,768]{1,0:T(8,128)(2,1)S(1)}, u32[]{:S(2)}, u32[]{:S(2)}) %collective-permute-start.38) | collective-permute-done | bytes 196640 | tf_op jit(solution)/shard_map/ppermute | solution.py:983
  235.4 11.8 %collective-permute-done.45.refs_11_ = bf16[48,768]{1,0:T(8,128)(2,1)S(1)} collective-permute-done((bf16[48,768]{1,0:T(8,128)(2,1)}, bf16[48,768]{1,0:T(8,128)(2,1)S(1)}, u32[]{:S(2)}, u32[]{:S(2)}) %collective-permute-start.45) | collective-permute-done | bytes 73760 | tf_op jit(solution)/shard_map/ppermute | solution.py:992
  247.2 3.1 add_second.1
  254.9 18.2 %collective-permute-done.46.refs_3_.refs_8_ = bf16[304,768]{1,0:T(8,128)(2,1)S(1)} collective-permute-done((bf16[304,768]{1,0:T(8,128)(2,1)}, bf16[304,768]{1,0:T(8,128)(2,1)S(1)}, u32[]{:S(2)}, u32[]{:S(2)}) %collective-permute-start.46) | collective-permute-done | bytes 466976 | tf_op jit(solution)/shard_map/ppermute | solution.py:988
  273.2 3.4 %collective-permute-start.49 = (bf16[112,768]{1,0:T(8,128)(2,1)}, bf16[112,768]{1,0:T(8,128)(2,1)S(1)}, u32[]{:S(2)}, u32[]{:S(2)}) collective-permute-start(bf16[112,768]{1,0:T(8,128)(2,1)} %get-tuple-element.195), channel_id=1, source_target_pairs={{0,24},{8,0},{16,8},{24,16},{1,25},{9,1},{17,9},{25,17},{2,26},{10... | collective-permute-start | bytes 516104 | tf_op jit(solution)/shard_map/ppermute | solution.py:988
  276.9 3.2 %split_gradients.2 = (bf16[64,768]{1,0:T(8,128)(2,1)}, bf16[64,768]{1,0:T(8,128)(2,1)}, bf16[64,768]{1,0:T(8,128)(2,1)}, bf16[64,768]{1,0:T(8,128)(2,1)}, f32[96...) custom-call(s32[3]{0:T(128)} %pad_add_fusion.1.me_ref, ...), custom_call_target="tpu_custom_call" | custom-call | tf_op jit(solution)/shard_map/split_gradients/pallas_call | solution.py:1019
  281.3 5.6 %collective-permute-start.57 = (bf16[24,768]{1,0:T(8,128)(2,1)}, bf16[24,768]{1,0:T(8,128)(2,1)S(1)}, u32[]{:S(2)}, u32[]{:S(2)}) collective-permute-start(bf16[24,768]{1,0:T(8,128)(2,1)} %get-tuple-element.208), channel_id=1, source_target_pairs={{0,0},{4,1},{8,2},{12,3},{16,4},{20,5},{24,6},{28,7},{1,8},{5,9},{... | collective-permute-start | bytes 110600 | tf_op jit(solution)/shard_map/ppermute | solution.py:1186
  286.9 4.0 %collective-permute-done.48.refs_3_ = bf16[112,768]{1,0:T(8,128)(2,1)S(1)} collective-permute-done((bf16[112,768]{1,0:T(8,128)(2,1)}, bf16[112,768]{1,0:T(8,128)(2,1)S(1)}, u32[]{:S(2)}, u32[]{:S(2)}) %collective-permute-start.48) | collective-permute-done | bytes 172064 | tf_op jit(solution)/shard_map/ppermute | solution.py:988
  294.0 3.2 %split_gradients.3 = (bf16[64,768]{1,0:T(8,128)(2,1)}, bf16[64,768]{1,0:T(8,128)(2,1)}, bf16[64,768]{1,0:T(8,128)(2,1)}, bf16[64,768]{1,0:T(8,128)(2,1)}, f32[96...) custom-call(s32[3]{0:T(128)} %pad_add_fusion.1.me_ref, ...), custom_call_target="tpu_custom_call" | custom-call | tf_op jit(solution)/shard_map/split_gradients/pallas_call | solution.py:1019
  299.1 5.4 %collective-permute-start.53 = (bf16[24,768]{1,0:T(8,128)(2,1)}, bf16[24,768]{1,0:T(8,128)(2,1)S(1)}, u32[]{:S(2)}, u32[]{:S(2)}) collective-permute-start(bf16[24,768]{1,0:T(8,128)(2,1)} %get-tuple-element.202), channel_id=1, source_target_pairs={{0,0},{4,1},{8,2},{12,3},{16,4},{20,5},{24,6},{28,7},{1,8},{5,9},{... | collective-permute-start | bytes 110600 | tf_op jit(solution)/shard_map/ppermute | solution.py:1186
  304.6 2.7 collective-permute-done.53.refs_6_
  308.0 2.9 unpack_gradients.1
  (274 shorter events, 95.2 us)
Async XLA Ops:
  19.6 21.6 %collective-permute-start.6 = (bf16[304,768]{1,0:T(8,128)(2,1)}, bf16[304,768]{1,0:T(8,128)(2,1)S(1)}, u32[]{:S(2)}, u32[]{:S(2)}) collective-permute-start(bf16[304,768]{1,0:T(8,128)(2,1)} %get-tuple-element.124.refs_0_.refs_8_), channel_id=1, source_target_pairs={{0,4},{4,0},{1,5},{5,1},{2,6},{6,2},{3,7},{7,3},{8,12},{12,8},{9,1... | collective-permute-start | bytes 1400840 | tf_op jit(solution)/shard_map/ppermute | solution.py:992
  19.6 21.6 %collective-permute-start.5 = (bf16[304,768]{1,0:T(8,128)(2,1)}, bf16[304,768]{1,0:T(8,128)(2,1)S(1)}, u32[]{:S(2)}, u32[]{:S(2)}) collective-permute-start(bf16[304,768]{1,0:T(8,128)(2,1)} %get-tuple-element.124.refs_0_.refs_8_), channel_id=1, source_target_pairs={{0,24},{8,0},{16,8},{24,16},{1,25},{9,1},{17,9},{25,17},{2,26},{10... | collective-permute-start | bytes 1400840 | tf_op jit(solution)/shard_map/ppermute | solution.py:988
  21.6 20.8 %collective-permute-start.4 = (bf16[304,768]{1,0:T(8,128)(2,1)}, bf16[304,768]{1,0:T(8,128)(2,1)S(1)}, u32[]{:S(2)}, u32[]{:S(2)}) collective-permute-start(bf16[304,768]{1,0:T(8,128)(2,1)} %get-tuple-element.124.refs_0_.refs_8_), channel_id=1, source_target_pairs={{0,8},{8,16},{16,24},{24,0},{1,9},{9,17},{17,25},{25,1},{2,10},{10... | collective-permute-start | bytes 1400840 | tf_op jit(solution)/shard_map/ppermute | solution.py:988
  21.6 19.6 %collective-permute-start.7 = (bf16[288,768]{1,0:T(8,128)(2,1)}, bf16[288,768]{1,0:T(8,128)(2,1)S(1)}, u32[]{:S(2)}, u32[]{:S(2)}) collective-permute-start(bf16[288,768]{1,0:T(8,128)(2,1)} %get-tuple-element.136.refs_0_), channel_id=1, source_target_pairs={{0,4},{4,0},{1,5},{5,1},{2,6},{6,2},{3,7},{7,3},{8,12},{12,8},{9,1... | collective-permute-start | bytes 1327112 | tf_op jit(solution)/shard_map/ppermute | solution.py:992
  42.4 24.4 %collective-permute-start.8 = (bf16[384,768]{1,0:T(8,128)(2,1)S(1)}, bf16[384,768]{1,0:T(8,128)(2,1)S(1)}, u32[]{:S(2)}, u32[]{:S(2)}) collective-permute-start(bf16[384,768]{1,0:T(8,128)(2,1)S(1)} %fusion.1.x0.g0), channel_id=1, source_target_pairs={{0,1},{1,0},{2,3},{3,2},{4,5},{5,4},{6,7},{7,6},{8,9},{9,8},{10,11... | collective-permute-start | bytes 1769480 | tf_op jit(solution)/shard_map/ppermute | solution.py:983
  44.4 22.4 %collective-permute-start.9 = (bf16[304,768]{1,0:T(8,128)(2,1)}, bf16[304,768]{1,0:T(8,128)(2,1)S(1)}, u32[]{:S(2)}, u32[]{:S(2)}) collective-permute-start(bf16[304,768]{1,0:T(8,128)(2,1)} %get-tuple-element.124.refs_0_.refs_8_), channel_id=1, source_target_pairs={{0,16},{8,24},{16,0},{24,8},{1,17},{9,25},{17,1},{25,9},{2,18},{10... | collective-permute-start | bytes 1400840 | tf_op jit(solution)/shard_map/ppermute | solution.py:988
  44.6 22.2 %collective-permute-start.10 = (bf16[304,768]{1,0:T(8,128)(2,1)S(1)}, bf16[304,768]{1,0:T(8,128)(2,1)S(1)}, u32[]{:S(2)}, u32[]{:S(2)}) collective-permute-start(bf16[304,768]{1,0:T(8,128)(2,1)S(1)} %collective-permute-done.4.refs_1_.refs_9_), channel_id=1, source_target_pairs={{0,4},{4,0},{1,5},{5,1},{2,6},{6,2},{3,7},{7,3},{8,12},{12,8},{9,1... | collective-permute-start | bytes 1400840 | tf_op jit(solution)/shard_map/ppermute | solution.py:992
  70.0 26.9 %collective-permute-start.19 = (bf16[288,768]{1,0:T(8,128)(2,1)}, bf16[288,768]{1,0:T(8,128)(2,1)S(1)}, u32[]{:S(2)}, u32[]{:S(2)}) collective-permute-start(bf16[288,768]{1,0:T(8,128)(2,1)} %get-tuple-element.136.refs_0_), channel_id=1, source_target_pairs={{0,24},{8,0},{16,8},{24,16},{1,25},{9,1},{17,9},{25,17},{2,26},{10... | collective-permute-start | bytes 1327112 | tf_op jit(solution)/shard_map/ppermute | solution.py:988
  71.1 25.7 %collective-permute-start.17 = (bf16[288,768]{1,0:T(8,128)(2,1)}, bf16[288,768]{1,0:T(8,128)(2,1)S(1)}, u32[]{:S(2)}, u32[]{:S(2)}) collective-permute-start(bf16[288,768]{1,0:T(8,128)(2,1)} %get-tuple-element.136.refs_0_), channel_id=1, source_target_pairs={{0,8},{8,16},{16,24},{24,0},{1,9},{9,17},{17,25},{25,1},{2,10},{10... | collective-permute-start | bytes 1327112 | tf_op jit(solution)/shard_map/ppermute | solution.py:988
  96.9 22.2 %collective-permute-start.22 = (bf16[288,768]{1,0:T(8,128)(2,1)S(1)}, bf16[288,768]{1,0:T(8,128)(2,1)S(1)}, u32[]{:S(2)}, u32[]{:S(2)}) collective-permute-start(bf16[288,768]{1,0:T(8,128)(2,1)S(1)} %copy-done.20), channel_id=1, source_target_pairs={{0,16},{8,24},{16,0},{24,8},{1,17},{9,25},{17,1},{25,9},{2,18},{10... | collective-permute-start | bytes 1327112 | tf_op jit(solution)/shard_map/ppermute | solution.py:988
  97.0 22.5 %collective-permute-start.20 = (bf16[288,768]{1,0:T(8,128)(2,1)S(1)}, bf16[288,768]{1,0:T(8,128)(2,1)S(1)}, u32[]{:S(2)}, u32[]{:S(2)}) collective-permute-start(bf16[288,768]{1,0:T(8,128)(2,1)S(1)} %collective-permute-done.19.refs_3_), channel_id=1, source_target_pairs={{0,4},{4,0},{1,5},{5,1},{2,6},{6,2},{3,7},{7,3},{8,12},{12,8},{9,1... | collective-permute-start | bytes 1327112 | tf_op jit(solution)/shard_map/ppermute | solution.py:992
  97.6 21.9 %collective-permute-start.18 = (bf16[288,768]{1,0:T(8,128)(2,1)S(1)}, bf16[288,768]{1,0:T(8,128)(2,1)S(1)}, u32[]{:S(2)}, u32[]{:S(2)}) collective-permute-start(bf16[288,768]{1,0:T(8,128)(2,1)S(1)} %collective-permute-done.17.refs_1_), channel_id=1, source_target_pairs={{0,4},{4,0},{1,5},{5,1},{2,6},{6,2},{3,7},{7,3},{8,12},{12,8},{9,1... | collective-permute-start | bytes 1327112 | tf_op jit(solution)/shard_map/ppermute | solution.py:992
  139.6 19.7 %collective-permute-start.28 = (bf16[4,144,768]{2,1,0:T(8,128)(2,1)}, bf16[4,144,768]{2,1,0:T(8,128)(2,1)S(1)}, u32[]{:S(2)}, u32[]{:S(2)}) collective-permute-start(bf16[4,144,768]{2,1,0:T(8,128)(2,1)} %get-tuple-element.148), channel_id=1, source_target_pairs={{0,4},{4,0},{1,5},{5,1},{2,6},{6,2},{3,7},{7,3},{8,12},{12,8},{9,1... | collective-permute-start | bytes 2654216 | tf_op jit(solution)/shard_map/ppermute | solution.py:992
  139.9 15.2 %collective-permute-start.24 = (bf16[2,48,768]{2,1,0:T(8,128)(2,1)}, bf16[2,48,768]{2,1,0:T(8,128)(2,1)S(1)}, u32[]{:S(2)}, u32[]{:S(2)}) collective-permute-start(bf16[2,48,768]{2,1,0:T(8,128)(2,1)} %get-tuple-element.144), channel_id=1, source_target_pairs={{0,8},{8,16},{16,24},{24,0},{1,9},{9,17},{17,25},{25,1},{2,10},{10... | collective-permute-start | bytes 442376 | tf_op jit(solution)/shard_map/ppermute | solution.py:988
  140.8 14.3 %collective-permute-start.25 = (bf16[2,48,768]{2,1,0:T(8,128)(2,1)}, bf16[2,48,768]{2,1,0:T(8,128)(2,1)S(1)}, u32[]{:S(2)}, u32[]{:S(2)}) collective-permute-start(bf16[2,48,768]{2,1,0:T(8,128)(2,1)} %get-tuple-element.145), channel_id=1, source_target_pairs={{0,16},{8,24},{16,0},{24,8},{1,17},{9,25},{17,1},{25,9},{2,18},{10... | collective-permute-start | bytes 442376 | tf_op jit(solution)/shard_map/ppermute | solution.py:988
  142.2 12.9 %collective-permute-start.26 = (bf16[2,48,768]{2,1,0:T(8,128)(2,1)}, bf16[2,48,768]{2,1,0:T(8,128)(2,1)S(1)}, u32[]{:S(2)}, u32[]{:S(2)}) collective-permute-start(bf16[2,48,768]{2,1,0:T(8,128)(2,1)} %get-tuple-element.146), channel_id=1, source_target_pairs={{0,24},{8,0},{16,8},{24,16},{1,25},{9,1},{17,9},{25,17},{2,26},{10... | collective-permute-start | bytes 442376 | tf_op jit(solution)/shard_map/ppermute | solution.py:988
  182.0 24.6 %collective-permute-start.34 = (bf16[4,112,768]{2,1,0:T(8,128)(2,1)S(1)}, bf16[4,112,768]{2,1,0:T(8,128)(2,1)S(1)}, u32[]{:S(2)}, u32[]{:S(2)}) collective-permute-start(bf16[4,112,768]{2,1,0:T(8,128)(2,1)S(1)} %copy-done.65), channel_id=1, source_target_pairs={{0,4},{4,0},{1,5},{5,1},{2,6},{6,2},{3,7},{7,3},{8,12},{12,8},{9,1... | collective-permute-start | bytes 2064392 | tf_op jit(solution)/shard_map/ppermute | solution.py:992
  191.1 20.3 %collective-permute-start.33 = (bf16[2,192,768]{2,1,0:T(8,128)(2,1)}, bf16[2,192,768]{2,1,0:T(8,128)(2,1)S(1)}, u32[]{:S(2)}, u32[]{:S(2)}) collective-permute-start(bf16[2,192,768]{2,1,0:T(8,128)(2,1)} %get-tuple-element.160), channel_id=1, source_target_pairs={{0,4},{4,0},{1,5},{5,1},{2,6},{6,2},{3,7},{7,3},{8,12},{12,8},{9,1... | collective-permute-start | bytes 1769480 | tf_op jit(solution)/shard_map/ppermute | solution.py:992
  192.0 14.6 %collective-permute-start.35 = (bf16[144,768]{1,0:T(8,128)(2,1)S(1)}, bf16[144,768]{1,0:T(8,128)(2,1)S(1)}, u32[]{:S(2)}, u32[]{:S(2)}) collective-permute-start(bf16[144,768]{1,0:T(8,128)(2,1)S(1)} %copy-done.70), channel_id=1, source_target_pairs={{0,16},{8,24},{16,0},{24,8},{1,17},{9,25},{17,1},{25,9},{2,18},{10... | collective-permute-start | bytes 663560 | tf_op jit(solution)/shard_map/ppermute | solution.py:988
  193.4 13.2 %collective-permute-start.36 = (bf16[144,768]{1,0:T(8,128)(2,1)S(1)}, bf16[144,768]{1,0:T(8,128)(2,1)S(1)}, u32[]{:S(2)}, u32[]{:S(2)}) collective-permute-start(bf16[144,768]{1,0:T(8,128)(2,1)S(1)} %copy-done.69), channel_id=1, source_target_pairs={{0,24},{8,0},{16,8},{24,16},{1,25},{9,1},{17,9},{25,17},{2,26},{10... | collective-permute-start | bytes 663560 | tf_op jit(solution)/shard_map/ppermute | solution.py:988
  216.5 18.8 %collective-permute-start.43 = (bf16[2,192,768]{2,1,0:T(8,128)(2,1)S(1)}, bf16[2,192,768]{2,1,0:T(8,128)(2,1)S(1)}, u32[]{:S(2)}, u32[]{:S(2)}) collective-permute-start(bf16[2,192,768]{2,1,0:T(8,128)(2,1)S(1)} %copy-done.66), channel_id=1, source_target_pairs={{0,4},{4,0},{1,5},{5,1},{2,6},{6,2},{3,7},{7,3},{8,12},{12,8},{9,1... | collective-permute-start | bytes 1769480 | tf_op jit(solution)/shard_map/ppermute | solution.py:992
  217.1 30.1 %collective-permute-start.42 = (bf16[304,768]{1,0:T(8,128)(2,1)}, bf16[304,768]{1,0:T(8,128)(2,1)S(1)}, u32[]{:S(2)}, u32[]{:S(2)}) collective-permute-start(bf16[304,768]{1,0:T(8,128)(2,1)} %get-tuple-element.168), channel_id=1, source_target_pairs={{0,8},{8,16},{16,24},{24,0},{1,9},{9,17},{17,25},{25,1},{2,10},{10... | collective-permute-start | bytes 1400840 | tf_op jit(solution)/shard_map/ppermute | solution.py:988
  218.7 28.5 %collective-permute-start.44 = (bf16[304,768]{1,0:T(8,128)(2,1)}, bf16[304,768]{1,0:T(8,128)(2,1)S(1)}, u32[]{:S(2)}, u32[]{:S(2)}) collective-permute-start(bf16[304,768]{1,0:T(8,128)(2,1)} %get-tuple-element.181), channel_id=1, source_target_pairs={{0,24},{8,0},{16,8},{24,16},{1,25},{9,1},{17,9},{25,17},{2,26},{10... | collective-permute-start | bytes 1400840 | tf_op jit(solution)/shard_map/ppermute | solution.py:988
  225.7 26.3 %collective-permute-start.41 = (bf16[4,112,768]{2,1,0:T(8,128)(2,1)S(1)}, bf16[4,112,768]{2,1,0:T(8,128)(2,1)S(1)}, u32[]{:S(2)}, u32[]{:S(2)}) collective-permute-start(bf16[4,112,768]{2,1,0:T(8,128)(2,1)S(1)} %copy-done.64), channel_id=1, source_target_pairs={{0,4},{4,0},{1,5},{5,1},{2,6},{6,2},{3,7},{7,3},{8,12},{12,8},{9,1... | collective-permute-start | bytes 2064392 | tf_op jit(solution)/shard_map/ppermute | solution.py:992
  229.9 17.3 %collective-permute-start.45 = (bf16[48,768]{1,0:T(8,128)(2,1)}, bf16[48,768]{1,0:T(8,128)(2,1)S(1)}, u32[]{:S(2)}, u32[]{:S(2)}) collective-permute-start(bf16[48,768]{1,0:T(8,128)(2,1)} %get-tuple-element.184), channel_id=1, source_target_pairs={{0,4},{4,0},{1,5},{5,1},{2,6},{6,2},{3,7},{7,3},{8,12},{12,8},{9,1... | collective-permute-start | bytes 221192 | tf_op jit(solution)/shard_map/ppermute | solution.py:992
  250.3 22.9 %collective-permute-start.46 = (bf16[304,768]{1,0:T(8,128)(2,1)}, bf16[304,768]{1,0:T(8,128)(2,1)S(1)}, u32[]{:S(2)}, u32[]{:S(2)}) collective-permute-start(bf16[304,768]{1,0:T(8,128)(2,1)} %add_second.1), channel_id=1, source_target_pairs={{0,16},{8,24},{16,0},{24,8},{1,17},{9,25},{17,1},{25,9},{2,18},{10... | collective-permute-start | bytes 1400840 | tf_op jit(solution)/shard_map/ppermute | solution.py:988
  273.2 13.6 %collective-permute-start.49 = (bf16[112,768]{1,0:T(8,128)(2,1)}, bf16[112,768]{1,0:T(8,128)(2,1)S(1)}, u32[]{:S(2)}, u32[]{:S(2)}) collective-permute-start(bf16[112,768]{1,0:T(8,128)(2,1)} %get-tuple-element.195), channel_id=1, source_target_pairs={{0,24},{8,0},{16,8},{24,16},{1,25},{9,1},{17,9},{25,17},{2,26},{10... | collective-permute-start | bytes 516104 | tf_op jit(solution)/shard_map/ppermute | solution.py:988
  276.6 14.3 %collective-permute-start.48 = (bf16[112,768]{1,0:T(8,128)(2,1)}, bf16[112,768]{1,0:T(8,128)(2,1)S(1)}, u32[]{:S(2)}, u32[]{:S(2)}) collective-permute-start(bf16[112,768]{1,0:T(8,128)(2,1)} %get-tuple-element.193), channel_id=1, source_target_pairs={{0,16},{8,24},{16,0},{24,8},{1,17},{9,25},{17,1},{25,9},{2,18},{10... | collective-permute-start | bytes 516104 | tf_op jit(solution)/shard_map/ppermute | solution.py:988
  276.6 16.7 %collective-permute-start.47 = (bf16[112,768]{1,0:T(8,128)(2,1)}, bf16[112,768]{1,0:T(8,128)(2,1)S(1)}, u32[]{:S(2)}, u32[]{:S(2)}) collective-permute-start(bf16[112,768]{1,0:T(8,128)(2,1)} %get-tuple-element.191), channel_id=1, source_target_pairs={{0,8},{8,16},{16,24},{24,0},{1,9},{9,17},{17,25},{25,1},{2,10},{10... | collective-permute-start | bytes 516104 | tf_op jit(solution)/shard_map/ppermute | solution.py:988
  280.0 18.2 %collective-permute-start.54 = (bf16[64,768]{1,0:T(8,128)(2,1)}, bf16[64,768]{1,0:T(8,128)(2,1)S(1)}, u32[]{:S(2)}, u32[]{:S(2)}) collective-permute-start(bf16[64,768]{1,0:T(8,128)(2,1)} %get-tuple-element.203), channel_id=1, source_target_pairs={{0,1},{1,0},{2,3},{3,2},{4,5},{5,4},{6,7},{7,6},{8,9},{9,8},{10,11... | collective-permute-start | bytes 294920 | tf_op jit(solution)/shard_map/ppermute | solution.py:983
  281.3 16.4 %collective-permute-start.57 = (bf16[24,768]{1,0:T(8,128)(2,1)}, bf16[24,768]{1,0:T(8,128)(2,1)S(1)}, u32[]{:S(2)}, u32[]{:S(2)}) collective-permute-start(bf16[24,768]{1,0:T(8,128)(2,1)} %get-tuple-element.208), channel_id=1, source_target_pairs={{0,0},{4,1},{8,2},{12,3},{16,4},{20,5},{24,6},{28,7},{1,8},{5,9},{... | collective-permute-start | bytes 110600 | tf_op jit(solution)/shard_map/ppermute | solution.py:1186
  290.9 13.7 %collective-permute-start.56 = (bf16[64,768]{1,0:T(8,128)(2,1)}, bf16[64,768]{1,0:T(8,128)(2,1)S(1)}, u32[]{:S(2)}, u32[]{:S(2)}) collective-permute-start(bf16[64,768]{1,0:T(8,128)(2,1)} %get-tuple-element.205), channel_id=1, source_target_pairs={{0,3},{1,2},{2,1},{3,0},{4,7},{5,6},{6,5},{7,4},{8,11},{9,10},{10,... | collective-permute-start | bytes 294920 | tf_op jit(solution)/shard_map/ppermute | solution.py:983
  (98 other events, 956.1 us)

commit v4 on v3

--- a/solution.py
+++ b/solution.py
@@ -946,7 +946,7 @@
     me = me_ref[0]
     (
         qkv_ref, qkv_b_ref, attn_ref, attn_b_ref, up_ref, up_b_ref, down_ref,
-        ga_ref, sa_ref, gm_ref, sm_ref,
+        down_b_ref, ga_ref, sa_ref, gm_ref, sm_ref,
     ) = refs[7 * LAYERS :]
     gain_refs = (ga_ref, sa_ref, gm_ref, sm_ref)
     for depth in range(LAYERS):
@@ -975,6 +975,7 @@
             ref[depth : depth + 1] = small[n : n + 1, :24]
         qkv_b_ref[depth : depth + 1] = small[4:5, :72]
         attn_b_ref[depth : depth + 1] = own_small[0:1, :24]
+        down_b_ref[depth : depth + 1] = own_small[0:1, :24]
         up_b_ref[depth : depth + 1] = own_small[1:2, :96]
 
 
@@ -1228,11 +1229,11 @@
         line_sum_body,
         [shape((EARLY, D), F32), shape((EARLY, D), BF)],
         "line_sum",
-        (e0, after(early[0], first_added), early[1], early[2]),
+        (e0, after(early[0], grad), early[1], early[2]),
     )
     e_other = line_flip(e_send)
     (both2,) = add_both(
-        after(m_second0, both1, both3, grad, activations, e_other), HALVES[1][:1], (0,), "add_second"
+        after(m_second0, both1, both3, grad, activations), HALVES[1][:1], (0,), "add_second"
     )
     a_added0 = add(
         block_a, a_keep0, after(a_other0, both2), (1, 2, 3), (1, 2, 3), "add_attend"
@@ -1253,12 +1254,12 @@
             shape((LAYERS, 24, 3 * D), F32), shape((LAYERS, 72), F32),
             shape((LAYERS, 24, D), F32), row_24,
             shape((LAYERS, 24, FF), F32), shape((LAYERS, 96), F32),
-            shape((LAYERS, 96, D), F32), row_24, row_24, row_24, row_24,
+            shape((LAYERS, 96, D), F32), row_24, row_24, row_24, row_24, row_24,
         ],
         "unpack_gradients",
         [array for group in outs for array in group],
     )
-    return (activations, grad, *final[:7], final[3], *final[7:])
+    return (activations, grad, *final)
 
 
 def whole_mesh_solution(mesh):

time: 316 us -> 310 us (0.981)
  waiting for transfers between devices: 130 us -> 126 us
    ppermute x14, waiting for transfers between devices: 56.9 us -> 48.3 us  [line_flip(): return lax.ppermute(piece, 'y', [(0, 1), (1, 0)])]
    unnamed x145 -> x144, local copies, waits for them, and re-layouts: 9.59 us -> 9.65 us
  transfers between devices with their start and end apart: 58 -> 58, of which waited for: 20 -> 21; matrix products, arithmetic and copies ran while one was open for 2% -> 2% of each run, Pallas kernels for 21% -> 21%
where the time goes in v4:
time: 310 us; the launch traced here: 307 us
  waiting for transfers between devices  126 us (41%)
  Pallas kernels  85.7 us (28%)
  starting transfers between devices  73 us (24%)
  other arithmetic  10.3 us (3%)
  local copies, waits for them, and re-layouts  9.66 us (3%)
    pallas_call x20, Pallas kernels, run(): pl.pallas_call(body, grid=(1,), out_shape=out_shape, in_specs=[pl.BlockSp...  85.7 us
    ppermute x18, waiting for transfers between devices, line_shift(): lax.ppermute(piece, 'z', [(i, (i + shift) % size) for i in range(size)])  50 us
    ppermute x14, waiting for transfers between devices, line_flip(): return lax.ppermute(piece, 'y', [(0, 1), (1, 0)])  48.3 us
    ppermute x23, starting transfers between devices, team_send(): return lax.ppermute(piece, TEAM_AXES, flips)  27.5 us
    ppermute x23, waiting for transfers between devices, team_send(): return lax.ppermute(piece, TEAM_AXES, flips)  19 us
    ppermute x18, starting transfers between devices, line_shift(): lax.ppermute(piece, 'z', [(i, (i + shift) % size) for i in range(size)])  17.5 us
    ppermute x2, starting transfers between devices, split(): attn_rows = lax.ppermute(mine[TEAM + 1], everywhere, gather_back)  11.7 us
    ppermute x14, starting transfers between devices, line_flip(): return lax.ppermute(piece, 'y', [(0, 1), (1, 0)])  10.8 us
  transfers between devices with their start and end apart: 58, of which 21 were waited for; matrix products, arithmetic and copies ran while one was open for 2% of the time, Pallas kernels for 21%

profile of v4, /device:TPU:5, one launch (start us, length us, event | category | flops | bytes accessed | tf_op | source)
XLA Modules:
  0.0 306.8 jit_solution(17289486331644578327)
XLA Ops:
  5.9 5.6 %collective-permute-start.3 = (bf16[2,24,768]{2,1,0:T(8,128)(2,1)}, bf16[2,24,768]{2,1,0:T(8,128)(2,1)S(1)}, u32[]{:S(2)}, u32[]{:S(2)}) collective-permute-start(bf16[2,24,768]{2,1,0:T(8,128)(2,1)} %param.20), channel_id=1, source_target_pairs={{0,0},{1,4},{2,8},{3,12},{4,16},{5,20},{6,24},{7,28},{8,1},{9,5},{... | collective-permute-start | bytes 221192 | tf_op jit(solution)/shard_map/ppermute | solution.py:1047
  11.4 4.9 %collective-permute-done.3.attn_ref = bf16[2,24,768]{2,1,0:T(8,128)(2,1)S(1)} collective-permute-done((bf16[2,24,768]{2,1,0:T(8,128)(2,1)}, bf16[2,24,768]{2,1,0:T(8,128)(2,1)S(1)}, u32[]{:S(2)}, u32[]{:S(2)}) %collective-permute-start.3) | collective-permute-done | bytes 73760 | tf_op jit(solution)/shard_map/ppermute | solution.py:1047
  23.2 18.0 %collective-permute-done.7.refs_4_ = bf16[288,768]{1,0:T(8,128)(2,1)S(1)} collective-permute-done((bf16[288,768]{1,0:T(8,128)(2,1)}, bf16[288,768]{1,0:T(8,128)(2,1)S(1)}, u32[]{:S(2)}, u32[]{:S(2)}) %collective-permute-start.7) | collective-permute-done | bytes 442400 | tf_op jit(solution)/shard_map/ppermute | solution.py:993
  45.3 7.1 %collective-permute-done.11.refs_7_.refs_15_ = bf16[304,768]{1,0:T(8,128)(2,1)S(1)} collective-permute-done((bf16[304,768]{1,0:T(8,128)(2,1)S(1)}, bf16[304,768]{1,0:T(8,128)(2,1)S(1)}, u32[]{:S(2)}, u32[]{:S(2)}) %collective-permute-start.11) | collective-permute-done | bytes 466976 | tf_op jit(solution)/shard_map/ppermute | solution.py:993
  52.4 14.4 %collective-permute-done.9.refs_2_.refs_10_ = bf16[304,768]{1,0:T(8,128)(2,1)S(1)} collective-permute-done((bf16[304,768]{1,0:T(8,128)(2,1)}, bf16[304,768]{1,0:T(8,128)(2,1)S(1)}, u32[]{:S(2)}, u32[]{:S(2)}) %collective-permute-start.9) | collective-permute-done | bytes 466976 | tf_op jit(solution)/shard_map/ppermute | solution.py:989
  76.4 6.9 %collective-permute-done.13.refs_6_.refs_14_ = bf16[304,768]{1,0:T(8,128)(2,1)S(1)} collective-permute-done((bf16[304,768]{1,0:T(8,128)(2,1)S(1)}, bf16[304,768]{1,0:T(8,128)(2,1)S(1)}, u32[]{:S(2)}, u32[]{:S(2)}) %collective-permute-start.13) | collective-permute-done | bytes 466976 | tf_op jit(solution)/shard_map/ppermute | solution.py:993
  84.1 6.2 %attend_forward.1 = (f32[512,768]{1,0:T(8,128)}, f32[2,8,768]{2,1,0:T(8,128)}) custom-call(s32[3]{0:T(128)} %pad_add_fusion.1.me_ref, bf16[384,768]{1,0:T(8,128)(2,1)} %copy-done.1, bf16[384,768]{1,0:T(8,128)(2,1)} %copy-done.2, bf16[768,768]{1,0:T(8,128)(2,1)} %copy-done, bf16[768,768]{1,0:T(8,128)(2,1)} %copy-done, ...), custom_call_target="tpu_custom_call" | custom-call | tf_op jit(solution)/shard_map/attend_forward/pallas_call | solution.py:1020
  90.3 5.1 %mlp_forward.1 = (f32[128,768]{1,0:T(8,128)}, f32[128,768]{1,0:T(8,128)}, bf16[256,768]{1,0:T(8,128)(2,1)}) custom-call(s32[3]{0:T(128)} %pad_add_fusion.1.me_ref, bf16[384,768]{1,0:T(8,128)(2,1)} %copy-done.1, bf16[384,768]{1,0:T(8,128)(2,1)} %copy-done.2, bf16[768,768]{1,0:T(8,128)(2,1)} %copy-done, bf16[768,768]{1,0:T(8,128)(2,1)} %copy-done, ...), custom_call_target="tpu_custom_call" | custom-call | tf_op jit(solution)/shard_map/mlp_forward/pallas_call | solution.py:1020
  100.9 4.5 %collective-permute-done.15.y2 = bf16[128,768]{1,0:T(8,128)(2,1)S(1)} collective-permute-done((bf16[128,768]{1,0:T(8,128)(2,1)S(1)}, bf16[128,768]{1,0:T(8,128)(2,1)S(1)}, u32[]{:S(2)}, u32[]{:S(2)}) %collective-permute-start.15) | collective-permute-done | bytes 196640 | tf_op jit(solution)/shard_map/ppermute | solution.py:984
  109.6 9.5 %collective-permute-done.22.refs_2_ = bf16[288,768]{1,0:T(8,128)(2,1)S(1)} collective-permute-done((bf16[288,768]{1,0:T(8,128)(2,1)S(1)}, bf16[288,768]{1,0:T(8,128)(2,1)S(1)}, u32[]{:S(2)}, u32[]{:S(2)}) %collective-permute-start.22) | collective-permute-done | bytes 442400 | tf_op jit(solution)/shard_map/ppermute | solution.py:989
  121.9 8.2 %collective-permute-done.23.refs_6_ = bf16[288,768]{1,0:T(8,128)(2,1)S(1)} collective-permute-done((bf16[288,768]{1,0:T(8,128)(2,1)S(1)}, bf16[288,768]{1,0:T(8,128)(2,1)S(1)}, u32[]{:S(2)}, u32[]{:S(2)}) %collective-permute-start.23) | collective-permute-done | bytes 442400 | tf_op jit(solution)/shard_map/ppermute | solution.py:993
  131.6 8.0 %mlp_both.2 = (f32[512,768]{1,0:T(8,128)}, f32[8,768]{1,0:T(8,128)}, f32[512,768]{1,0:T(8,128)}, bf16[2,48,768]{2,1,0:T(8,128)(2,1)}, bf16[2,48,768]{2,1,0:T(8,1...) custom-call(s32[3]{0:T(128)} %pad_add_fusion.1.me_ref, ...), custom_call_target="tpu_custom_call" | custom-call | tf_op jit(solution)/shard_map/mlp_both/pallas_call | solution.py:1020
  143.4 11.7 %attend_both.2 = (bf16[4,112,768]{2,1,0:T(8,128)(2,1)}, bf16[4,112,768]{2,1,0:T(8,128)(2,1)}, f32[128,768]{1,0:T(8,128)}, f32[128,768]{1,0:T(8,128)}, bf16[256,7...) custom-call(s32[3]{0:T(128)} %pad_add_fusion.1.me_ref, ...), custom_call_target="tpu_custom_call" | custom-call | tf_op jit(solution)/shard_map/attend_both/pallas_call | solution.py:1020
  155.2 2.6 collective-permute-start.27
  162.0 3.3 %collective-permute-done.29.n2 = bf16[128,768]{1,0:T(8,128)(2,1)S(1)} collective-permute-done((bf16[128,768]{1,0:T(8,128)(2,1)S(1)}, bf16[128,768]{1,0:T(8,128)(2,1)S(1)}, u32[]{:S(2)}, u32[]{:S(2)}) %collective-permute-start.29) | collective-permute-done | bytes 196640 | tf_op jit(solution)/shard_map/ppermute | solution.py:984
  165.9 2.6 norm_backward.2
  169.8 3.5 %collective-permute-done.30.g1 = bf16[128,768]{1,0:T(8,128)(2,1)S(1)} collective-permute-done((bf16[128,768]{1,0:T(8,128)(2,1)}, bf16[128,768]{1,0:T(8,128)(2,1)S(1)}, u32[]{:S(2)}, u32[]{:S(2)}) %collective-permute-start.30) | collective-permute-done | bytes 196640 | tf_op jit(solution)/shard_map/ppermute | solution.py:984
  174.3 4.9 %collective-permute-start.31 = (bf16[256,768]{1,0:T(8,128)(2,1)S(1)}, bf16[256,768]{1,0:T(8,128)(2,1)S(1)}, u32[]{:S(2)}, u32[]{:S(2)}) collective-permute-start(bf16[256,768]{1,0:T(8,128)(2,1)S(1)} %pad_maximum_fusion.3), channel_id=1, source_target_pairs={{0,2},{1,3},{2,0},{3,1},{4,6},{5,7},{6,4},{7,5},{8,10},{9,11},{10,... | collective-permute-start | bytes 1179656 | tf_op jit(solution)/shard_map/ppermute | solution.py:984
  183.4 7.6 %mlp_both.3 = (f32[512,768]{1,0:T(8,128)}, f32[8,768]{1,0:T(8,128)}, bf16[4,192,768]{2,1,0:T(8,128)(2,1)}, bf16[2,192,768]{2,1,0:T(8,128)(2,1)}, bf16[2,192,768]{2,1,0:T(8,128)(2,1)}) custom-call(s32[3]{0:T(128)} %pad_add_fusion.1.me_ref, bf16[384,768]{1,0:T(8,128)(2,1)} %copy-done.1, bf16[384,768]{1,0:T(8,128)(2,1)} %copy-done.2, bf16[768,768]{1,0:T(8,128)(2,1)} %copy-done, ...), custom_call_target="tpu_custom_call" | custom-call | tf_op jit(solution)/shard_map/mlp_both/pallas_call | solution.py:1020
  195.4 11.3 %attend_both.3 = (bf16[4,112,768]{2,1,0:T(8,128)(2,1)}, bf16[4,112,768]{2,1,0:T(8,128)(2,1)}, f32[128,768]{1,0:T(8,128)}, f32[128,768]{1,0:T(8,128)}, bf16[256,768]{1,0:T(8,128)(2,1)}) custom-call(s32[3]{0:T(128)} %pad_add_fusion.1.me_ref, bf16[384,768]{1,0:T(8,128)(2,1)} %copy-done.1, bf16[384,768]{1,0:T(8,128)(2,1)} %copy-done.2, ...), custom_call_target="tpu_custom_call" | custom-call | tf_op jit(solution)/shard_map/attend_both/pallas_call | solution.py:1020
  206.7 4.7 %collective-permute-done.33.m_received = bf16[2,192,768]{2,1,0:T(8,128)(2,1)S(1)} collective-permute-done((bf16[2,192,768]{2,1,0:T(8,128)(2,1)}, bf16[2,192,768]{2,1,0:T(8,128)(2,1)S(1)}, u32[]{:S(2)}, u32[]{:S(2)}) %collective-permute-start.33) | collective-permute-done | bytes 589856 | tf_op jit(solution)/shard_map/ppermute | solution.py:993
  212.3 3.0 add_first.1
  222.4 3.8 %collective-permute-done.38.y2 = bf16[128,768]{1,0:T(8,128)(2,1)S(1)} collective-permute-done((bf16[128,768]{1,0:T(8,128)(2,1)S(1)}, bf16[128,768]{1,0:T(8,128)(2,1)S(1)}, u32[]{:S(2)}, u32[]{:S(2)}) %collective-permute-start.38) | collective-permute-done | bytes 196640 | tf_op jit(solution)/shard_map/ppermute | solution.py:984
  234.2 6.8 %collective-permute-done.44.refs_4_.refs_9_ = bf16[304,768]{1,0:T(8,128)(2,1)S(1)} collective-permute-done((bf16[304,768]{1,0:T(8,128)(2,1)}, bf16[304,768]{1,0:T(8,128)(2,1)S(1)}, u32[]{:S(2)}, u32[]{:S(2)}) %collective-permute-start.44) | collective-permute-done | bytes 466976 | tf_op jit(solution)/shard_map/ppermute | solution.py:989
  241.0 3.1 %add_second.1 = bf16[304,768]{1,0:T(8,128)(2,1)} custom-call(s32[3]{0:T(128)} %pad_add_fusion.1.me_ref, bf16[4,192,768]{2,1,0:T(8,128)(2,1)} %get-tuple-element.159.m_keep.refs_5_, bf16[2,192,768]{2,1,0:T(8,128)(2,1)} %copy-done.15, bf16[4,112,768]{2,1,0:T(8,128)(2,1)} %get-tuple-element.168.a_keep.refs_0_, bf16[4,112,768]{2,1,0:T(8,128)(2,1)} %copy-done.12), custom_call_target="tpu_custom_call" | custom-call | tf_op jit(solution)/shard_map/add_second/pallas_call | solution.py:1020
  248.7 18.1 %collective-permute-done.45.refs_3_.refs_8_ = bf16[304,768]{1,0:T(8,128)(2,1)S(1)} collective-permute-done((bf16[304,768]{1,0:T(8,128)(2,1)}, bf16[304,768]{1,0:T(8,128)(2,1)S(1)}, u32[]{:S(2)}, u32[]{:S(2)}) %collective-permute-start.45) | collective-permute-done | bytes 466976 | tf_op jit(solution)/shard_map/ppermute | solution.py:989
  275.5 3.2 %split_gradients.2 = (bf16[64,768]{1,0:T(8,128)(2,1)}, bf16[64,768]{1,0:T(8,128)(2,1)}, bf16[64,768]{1,0:T(8,128)(2,1)}, bf16[64,768]{1,0:T(8,128)(2,1)}, f32[96...) custom-call(s32[3]{0:T(128)} %pad_add_fusion.1.me_ref, ...), custom_call_target="tpu_custom_call" | custom-call | tf_op jit(solution)/shard_map/split_gradients/pallas_call | solution.py:1020
  280.1 7.5 %collective-permute-start.57 = (bf16[24,768]{1,0:T(8,128)(2,1)}, bf16[24,768]{1,0:T(8,128)(2,1)S(1)}, u32[]{:S(2)}, u32[]{:S(2)}) collective-permute-start(bf16[24,768]{1,0:T(8,128)(2,1)} %get-tuple-element.209), channel_id=1, source_target_pairs={{0,0},{4,1},{8,2},{12,3},{16,4},{20,5},{24,6},{28,7},{1,8},{5,9},{... | collective-permute-start | bytes 110600 | tf_op jit(solution)/shard_map/ppermute | solution.py:1187
  289.2 3.2 %split_gradients.3 = (bf16[64,768]{1,0:T(8,128)(2,1)}, bf16[64,768]{1,0:T(8,128)(2,1)}, bf16[64,768]{1,0:T(8,128)(2,1)}, bf16[64,768]{1,0:T(8,128)(2,1)}, f32[96...) custom-call(s32[3]{0:T(128)} %pad_add_fusion.1.me_ref, ...), custom_call_target="tpu_custom_call" | custom-call | tf_op jit(solution)/shard_map/split_gradients/pallas_call | solution.py:1020
  294.5 4.2 %collective-permute-start.53 = (bf16[24,768]{1,0:T(8,128)(2,1)}, bf16[24,768]{1,0:T(8,128)(2,1)S(1)}, u32[]{:S(2)}, u32[]{:S(2)}) collective-permute-start(bf16[24,768]{1,0:T(8,128)(2,1)} %get-tuple-element.203), channel_id=1, source_target_pairs={{0,0},{4,1},{8,2},{12,3},{16,4},{20,5},{24,6},{28,7},{1,8},{5,9},{... | collective-permute-start | bytes 110600 | tf_op jit(solution)/shard_map/ppermute | solution.py:1187
  298.7 4.0 %collective-permute-done.53.refs_6_ = bf16[24,768]{1,0:T(8,128)(2,1)S(1)} collective-permute-done((bf16[24,768]{1,0:T(8,128)(2,1)}, bf16[24,768]{1,0:T(8,128)(2,1)S(1)}, u32[]{:S(2)}, u32[]{:S(2)}) %collective-permute-start.53) | collective-permute-done | bytes 36896 | tf_op jit(solution)/shard_map/ppermute | solution.py:1187
  303.5 2.9 unpack_gradients.1
  (273 shorter events, 94.6 us)
Async XLA Ops:
  3.5 12.8 %collective-permute-start = (bf16[112,768]{1,0:T(8,128)(2,1)}, bf16[112,768]{1,0:T(8,128)(2,1)S(1)}, u32[]{:S(2)}, u32[]{:S(2)}) collective-permute-start(bf16[112,768]{1,0:T(8,128)(2,1)} %get-tuple-element.119), channel_id=1, source_target_pairs={{0,1},{1,0},{2,3},{3,2},{4,5},{5,4},{6,7},{7,6},{8,9},{9,8},{10,11... | collective-permute-start | bytes 516104 | tf_op jit(solution)/shard_map/ppermute | solution.py:984
  19.6 21.6 %collective-permute-start.6 = (bf16[304,768]{1,0:T(8,128)(2,1)}, bf16[304,768]{1,0:T(8,128)(2,1)S(1)}, u32[]{:S(2)}, u32[]{:S(2)}) collective-permute-start(bf16[304,768]{1,0:T(8,128)(2,1)} %get-tuple-element.125.refs_0_.refs_8_), channel_id=1, source_target_pairs={{0,4},{4,0},{1,5},{5,1},{2,6},{6,2},{3,7},{7,3},{8,12},{12,8},{9,1... | collective-permute-start | bytes 1400840 | tf_op jit(solution)/shard_map/ppermute | solution.py:993
  19.6 21.6 %collective-permute-start.5 = (bf16[304,768]{1,0:T(8,128)(2,1)}, bf16[304,768]{1,0:T(8,128)(2,1)S(1)}, u32[]{:S(2)}, u32[]{:S(2)}) collective-permute-start(bf16[304,768]{1,0:T(8,128)(2,1)} %get-tuple-element.125.refs_0_.refs_8_), channel_id=1, source_target_pairs={{0,24},{8,0},{16,8},{24,16},{1,25},{9,1},{17,9},{25,17},{2,26},{10... | collective-permute-start | bytes 1400840 | tf_op jit(solution)/shard_map/ppermute | solution.py:989
  21.6 20.8 %collective-permute-start.4 = (bf16[304,768]{1,0:T(8,128)(2,1)}, bf16[304,768]{1,0:T(8,128)(2,1)S(1)}, u32[]{:S(2)}, u32[]{:S(2)}) collective-permute-start(bf16[304,768]{1,0:T(8,128)(2,1)} %get-tuple-element.125.refs_0_.refs_8_), channel_id=1, source_target_pairs={{0,8},{8,16},{16,24},{24,0},{1,9},{9,17},{17,25},{25,1},{2,10},{10... | collective-permute-start | bytes 1400840 | tf_op jit(solution)/shard_map/ppermute | solution.py:989
  21.6 19.6 %collective-permute-start.7 = (bf16[288,768]{1,0:T(8,128)(2,1)}, bf16[288,768]{1,0:T(8,128)(2,1)S(1)}, u32[]{:S(2)}, u32[]{:S(2)}) collective-permute-start(bf16[288,768]{1,0:T(8,128)(2,1)} %get-tuple-element.137.refs_0_), channel_id=1, source_target_pairs={{0,4},{4,0},{1,5},{5,1},{2,6},{6,2},{3,7},{7,3},{8,12},{12,8},{9,1... | collective-permute-start | bytes 1327112 | tf_op jit(solution)/shard_map/ppermute | solution.py:993
  42.4 24.4 %collective-permute-start.8 = (bf16[384,768]{1,0:T(8,128)(2,1)S(1)}, bf16[384,768]{1,0:T(8,128)(2,1)S(1)}, u32[]{:S(2)}, u32[]{:S(2)}) collective-permute-start(bf16[384,768]{1,0:T(8,128)(2,1)S(1)} %fusion.1.x0.g0), channel_id=1, source_target_pairs={{0,1},{1,0},{2,3},{3,2},{4,5},{5,4},{6,7},{7,6},{8,9},{9,8},{10,11... | collective-permute-start | bytes 1769480 | tf_op jit(solution)/shard_map/ppermute | solution.py:984
  44.4 22.4 %collective-permute-start.9 = (bf16[304,768]{1,0:T(8,128)(2,1)}, bf16[304,768]{1,0:T(8,128)(2,1)S(1)}, u32[]{:S(2)}, u32[]{:S(2)}) collective-permute-start(bf16[304,768]{1,0:T(8,128)(2,1)} %get-tuple-element.125.refs_0_.refs_8_), channel_id=1, source_target_pairs={{0,16},{8,24},{16,0},{24,8},{1,17},{9,25},{17,1},{25,9},{2,18},{10... | collective-permute-start | bytes 1400840 | tf_op jit(solution)/shard_map/ppermute | solution.py:989
  44.6 22.2 %collective-permute-start.10 = (bf16[304,768]{1,0:T(8,128)(2,1)S(1)}, bf16[304,768]{1,0:T(8,128)(2,1)S(1)}, u32[]{:S(2)}, u32[]{:S(2)}) collective-permute-start(bf16[304,768]{1,0:T(8,128)(2,1)S(1)} %collective-permute-done.4.refs_1_.refs_9_), channel_id=1, source_target_pairs={{0,4},{4,0},{1,5},{5,1},{2,6},{6,2},{3,7},{7,3},{8,12},{12,8},{9,1... | collective-permute-start | bytes 1400840 | tf_op jit(solution)/shard_map/ppermute | solution.py:993
  70.0 26.9 %collective-permute-start.19 = (bf16[288,768]{1,0:T(8,128)(2,1)}, bf16[288,768]{1,0:T(8,128)(2,1)S(1)}, u32[]{:S(2)}, u32[]{:S(2)}) collective-permute-start(bf16[288,768]{1,0:T(8,128)(2,1)} %get-tuple-element.137.refs_0_), channel_id=1, source_target_pairs={{0,24},{8,0},{16,8},{24,16},{1,25},{9,1},{17,9},{25,17},{2,26},{10... | collective-permute-start | bytes 1327112 | tf_op jit(solution)/shard_map/ppermute | solution.py:989
  71.1 25.7 %collective-permute-start.17 = (bf16[288,768]{1,0:T(8,128)(2,1)}, bf16[288,768]{1,0:T(8,128)(2,1)S(1)}, u32[]{:S(2)}, u32[]{:S(2)}) collective-permute-start(bf16[288,768]{1,0:T(8,128)(2,1)} %get-tuple-element.137.refs_0_), channel_id=1, source_target_pairs={{0,8},{8,16},{16,24},{24,0},{1,9},{9,17},{17,25},{25,1},{2,10},{10... | collective-permute-start | bytes 1327112 | tf_op jit(solution)/shard_map/ppermute | solution.py:989
  71.6 11.7 %collective-permute-start.13 = (bf16[304,768]{1,0:T(8,128)(2,1)S(1)}, bf16[304,768]{1,0:T(8,128)(2,1)S(1)}, u32[]{:S(2)}, u32[]{:S(2)}) collective-permute-start(bf16[304,768]{1,0:T(8,128)(2,1)S(1)} %collective-permute-done.9.refs_2_.refs_10_), channel_id=1, source_target_pairs={{0,4},{4,0},{1,5},{5,1},{2,6},{6,2},{3,7},{7,3},{8,12},{12,8},{9,1... | collective-permute-start | bytes 1400840 | tf_op jit(solution)/shard_map/ppermute | solution.py:993
  96.9 22.2 %collective-permute-start.22 = (bf16[288,768]{1,0:T(8,128)(2,1)S(1)}, bf16[288,768]{1,0:T(8,128)(2,1)S(1)}, u32[]{:S(2)}, u32[]{:S(2)}) collective-permute-start(bf16[288,768]{1,0:T(8,128)(2,1)S(1)} %copy-done.20), channel_id=1, source_target_pairs={{0,16},{8,24},{16,0},{24,8},{1,17},{9,25},{17,1},{25,9},{2,18},{10... | collective-permute-start | bytes 1327112 | tf_op jit(solution)/shard_map/ppermute | solution.py:989
  97.0 22.5 %collective-permute-start.20 = (bf16[288,768]{1,0:T(8,128)(2,1)S(1)}, bf16[288,768]{1,0:T(8,128)(2,1)S(1)}, u32[]{:S(2)}, u32[]{:S(2)}) collective-permute-start(bf16[288,768]{1,0:T(8,128)(2,1)S(1)} %collective-permute-done.19.refs_3_), channel_id=1, source_target_pairs={{0,4},{4,0},{1,5},{5,1},{2,6},{6,2},{3,7},{7,3},{8,12},{12,8},{9,1... | collective-permute-start | bytes 1327112 | tf_op jit(solution)/shard_map/ppermute | solution.py:993
  97.6 21.9 %collective-permute-start.18 = (bf16[288,768]{1,0:T(8,128)(2,1)S(1)}, bf16[288,768]{1,0:T(8,128)(2,1)S(1)}, u32[]{:S(2)}, u32[]{:S(2)}) collective-permute-start(bf16[288,768]{1,0:T(8,128)(2,1)S(1)} %collective-permute-done.17.refs_1_), channel_id=1, source_target_pairs={{0,4},{4,0},{1,5},{5,1},{2,6},{6,2},{3,7},{7,3},{8,12},{12,8},{9,1... | collective-permute-start | bytes 1327112 | tf_op jit(solution)/shard_map/ppermute | solution.py:993
  139.6 19.7 %collective-permute-start.28 = (bf16[4,144,768]{2,1,0:T(8,128)(2,1)}, bf16[4,144,768]{2,1,0:T(8,128)(2,1)S(1)}, u32[]{:S(2)}, u32[]{:S(2)}) collective-permute-start(bf16[4,144,768]{2,1,0:T(8,128)(2,1)} %get-tuple-element.149), channel_id=1, source_target_pairs={{0,4},{4,0},{1,5},{5,1},{2,6},{6,2},{3,7},{7,3},{8,12},{12,8},{9,1... | collective-permute-start | bytes 2654216 | tf_op jit(solution)/shard_map/ppermute | solution.py:993
  139.9 15.2 %collective-permute-start.24 = (bf16[2,48,768]{2,1,0:T(8,128)(2,1)}, bf16[2,48,768]{2,1,0:T(8,128)(2,1)S(1)}, u32[]{:S(2)}, u32[]{:S(2)}) collective-permute-start(bf16[2,48,768]{2,1,0:T(8,128)(2,1)} %get-tuple-element.145), channel_id=1, source_target_pairs={{0,8},{8,16},{16,24},{24,0},{1,9},{9,17},{17,25},{25,1},{2,10},{10... | collective-permute-start | bytes 442376 | tf_op jit(solution)/shard_map/ppermute | solution.py:989
  140.8 14.3 %collective-permute-start.25 = (bf16[2,48,768]{2,1,0:T(8,128)(2,1)}, bf16[2,48,768]{2,1,0:T(8,128)(2,1)S(1)}, u32[]{:S(2)}, u32[]{:S(2)}) collective-permute-start(bf16[2,48,768]{2,1,0:T(8,128)(2,1)} %get-tuple-element.146), channel_id=1, source_target_pairs={{0,16},{8,24},{16,0},{24,8},{1,17},{9,25},{17,1},{25,9},{2,18},{10... | collective-permute-start | bytes 442376 | tf_op jit(solution)/shard_map/ppermute | solution.py:989
  142.2 12.9 %collective-permute-start.26 = (bf16[2,48,768]{2,1,0:T(8,128)(2,1)}, bf16[2,48,768]{2,1,0:T(8,128)(2,1)S(1)}, u32[]{:S(2)}, u32[]{:S(2)}) collective-permute-start(bf16[2,48,768]{2,1,0:T(8,128)(2,1)} %get-tuple-element.147), channel_id=1, source_target_pairs={{0,24},{8,0},{16,8},{24,16},{1,25},{9,1},{17,9},{25,17},{2,26},{10... | collective-permute-start | bytes 442376 | tf_op jit(solution)/shard_map/ppermute | solution.py:989
  182.0 24.6 %collective-permute-start.34 = (bf16[4,112,768]{2,1,0:T(8,128)(2,1)S(1)}, bf16[4,112,768]{2,1,0:T(8,128)(2,1)S(1)}, u32[]{:S(2)}, u32[]{:S(2)}) collective-permute-start(bf16[4,112,768]{2,1,0:T(8,128)(2,1)S(1)} %copy-done.64), channel_id=1, source_target_pairs={{0,4},{4,0},{1,5},{5,1},{2,6},{6,2},{3,7},{7,3},{8,12},{12,8},{9,1... | collective-permute-start | bytes 2064392 | tf_op jit(solution)/shard_map/ppermute | solution.py:993
  191.1 20.3 %collective-permute-start.33 = (bf16[2,192,768]{2,1,0:T(8,128)(2,1)}, bf16[2,192,768]{2,1,0:T(8,128)(2,1)S(1)}, u32[]{:S(2)}, u32[]{:S(2)}) collective-permute-start(bf16[2,192,768]{2,1,0:T(8,128)(2,1)} %get-tuple-element.161), channel_id=1, source_target_pairs={{0,4},{4,0},{1,5},{5,1},{2,6},{6,2},{3,7},{7,3},{8,12},{12,8},{9,1... | collective-permute-start | bytes 1769480 | tf_op jit(solution)/shard_map/ppermute | solution.py:993
  192.0 14.6 %collective-permute-start.35 = (bf16[144,768]{1,0:T(8,128)(2,1)S(1)}, bf16[144,768]{1,0:T(8,128)(2,1)S(1)}, u32[]{:S(2)}, u32[]{:S(2)}) collective-permute-start(bf16[144,768]{1,0:T(8,128)(2,1)S(1)} %copy-done.70), channel_id=1, source_target_pairs={{0,16},{8,24},{16,0},{24,8},{1,17},{9,25},{17,1},{25,9},{2,18},{10... | collective-permute-start | bytes 663560 | tf_op jit(solution)/shard_map/ppermute | solution.py:989
  193.4 13.2 %collective-permute-start.36 = (bf16[144,768]{1,0:T(8,128)(2,1)S(1)}, bf16[144,768]{1,0:T(8,128)(2,1)S(1)}, u32[]{:S(2)}, u32[]{:S(2)}) collective-permute-start(bf16[144,768]{1,0:T(8,128)(2,1)S(1)} %copy-done.69), channel_id=1, source_target_pairs={{0,24},{8,0},{16,8},{24,16},{1,25},{9,1},{17,9},{25,17},{2,26},{10... | collective-permute-start | bytes 663560 | tf_op jit(solution)/shard_map/ppermute | solution.py:989
  216.5 17.7 %collective-permute-start.43 = (bf16[2,192,768]{2,1,0:T(8,128)(2,1)S(1)}, bf16[2,192,768]{2,1,0:T(8,128)(2,1)S(1)}, u32[]{:S(2)}, u32[]{:S(2)}) collective-permute-start(bf16[2,192,768]{2,1,0:T(8,128)(2,1)S(1)} %copy-done.66), channel_id=1, source_target_pairs={{0,4},{4,0},{1,5},{5,1},{2,6},{6,2},{3,7},{7,3},{8,12},{12,8},{9,1... | collective-permute-start | bytes 1769480 | tf_op jit(solution)/shard_map/ppermute | solution.py:993
  217.1 28.6 %collective-permute-start.41 = (bf16[4,112,768]{2,1,0:T(8,128)(2,1)S(1)}, bf16[4,112,768]{2,1,0:T(8,128)(2,1)S(1)}, u32[]{:S(2)}, u32[]{:S(2)}) collective-permute-start(bf16[4,112,768]{2,1,0:T(8,128)(2,1)S(1)} %copy-done.65), channel_id=1, source_target_pairs={{0,4},{4,0},{1,5},{5,1},{2,6},{6,2},{3,7},{7,3},{8,12},{12,8},{9,1... | collective-permute-start | bytes 2064392 | tf_op jit(solution)/shard_map/ppermute | solution.py:993
  218.0 23.0 %collective-permute-start.42 = (bf16[304,768]{1,0:T(8,128)(2,1)}, bf16[304,768]{1,0:T(8,128)(2,1)S(1)}, u32[]{:S(2)}, u32[]{:S(2)}) collective-permute-start(bf16[304,768]{1,0:T(8,128)(2,1)} %get-tuple-element.169), channel_id=1, source_target_pairs={{0,8},{8,16},{16,24},{24,0},{1,9},{9,17},{17,25},{25,1},{2,10},{10... | collective-permute-start | bytes 1400840 | tf_op jit(solution)/shard_map/ppermute | solution.py:989
  219.0 22.0 %collective-permute-start.44 = (bf16[304,768]{1,0:T(8,128)(2,1)}, bf16[304,768]{1,0:T(8,128)(2,1)S(1)}, u32[]{:S(2)}, u32[]{:S(2)}) collective-permute-start(bf16[304,768]{1,0:T(8,128)(2,1)} %get-tuple-element.182), channel_id=1, source_target_pairs={{0,24},{8,0},{16,8},{24,16},{1,25},{9,1},{17,9},{25,17},{2,26},{10... | collective-permute-start | bytes 1400840 | tf_op jit(solution)/shard_map/ppermute | solution.py:989
  244.1 22.7 %collective-permute-start.45 = (bf16[304,768]{1,0:T(8,128)(2,1)}, bf16[304,768]{1,0:T(8,128)(2,1)S(1)}, u32[]{:S(2)}, u32[]{:S(2)}) collective-permute-start(bf16[304,768]{1,0:T(8,128)(2,1)} %add_second.1), channel_id=1, source_target_pairs={{0,16},{8,24},{16,0},{24,8},{1,17},{9,25},{17,1},{25,9},{2,18},{10... | collective-permute-start | bytes 1400840 | tf_op jit(solution)/shard_map/ppermute | solution.py:989
  266.8 20.9 %collective-permute-start.49 = (bf16[112,768]{1,0:T(8,128)(2,1)}, bf16[112,768]{1,0:T(8,128)(2,1)S(1)}, u32[]{:S(2)}, u32[]{:S(2)}) collective-permute-start(bf16[112,768]{1,0:T(8,128)(2,1)} %get-tuple-element.196), channel_id=1, source_target_pairs={{0,24},{8,0},{16,8},{24,16},{1,25},{9,1},{17,9},{25,17},{2,26},{10... | collective-permute-start | bytes 516104 | tf_op jit(solution)/shard_map/ppermute | solution.py:989
  268.9 18.9 %collective-permute-start.48 = (bf16[112,768]{1,0:T(8,128)(2,1)}, bf16[112,768]{1,0:T(8,128)(2,1)S(1)}, u32[]{:S(2)}, u32[]{:S(2)}) collective-permute-start(bf16[112,768]{1,0:T(8,128)(2,1)} %get-tuple-element.194), channel_id=1, source_target_pairs={{0,16},{8,24},{16,0},{24,8},{1,17},{9,25},{17,1},{25,9},{2,18},{10... | collective-permute-start | bytes 516104 | tf_op jit(solution)/shard_map/ppermute | solution.py:989
  268.9 19.6 %collective-permute-start.47 = (bf16[112,768]{1,0:T(8,128)(2,1)}, bf16[112,768]{1,0:T(8,128)(2,1)S(1)}, u32[]{:S(2)}, u32[]{:S(2)}) collective-permute-start(bf16[112,768]{1,0:T(8,128)(2,1)} %get-tuple-element.192), channel_id=1, source_target_pairs={{0,8},{8,16},{16,24},{24,0},{1,9},{9,17},{17,25},{25,1},{2,10},{10... | collective-permute-start | bytes 516104 | tf_op jit(solution)/shard_map/ppermute | solution.py:989
  278.6 15.3 %collective-permute-start.54 = (bf16[64,768]{1,0:T(8,128)(2,1)}, bf16[64,768]{1,0:T(8,128)(2,1)S(1)}, u32[]{:S(2)}, u32[]{:S(2)}) collective-permute-start(bf16[64,768]{1,0:T(8,128)(2,1)} %get-tuple-element.204), channel_id=1, source_target_pairs={{0,1},{1,0},{2,3},{3,2},{4,5},{5,4},{6,7},{7,6},{8,9},{9,8},{10,11... | collective-permute-start | bytes 294920 | tf_op jit(solution)/shard_map/ppermute | solution.py:984
  280.1 13.4 %collective-permute-start.57 = (bf16[24,768]{1,0:T(8,128)(2,1)}, bf16[24,768]{1,0:T(8,128)(2,1)S(1)}, u32[]{:S(2)}, u32[]{:S(2)}) collective-permute-start(bf16[24,768]{1,0:T(8,128)(2,1)} %get-tuple-element.209), channel_id=1, source_target_pairs={{0,0},{4,1},{8,2},{12,3},{16,4},{20,5},{24,6},{28,7},{1,8},{5,9},{... | collective-permute-start | bytes 110600 | tf_op jit(solution)/shard_map/ppermute | solution.py:1187
  (98 other events, 908.9 us)

commit v5 on v4

--- a/solution.py
+++ b/solution.py
@@ -1236,10 +1236,10 @@
         after(m_second0, both1, both3, grad, activations), HALVES[1][:1], (0,), "add_second"
     )
     a_added0 = add(
-        block_a, a_keep0, after(a_other0, both2), (1, 2, 3), (1, 2, 3), "add_attend"
+        block_a, a_keep0, after(a_other0, both2, e_keep), (1, 2, 3), (1, 2, 3), "add_attend"
     )
     both2 = line_shift(both2, 2)
-    a_sums0 = shifts([after(piece, both2) for piece in a_added0])
+    a_sums0 = shifts([after(piece, both2, e_other) for piece in a_added0])
     both = (both1, both2, both3)
     outs[1] = split(
         (a_keep1, a_other1, *both), (m_keep1, one_of(m_other1, 0), *m_sums1), (e_keep, e_other)

time: 310 us -> 307 us (level)
  waiting for transfers between devices: 126 us -> 121 us
    ppermute x14, waiting for transfers between devices: 48.3 us -> 45 us  [line_flip(): return lax.ppermute(piece, 'y', [(0, 1), (1, 0)])]
  transfers between devices with their start and end apart: 58 -> 58, of which waited for: 21 -> 20; matrix products, arithmetic and copies ran while one was open for 2% -> 2% of each run, Pallas kernels for 21% -> 21%
where the time goes in v5:
time: 307 us; the launch traced here: 304 us
  waiting for transfers between devices  121 us (39%)
  Pallas kernels  85.6 us (28%)
  starting transfers between devices  75.6 us (25%)
  other arithmetic  10.4 us (3%)
  local copies, waits for them, and re-layouts  8.99 us (3%)
    pallas_call x20, Pallas kernels, run(): pl.pallas_call(body, grid=(1,), out_shape=out_shape, in_specs=[pl.BlockSp...  85.6 us
    ppermute x18, waiting for transfers between devices, line_shift(): lax.ppermute(piece, 'z', [(i, (i + shift) % size) for i in range(size)])  50.4 us
    ppermute x14, waiting for transfers between devices, line_flip(): return lax.ppermute(piece, 'y', [(0, 1), (1, 0)])  45 us
    ppermute x23, starting transfers between devices, team_send(): return lax.ppermute(piece, TEAM_AXES, flips)  28.7 us
    ppermute x23, waiting for transfers between devices, team_send(): return lax.ppermute(piece, TEAM_AXES, flips)  19 us
    ppermute x18, starting transfers between devices, line_shift(): lax.ppermute(piece, 'z', [(i, (i + shift) % size) for i in range(size)])  17.6 us
    ppermute x2, starting transfers between devices, split(): attn_rows = lax.ppermute(mine[TEAM + 1], everywhere, gather_back)  13.4 us
    ppermute x14, starting transfers between devices, line_flip(): return lax.ppermute(piece, 'y', [(0, 1), (1, 0)])  10.3 us
  transfers between devices with their start and end apart: 58, of which 20 were waited for; matrix products, arithmetic and copies ran while one was open for 2% of the time, Pallas kernels for 21%

profile of v5, /device:TPU:5, one launch (start us, length us, event | category | flops | bytes accessed | tf_op | source)
XLA Modules:
  0.0 303.6 jit_solution(8745373072790273030)
XLA Ops:
  5.9 5.6 %collective-permute-start.3 = (bf16[2,24,768]{2,1,0:T(8,128)(2,1)}, bf16[2,24,768]{2,1,0:T(8,128)(2,1)S(1)}, u32[]{:S(2)}, u32[]{:S(2)}) collective-permute-start(bf16[2,24,768]{2,1,0:T(8,128)(2,1)} %param.20), channel_id=1, source_target_pairs={{0,0},{1,4},{2,8},{3,12},{4,16},{5,20},{6,24},{7,28},{8,1},{9,5},{... | collective-permute-start | bytes 221192 | tf_op jit(solution)/shard_map/ppermute | solution.py:1047
  11.4 4.9 %collective-permute-done.3.attn_ref = bf16[2,24,768]{2,1,0:T(8,128)(2,1)S(1)} collective-permute-done((bf16[2,24,768]{2,1,0:T(8,128)(2,1)}, bf16[2,24,768]{2,1,0:T(8,128)(2,1)S(1)}, u32[]{:S(2)}, u32[]{:S(2)}) %collective-permute-start.3) | collective-permute-done | bytes 73760 | tf_op jit(solution)/shard_map/ppermute | solution.py:1047
  23.2 18.0 %collective-permute-done.7.refs_4_ = bf16[288,768]{1,0:T(8,128)(2,1)S(1)} collective-permute-done((bf16[288,768]{1,0:T(8,128)(2,1)}, bf16[288,768]{1,0:T(8,128)(2,1)S(1)}, u32[]{:S(2)}, u32[]{:S(2)}) %collective-permute-start.7) | collective-permute-done | bytes 442400 | tf_op jit(solution)/shard_map/ppermute | solution.py:993
  45.3 7.1 %collective-permute-done.11.refs_7_.refs_15_ = bf16[304,768]{1,0:T(8,128)(2,1)S(1)} collective-permute-done((bf16[304,768]{1,0:T(8,128)(2,1)S(1)}, bf16[304,768]{1,0:T(8,128)(2,1)S(1)}, u32[]{:S(2)}, u32[]{:S(2)}) %collective-permute-start.11) | collective-permute-done | bytes 466976 | tf_op jit(solution)/shard_map/ppermute | solution.py:993
  52.4 14.4 %collective-permute-done.9.refs_2_.refs_10_ = bf16[304,768]{1,0:T(8,128)(2,1)S(1)} collective-permute-done((bf16[304,768]{1,0:T(8,128)(2,1)}, bf16[304,768]{1,0:T(8,128)(2,1)S(1)}, u32[]{:S(2)}, u32[]{:S(2)}) %collective-permute-start.9) | collective-permute-done | bytes 466976 | tf_op jit(solution)/shard_map/ppermute | solution.py:989
  76.4 6.9 %collective-permute-done.13.refs_6_.refs_14_ = bf16[304,768]{1,0:T(8,128)(2,1)S(1)} collective-permute-done((bf16[304,768]{1,0:T(8,128)(2,1)S(1)}, bf16[304,768]{1,0:T(8,128)(2,1)S(1)}, u32[]{:S(2)}, u32[]{:S(2)}) %collective-permute-start.13) | collective-permute-done | bytes 466976 | tf_op jit(solution)/shard_map/ppermute | solution.py:993
  84.1 6.2 %attend_forward.1 = (f32[512,768]{1,0:T(8,128)}, f32[2,8,768]{2,1,0:T(8,128)}) custom-call(s32[3]{0:T(128)} %pad_add_fusion.1.me_ref, bf16[384,768]{1,0:T(8,128)(2,1)} %copy-done.1, bf16[384,768]{1,0:T(8,128)(2,1)} %copy-done.2, bf16[768,768]{1,0:T(8,128)(2,1)} %copy-done, bf16[768,768]{1,0:T(8,128)(2,1)} %copy-done, ...), custom_call_target="tpu_custom_call" | custom-call | tf_op jit(solution)/shard_map/attend_forward/pallas_call | solution.py:1020
  90.3 5.2 %mlp_forward.1 = (f32[128,768]{1,0:T(8,128)}, f32[128,768]{1,0:T(8,128)}, bf16[256,768]{1,0:T(8,128)(2,1)}) custom-call(s32[3]{0:T(128)} %pad_add_fusion.1.me_ref, bf16[384,768]{1,0:T(8,128)(2,1)} %copy-done.1, bf16[384,768]{1,0:T(8,128)(2,1)} %copy-done.2, bf16[768,768]{1,0:T(8,128)(2,1)} %copy-done, bf16[768,768]{1,0:T(8,128)(2,1)} %copy-done, ...), custom_call_target="tpu_custom_call" | custom-call | tf_op jit(solution)/shard_map/mlp_forward/pallas_call | solution.py:1020
  101.0 4.4 %collective-permute-done.15.y2 = bf16[128,768]{1,0:T(8,128)(2,1)S(1)} collective-permute-done((bf16[128,768]{1,0:T(8,128)(2,1)S(1)}, bf16[128,768]{1,0:T(8,128)(2,1)S(1)}, u32[]{:S(2)}, u32[]{:S(2)}) %collective-permute-start.15) | collective-permute-done | bytes 196640 | tf_op jit(solution)/shard_map/ppermute | solution.py:984
  109.6 9.5 %collective-permute-done.22.refs_2_ = bf16[288,768]{1,0:T(8,128)(2,1)S(1)} collective-permute-done((bf16[288,768]{1,0:T(8,128)(2,1)S(1)}, bf16[288,768]{1,0:T(8,128)(2,1)S(1)}, u32[]{:S(2)}, u32[]{:S(2)}) %collective-permute-start.22) | collective-permute-done | bytes 442400 | tf_op jit(solution)/shard_map/ppermute | solution.py:989
  121.9 8.1 %collective-permute-done.23.refs_6_ = bf16[288,768]{1,0:T(8,128)(2,1)S(1)} collective-permute-done((bf16[288,768]{1,0:T(8,128)(2,1)S(1)}, bf16[288,768]{1,0:T(8,128)(2,1)S(1)}, u32[]{:S(2)}, u32[]{:S(2)}) %collective-permute-start.23) | collective-permute-done | bytes 442400 | tf_op jit(solution)/shard_map/ppermute | solution.py:993
  131.6 8.0 %mlp_both.2 = (f32[512,768]{1,0:T(8,128)}, f32[8,768]{1,0:T(8,128)}, f32[512,768]{1,0:T(8,128)}, bf16[2,48,768]{2,1,0:T(8,128)(2,1)}, bf16[2,48,768]{2,1,0:T(8,1...) custom-call(s32[3]{0:T(128)} %pad_add_fusion.1.me_ref, ...), custom_call_target="tpu_custom_call" | custom-call | tf_op jit(solution)/shard_map/mlp_both/pallas_call | solution.py:1020
  143.4 11.7 %attend_both.2 = (bf16[4,112,768]{2,1,0:T(8,128)(2,1)}, bf16[4,112,768]{2,1,0:T(8,128)(2,1)}, f32[128,768]{1,0:T(8,128)}, f32[128,768]{1,0:T(8,128)}, bf16[256,7...) custom-call(s32[3]{0:T(128)} %pad_add_fusion.1.me_ref, ...), custom_call_target="tpu_custom_call" | custom-call | tf_op jit(solution)/shard_map/attend_both/pallas_call | solution.py:1020
  155.1 2.6 collective-permute-start.27
  161.8 3.3 %collective-permute-done.29.n2 = bf16[128,768]{1,0:T(8,128)(2,1)S(1)} collective-permute-done((bf16[128,768]{1,0:T(8,128)(2,1)S(1)}, bf16[128,768]{1,0:T(8,128)(2,1)S(1)}, u32[]{:S(2)}, u32[]{:S(2)}) %collective-permute-start.29) | collective-permute-done | bytes 196640 | tf_op jit(solution)/shard_map/ppermute | solution.py:984
  165.9 2.5 norm_backward.2
  169.6 3.6 %collective-permute-done.30.g1 = bf16[128,768]{1,0:T(8,128)(2,1)S(1)} collective-permute-done((bf16[128,768]{1,0:T(8,128)(2,1)}, bf16[128,768]{1,0:T(8,128)(2,1)S(1)}, u32[]{:S(2)}, u32[]{:S(2)}) %collective-permute-start.30) | collective-permute-done | bytes 196640 | tf_op jit(solution)/shard_map/ppermute | solution.py:984
  174.2 4.9 %collective-permute-start.31 = (bf16[256,768]{1,0:T(8,128)(2,1)S(1)}, bf16[256,768]{1,0:T(8,128)(2,1)S(1)}, u32[]{:S(2)}, u32[]{:S(2)}) collective-permute-start(bf16[256,768]{1,0:T(8,128)(2,1)S(1)} %pad_maximum_fusion.3), channel_id=1, source_target_pairs={{0,2},{1,3},{2,0},{3,1},{4,6},{5,7},{6,4},{7,5},{8,10},{9,11},{10,... | collective-permute-start | bytes 1179656 | tf_op jit(solution)/shard_map/ppermute | solution.py:984
  183.4 7.6 %mlp_both.3 = (f32[512,768]{1,0:T(8,128)}, f32[8,768]{1,0:T(8,128)}, bf16[4,192,768]{2,1,0:T(8,128)(2,1)}, bf16[2,192,768]{2,1,0:T(8,128)(2,1)}, bf16[2,192,768]{2,1,0:T(8,128)(2,1)}) custom-call(s32[3]{0:T(128)} %pad_add_fusion.1.me_ref, bf16[384,768]{1,0:T(8,128)(2,1)} %copy-done.1, bf16[384,768]{1,0:T(8,128)(2,1)} %copy-done.2, bf16[768,768]{1,0:T(8,128)(2,1)} %copy-done, ...), custom_call_target="tpu_custom_call" | custom-call | tf_op jit(solution)/shard_map/mlp_both/pallas_call | solution.py:1020
  195.2 11.3 %attend_both.3 = (bf16[4,112,768]{2,1,0:T(8,128)(2,1)}, bf16[4,112,768]{2,1,0:T(8,128)(2,1)}, f32[128,768]{1,0:T(8,128)}, f32[128,768]{1,0:T(8,128)}, bf16[256,768]{1,0:T(8,128)(2,1)}) custom-call(s32[3]{0:T(128)} %pad_add_fusion.1.me_ref, bf16[384,768]{1,0:T(8,128)(2,1)} %copy-done.1, bf16[384,768]{1,0:T(8,128)(2,1)} %copy-done.2, ...), custom_call_target="tpu_custom_call" | custom-call | tf_op jit(solution)/shard_map/attend_both/pallas_call | solution.py:1020
  206.6 4.8 %collective-permute-done.33.m_received = bf16[2,192,768]{2,1,0:T(8,128)(2,1)S(1)} collective-permute-done((bf16[2,192,768]{2,1,0:T(8,128)(2,1)}, bf16[2,192,768]{2,1,0:T(8,128)(2,1)S(1)}, u32[]{:S(2)}, u32[]{:S(2)}) %collective-permute-start.33) | collective-permute-done | bytes 589856 | tf_op jit(solution)/shard_map/ppermute | solution.py:993
  212.2 3.1 %add_first.1 = (bf16[304,768]{1,0:T(8,128)(2,1)}, bf16[304,768]{1,0:T(8,128)(2,1)}) custom-call(s32[3]{0:T(128)} %pad_add_fusion.1.me_ref, bf16[4,192,768]{2,1,0:T(8,128)(2,1)} %get-tuple-element.159.m_keep.refs_5_, bf16[2,192,768]{2,1,0:T(8,128)(2,1)} %copy-done.35, bf16[4,112,768]{2,1,0:T(8,128)(2,1)} %get-tuple-element.168.a_keep.refs_0_, ...), custom_call_target="tpu_custom_call" | custom-call | tf_op jit(solution)/shard_map/add_first/pallas_call | solution.py:1020
  222.3 3.8 %collective-permute-done.38.y2 = bf16[128,768]{1,0:T(8,128)(2,1)S(1)} collective-permute-done((bf16[128,768]{1,0:T(8,128)(2,1)S(1)}, bf16[128,768]{1,0:T(8,128)(2,1)S(1)}, u32[]{:S(2)}, u32[]{:S(2)}) %collective-permute-start.38) | collective-permute-done | bytes 196640 | tf_op jit(solution)/shard_map/ppermute | solution.py:984
  234.2 6.7 %collective-permute-done.44.refs_4_.refs_9_ = bf16[304,768]{1,0:T(8,128)(2,1)S(1)} collective-permute-done((bf16[304,768]{1,0:T(8,128)(2,1)}, bf16[304,768]{1,0:T(8,128)(2,1)S(1)}, u32[]{:S(2)}, u32[]{:S(2)}) %collective-permute-start.44) | collective-permute-done | bytes 466976 | tf_op jit(solution)/shard_map/ppermute | solution.py:989
  240.9 3.1 %add_second.1 = bf16[304,768]{1,0:T(8,128)(2,1)} custom-call(s32[3]{0:T(128)} %pad_add_fusion.1.me_ref, bf16[4,192,768]{2,1,0:T(8,128)(2,1)} %get-tuple-element.159.m_keep.refs_5_, bf16[2,192,768]{2,1,0:T(8,128)(2,1)} %copy-done.15, bf16[4,112,768]{2,1,0:T(8,128)(2,1)} %get-tuple-element.168.a_keep.refs_0_, bf16[4,112,768]{2,1,0:T(8,128)(2,1)} %copy-done.12), custom_call_target="tpu_custom_call" | custom-call | tf_op jit(solution)/shard_map/add_second/pallas_call | solution.py:1020
  250.5 16.2 %collective-permute-done.45.refs_3_.refs_8_ = bf16[304,768]{1,0:T(8,128)(2,1)S(1)} collective-permute-done((bf16[304,768]{1,0:T(8,128)(2,1)}, bf16[304,768]{1,0:T(8,128)(2,1)S(1)}, u32[]{:S(2)}, u32[]{:S(2)}) %collective-permute-start.45) | collective-permute-done | bytes 466976 | tf_op jit(solution)/shard_map/ppermute | solution.py:989
  269.1 3.2 %split_gradients.2 = (bf16[64,768]{1,0:T(8,128)(2,1)}, bf16[64,768]{1,0:T(8,128)(2,1)}, bf16[64,768]{1,0:T(8,128)(2,1)}, bf16[64,768]{1,0:T(8,128)(2,1)}, f32[96...) custom-call(s32[3]{0:T(128)} %pad_add_fusion.1.me_ref, ...), custom_call_target="tpu_custom_call" | custom-call | tf_op jit(solution)/shard_map/split_gradients/pallas_call | solution.py:1020
  273.5 7.1 %collective-permute-start.57 = (bf16[24,768]{1,0:T(8,128)(2,1)}, bf16[24,768]{1,0:T(8,128)(2,1)S(1)}, u32[]{:S(2)}, u32[]{:S(2)}) collective-permute-start(bf16[24,768]{1,0:T(8,128)(2,1)} %get-tuple-element.209), channel_id=1, source_target_pairs={{0,0},{4,1},{8,2},{12,3},{16,4},{20,5},{24,6},{28,7},{1,8},{5,9},{... | collective-permute-start | bytes 110600 | tf_op jit(solution)/shard_map/ppermute | solution.py:1187
  283.0 2.5 collective-permute-start.56
  286.3 3.2 %split_gradients.3 = (bf16[64,768]{1,0:T(8,128)(2,1)}, bf16[64,768]{1,0:T(8,128)(2,1)}, bf16[64,768]{1,0:T(8,128)(2,1)}, bf16[64,768]{1,0:T(8,128)(2,1)}, f32[96...) custom-call(s32[3]{0:T(128)} %pad_add_fusion.1.me_ref, ...), custom_call_target="tpu_custom_call" | custom-call | tf_op jit(solution)/shard_map/split_gradients/pallas_call | solution.py:1020
  291.4 6.3 %collective-permute-start.53 = (bf16[24,768]{1,0:T(8,128)(2,1)}, bf16[24,768]{1,0:T(8,128)(2,1)S(1)}, u32[]{:S(2)}, u32[]{:S(2)}) collective-permute-start(bf16[24,768]{1,0:T(8,128)(2,1)} %get-tuple-element.203), channel_id=1, source_target_pairs={{0,0},{4,1},{8,2},{12,3},{16,4},{20,5},{24,6},{28,7},{1,8},{5,9},{... | collective-permute-start | bytes 110600 | tf_op jit(solution)/shard_map/ppermute | solution.py:1187
  300.3 2.9 unpack_gradients.1
  (273 shorter events, 93.2 us)
Async XLA Ops:
  3.6 12.8 %collective-permute-start = (bf16[112,768]{1,0:T(8,128)(2,1)}, bf16[112,768]{1,0:T(8,128)(2,1)S(1)}, u32[]{:S(2)}, u32[]{:S(2)}) collective-permute-start(bf16[112,768]{1,0:T(8,128)(2,1)} %get-tuple-element.119), channel_id=1, source_target_pairs={{0,1},{1,0},{2,3},{3,2},{4,5},{5,4},{6,7},{7,6},{8,9},{9,8},{10,11... | collective-permute-start | bytes 516104 | tf_op jit(solution)/shard_map/ppermute | solution.py:984
  19.6 21.6 %collective-permute-start.6 = (bf16[304,768]{1,0:T(8,128)(2,1)}, bf16[304,768]{1,0:T(8,128)(2,1)S(1)}, u32[]{:S(2)}, u32[]{:S(2)}) collective-permute-start(bf16[304,768]{1,0:T(8,128)(2,1)} %get-tuple-element.125.refs_0_.refs_8_), channel_id=1, source_target_pairs={{0,4},{4,0},{1,5},{5,1},{2,6},{6,2},{3,7},{7,3},{8,12},{12,8},{9,1... | collective-permute-start | bytes 1400840 | tf_op jit(solution)/shard_map/ppermute | solution.py:993
  19.7 21.6 %collective-permute-start.5 = (bf16[304,768]{1,0:T(8,128)(2,1)}, bf16[304,768]{1,0:T(8,128)(2,1)S(1)}, u32[]{:S(2)}, u32[]{:S(2)}) collective-permute-start(bf16[304,768]{1,0:T(8,128)(2,1)} %get-tuple-element.125.refs_0_.refs_8_), channel_id=1, source_target_pairs={{0,24},{8,0},{16,8},{24,16},{1,25},{9,1},{17,9},{25,17},{2,26},{10... | collective-permute-start | bytes 1400840 | tf_op jit(solution)/shard_map/ppermute | solution.py:989
  21.6 20.8 %collective-permute-start.4 = (bf16[304,768]{1,0:T(8,128)(2,1)}, bf16[304,768]{1,0:T(8,128)(2,1)S(1)}, u32[]{:S(2)}, u32[]{:S(2)}) collective-permute-start(bf16[304,768]{1,0:T(8,128)(2,1)} %get-tuple-element.125.refs_0_.refs_8_), channel_id=1, source_target_pairs={{0,8},{8,16},{16,24},{24,0},{1,9},{9,17},{17,25},{25,1},{2,10},{10... | collective-permute-start | bytes 1400840 | tf_op jit(solution)/shard_map/ppermute | solution.py:989
  21.6 19.6 %collective-permute-start.7 = (bf16[288,768]{1,0:T(8,128)(2,1)}, bf16[288,768]{1,0:T(8,128)(2,1)S(1)}, u32[]{:S(2)}, u32[]{:S(2)}) collective-permute-start(bf16[288,768]{1,0:T(8,128)(2,1)} %get-tuple-element.137.refs_0_), channel_id=1, source_target_pairs={{0,4},{4,0},{1,5},{5,1},{2,6},{6,2},{3,7},{7,3},{8,12},{12,8},{9,1... | collective-permute-start | bytes 1327112 | tf_op jit(solution)/shard_map/ppermute | solution.py:993
  42.4 24.4 %collective-permute-start.8 = (bf16[384,768]{1,0:T(8,128)(2,1)S(1)}, bf16[384,768]{1,0:T(8,128)(2,1)S(1)}, u32[]{:S(2)}, u32[]{:S(2)}) collective-permute-start(bf16[384,768]{1,0:T(8,128)(2,1)S(1)} %fusion.1.x0.g0), channel_id=1, source_target_pairs={{0,1},{1,0},{2,3},{3,2},{4,5},{5,4},{6,7},{7,6},{8,9},{9,8},{10,11... | collective-permute-start | bytes 1769480 | tf_op jit(solution)/shard_map/ppermute | solution.py:984
  44.4 22.4 %collective-permute-start.9 = (bf16[304,768]{1,0:T(8,128)(2,1)}, bf16[304,768]{1,0:T(8,128)(2,1)S(1)}, u32[]{:S(2)}, u32[]{:S(2)}) collective-permute-start(bf16[304,768]{1,0:T(8,128)(2,1)} %get-tuple-element.125.refs_0_.refs_8_), channel_id=1, source_target_pairs={{0,16},{8,24},{16,0},{24,8},{1,17},{9,25},{17,1},{25,9},{2,18},{10... | collective-permute-start | bytes 1400840 | tf_op jit(solution)/shard_map/ppermute | solution.py:989
  44.7 22.2 %collective-permute-start.10 = (bf16[304,768]{1,0:T(8,128)(2,1)S(1)}, bf16[304,768]{1,0:T(8,128)(2,1)S(1)}, u32[]{:S(2)}, u32[]{:S(2)}) collective-permute-start(bf16[304,768]{1,0:T(8,128)(2,1)S(1)} %collective-permute-done.4.refs_1_.refs_9_), channel_id=1, source_target_pairs={{0,4},{4,0},{1,5},{5,1},{2,6},{6,2},{3,7},{7,3},{8,12},{12,8},{9,1... | collective-permute-start | bytes 1400840 | tf_op jit(solution)/shard_map/ppermute | solution.py:993
  70.0 26.9 %collective-permute-start.19 = (bf16[288,768]{1,0:T(8,128)(2,1)}, bf16[288,768]{1,0:T(8,128)(2,1)S(1)}, u32[]{:S(2)}, u32[]{:S(2)}) collective-permute-start(bf16[288,768]{1,0:T(8,128)(2,1)} %get-tuple-element.137.refs_0_), channel_id=1, source_target_pairs={{0,24},{8,0},{16,8},{24,16},{1,25},{9,1},{17,9},{25,17},{2,26},{10... | collective-permute-start | bytes 1327112 | tf_op jit(solution)/shard_map/ppermute | solution.py:989
  71.2 25.7 %collective-permute-start.17 = (bf16[288,768]{1,0:T(8,128)(2,1)}, bf16[288,768]{1,0:T(8,128)(2,1)S(1)}, u32[]{:S(2)}, u32[]{:S(2)}) collective-permute-start(bf16[288,768]{1,0:T(8,128)(2,1)} %get-tuple-element.137.refs_0_), channel_id=1, source_target_pairs={{0,8},{8,16},{16,24},{24,0},{1,9},{9,17},{17,25},{25,1},{2,10},{10... | collective-permute-start | bytes 1327112 | tf_op jit(solution)/shard_map/ppermute | solution.py:989
  97.0 22.2 %collective-permute-start.22 = (bf16[288,768]{1,0:T(8,128)(2,1)S(1)}, bf16[288,768]{1,0:T(8,128)(2,1)S(1)}, u32[]{:S(2)}, u32[]{:S(2)}) collective-permute-start(bf16[288,768]{1,0:T(8,128)(2,1)S(1)} %copy-done.20), channel_id=1, source_target_pairs={{0,16},{8,24},{16,0},{24,8},{1,17},{9,25},{17,1},{25,9},{2,18},{10... | collective-permute-start | bytes 1327112 | tf_op jit(solution)/shard_map/ppermute | solution.py:989
  97.1 22.5 %collective-permute-start.20 = (bf16[288,768]{1,0:T(8,128)(2,1)S(1)}, bf16[288,768]{1,0:T(8,128)(2,1)S(1)}, u32[]{:S(2)}, u32[]{:S(2)}) collective-permute-start(bf16[288,768]{1,0:T(8,128)(2,1)S(1)} %collective-permute-done.19.refs_3_), channel_id=1, source_target_pairs={{0,4},{4,0},{1,5},{5,1},{2,6},{6,2},{3,7},{7,3},{8,12},{12,8},{9,1... | collective-permute-start | bytes 1327112 | tf_op jit(solution)/shard_map/ppermute | solution.py:993
  97.7 21.9 %collective-permute-start.18 = (bf16[288,768]{1,0:T(8,128)(2,1)S(1)}, bf16[288,768]{1,0:T(8,128)(2,1)S(1)}, u32[]{:S(2)}, u32[]{:S(2)}) collective-permute-start(bf16[288,768]{1,0:T(8,128)(2,1)S(1)} %collective-permute-done.17.refs_1_), channel_id=1, source_target_pairs={{0,4},{4,0},{1,5},{5,1},{2,6},{6,2},{3,7},{7,3},{8,12},{12,8},{9,1... | collective-permute-start | bytes 1327112 | tf_op jit(solution)/shard_map/ppermute | solution.py:993
  139.6 19.7 %collective-permute-start.28 = (bf16[4,144,768]{2,1,0:T(8,128)(2,1)}, bf16[4,144,768]{2,1,0:T(8,128)(2,1)S(1)}, u32[]{:S(2)}, u32[]{:S(2)}) collective-permute-start(bf16[4,144,768]{2,1,0:T(8,128)(2,1)} %get-tuple-element.149), channel_id=1, source_target_pairs={{0,4},{4,0},{1,5},{5,1},{2,6},{6,2},{3,7},{7,3},{8,12},{12,8},{9,1... | collective-permute-start | bytes 2654216 | tf_op jit(solution)/shard_map/ppermute | solution.py:993
  139.9 15.1 %collective-permute-start.24 = (bf16[2,48,768]{2,1,0:T(8,128)(2,1)}, bf16[2,48,768]{2,1,0:T(8,128)(2,1)S(1)}, u32[]{:S(2)}, u32[]{:S(2)}) collective-permute-start(bf16[2,48,768]{2,1,0:T(8,128)(2,1)} %get-tuple-element.145), channel_id=1, source_target_pairs={{0,8},{8,16},{16,24},{24,0},{1,9},{9,17},{17,25},{25,1},{2,10},{10... | collective-permute-start | bytes 442376 | tf_op jit(solution)/shard_map/ppermute | solution.py:989
  140.8 14.3 %collective-permute-start.25 = (bf16[2,48,768]{2,1,0:T(8,128)(2,1)}, bf16[2,48,768]{2,1,0:T(8,128)(2,1)S(1)}, u32[]{:S(2)}, u32[]{:S(2)}) collective-permute-start(bf16[2,48,768]{2,1,0:T(8,128)(2,1)} %get-tuple-element.146), channel_id=1, source_target_pairs={{0,16},{8,24},{16,0},{24,8},{1,17},{9,25},{17,1},{25,9},{2,18},{10... | collective-permute-start | bytes 442376 | tf_op jit(solution)/shard_map/ppermute | solution.py:989
  142.2 12.9 %collective-permute-start.26 = (bf16[2,48,768]{2,1,0:T(8,128)(2,1)}, bf16[2,48,768]{2,1,0:T(8,128)(2,1)S(1)}, u32[]{:S(2)}, u32[]{:S(2)}) collective-permute-start(bf16[2,48,768]{2,1,0:T(8,128)(2,1)} %get-tuple-element.147), channel_id=1, source_target_pairs={{0,24},{8,0},{16,8},{24,16},{1,25},{9,1},{17,9},{25,17},{2,26},{10... | collective-permute-start | bytes 442376 | tf_op jit(solution)/shard_map/ppermute | solution.py:989
  182.0 24.6 %collective-permute-start.34 = (bf16[4,112,768]{2,1,0:T(8,128)(2,1)S(1)}, bf16[4,112,768]{2,1,0:T(8,128)(2,1)S(1)}, u32[]{:S(2)}, u32[]{:S(2)}) collective-permute-start(bf16[4,112,768]{2,1,0:T(8,128)(2,1)S(1)} %copy-done.65), channel_id=1, source_target_pairs={{0,4},{4,0},{1,5},{5,1},{2,6},{6,2},{3,7},{7,3},{8,12},{12,8},{9,1... | collective-permute-start | bytes 2064392 | tf_op jit(solution)/shard_map/ppermute | solution.py:993
  191.0 20.4 %collective-permute-start.33 = (bf16[2,192,768]{2,1,0:T(8,128)(2,1)}, bf16[2,192,768]{2,1,0:T(8,128)(2,1)S(1)}, u32[]{:S(2)}, u32[]{:S(2)}) collective-permute-start(bf16[2,192,768]{2,1,0:T(8,128)(2,1)} %get-tuple-element.161), channel_id=1, source_target_pairs={{0,4},{4,0},{1,5},{5,1},{2,6},{6,2},{3,7},{7,3},{8,12},{12,8},{9,1... | collective-permute-start | bytes 1769480 | tf_op jit(solution)/shard_map/ppermute | solution.py:993
  191.9 14.7 %collective-permute-start.35 = (bf16[144,768]{1,0:T(8,128)(2,1)S(1)}, bf16[144,768]{1,0:T(8,128)(2,1)S(1)}, u32[]{:S(2)}, u32[]{:S(2)}) collective-permute-start(bf16[144,768]{1,0:T(8,128)(2,1)S(1)} %copy-done.70), channel_id=1, source_target_pairs={{0,16},{8,24},{16,0},{24,8},{1,17},{9,25},{17,1},{25,9},{2,18},{10... | collective-permute-start | bytes 663560 | tf_op jit(solution)/shard_map/ppermute | solution.py:989
  193.3 13.2 %collective-permute-start.36 = (bf16[144,768]{1,0:T(8,128)(2,1)S(1)}, bf16[144,768]{1,0:T(8,128)(2,1)S(1)}, u32[]{:S(2)}, u32[]{:S(2)}) collective-permute-start(bf16[144,768]{1,0:T(8,128)(2,1)S(1)} %copy-done.69), channel_id=1, source_target_pairs={{0,24},{8,0},{16,8},{24,16},{1,25},{9,1},{17,9},{25,17},{2,26},{10... | collective-permute-start | bytes 663560 | tf_op jit(solution)/shard_map/ppermute | solution.py:989
  216.5 17.7 %collective-permute-start.43 = (bf16[2,192,768]{2,1,0:T(8,128)(2,1)S(1)}, bf16[2,192,768]{2,1,0:T(8,128)(2,1)S(1)}, u32[]{:S(2)}, u32[]{:S(2)}) collective-permute-start(bf16[2,192,768]{2,1,0:T(8,128)(2,1)S(1)} %copy-done.66), channel_id=1, source_target_pairs={{0,4},{4,0},{1,5},{5,1},{2,6},{6,2},{3,7},{7,3},{8,12},{12,8},{9,1... | collective-permute-start | bytes 1769480 | tf_op jit(solution)/shard_map/ppermute | solution.py:993
  217.1 30.3 %collective-permute-start.41 = (bf16[4,112,768]{2,1,0:T(8,128)(2,1)S(1)}, bf16[4,112,768]{2,1,0:T(8,128)(2,1)S(1)}, u32[]{:S(2)}, u32[]{:S(2)}) collective-permute-start(bf16[4,112,768]{2,1,0:T(8,128)(2,1)S(1)} %copy-done.64), channel_id=1, source_target_pairs={{0,4},{4,0},{1,5},{5,1},{2,6},{6,2},{3,7},{7,3},{8,12},{12,8},{9,1... | collective-permute-start | bytes 2064392 | tf_op jit(solution)/shard_map/ppermute | solution.py:993
  217.9 23.0 %collective-permute-start.42 = (bf16[304,768]{1,0:T(8,128)(2,1)}, bf16[304,768]{1,0:T(8,128)(2,1)S(1)}, u32[]{:S(2)}, u32[]{:S(2)}) collective-permute-start(bf16[304,768]{1,0:T(8,128)(2,1)} %get-tuple-element.169), channel_id=1, source_target_pairs={{0,8},{8,16},{16,24},{24,0},{1,9},{9,17},{17,25},{25,1},{2,10},{10... | collective-permute-start | bytes 1400840 | tf_op jit(solution)/shard_map/ppermute | solution.py:989
  219.0 21.9 %collective-permute-start.44 = (bf16[304,768]{1,0:T(8,128)(2,1)}, bf16[304,768]{1,0:T(8,128)(2,1)S(1)}, u32[]{:S(2)}, u32[]{:S(2)}) collective-permute-start(bf16[304,768]{1,0:T(8,128)(2,1)} %get-tuple-element.182), channel_id=1, source_target_pairs={{0,24},{8,0},{16,8},{24,16},{1,25},{9,1},{17,9},{25,17},{2,26},{10... | collective-permute-start | bytes 1400840 | tf_op jit(solution)/shard_map/ppermute | solution.py:989
  244.0 22.6 %collective-permute-start.45 = (bf16[304,768]{1,0:T(8,128)(2,1)}, bf16[304,768]{1,0:T(8,128)(2,1)S(1)}, u32[]{:S(2)}, u32[]{:S(2)}) collective-permute-start(bf16[304,768]{1,0:T(8,128)(2,1)} %add_second.1), channel_id=1, source_target_pairs={{0,16},{8,24},{16,0},{24,8},{1,17},{9,25},{17,1},{25,9},{2,18},{10... | collective-permute-start | bytes 1400840 | tf_op jit(solution)/shard_map/ppermute | solution.py:989
  266.6 14.0 %collective-permute-start.49 = (bf16[112,768]{1,0:T(8,128)(2,1)}, bf16[112,768]{1,0:T(8,128)(2,1)S(1)}, u32[]{:S(2)}, u32[]{:S(2)}) collective-permute-start(bf16[112,768]{1,0:T(8,128)(2,1)} %get-tuple-element.196), channel_id=1, source_target_pairs={{0,24},{8,0},{16,8},{24,16},{1,25},{9,1},{17,9},{25,17},{2,26},{10... | collective-permute-start | bytes 516104 | tf_op jit(solution)/shard_map/ppermute | solution.py:989
  268.8 14.3 %collective-permute-start.48 = (bf16[112,768]{1,0:T(8,128)(2,1)}, bf16[112,768]{1,0:T(8,128)(2,1)S(1)}, u32[]{:S(2)}, u32[]{:S(2)}) collective-permute-start(bf16[112,768]{1,0:T(8,128)(2,1)} %get-tuple-element.194), channel_id=1, source_target_pairs={{0,16},{8,24},{16,0},{24,8},{1,17},{9,25},{17,1},{25,9},{2,18},{10... | collective-permute-start | bytes 516104 | tf_op jit(solution)/shard_map/ppermute | solution.py:989
  268.8 16.8 %collective-permute-start.47 = (bf16[112,768]{1,0:T(8,128)(2,1)}, bf16[112,768]{1,0:T(8,128)(2,1)S(1)}, u32[]{:S(2)}, u32[]{:S(2)}) collective-permute-start(bf16[112,768]{1,0:T(8,128)(2,1)} %get-tuple-element.192), channel_id=1, source_target_pairs={{0,8},{8,16},{16,24},{24,0},{1,9},{9,17},{17,25},{25,1},{2,10},{10... | collective-permute-start | bytes 516104 | tf_op jit(solution)/shard_map/ppermute | solution.py:989
  272.2 18.3 %collective-permute-start.54 = (bf16[64,768]{1,0:T(8,128)(2,1)}, bf16[64,768]{1,0:T(8,128)(2,1)S(1)}, u32[]{:S(2)}, u32[]{:S(2)}) collective-permute-start(bf16[64,768]{1,0:T(8,128)(2,1)} %get-tuple-element.204), channel_id=1, source_target_pairs={{0,1},{1,0},{2,3},{3,2},{4,5},{5,4},{6,7},{7,6},{8,9},{9,8},{10,11... | collective-permute-start | bytes 294920 | tf_op jit(solution)/shard_map/ppermute | solution.py:984
  273.5 16.3 %collective-permute-start.57 = (bf16[24,768]{1,0:T(8,128)(2,1)}, bf16[24,768]{1,0:T(8,128)(2,1)S(1)}, u32[]{:S(2)}, u32[]{:S(2)}) collective-permute-start(bf16[24,768]{1,0:T(8,128)(2,1)} %get-tuple-element.209), channel_id=1, source_target_pairs={{0,0},{4,1},{8,2},{12,3},{16,4},{20,5},{24,6},{28,7},{1,8},{5,9},{... | collective-permute-start | bytes 110600 | tf_op jit(solution)/shard_map/ppermute | solution.py:1187
  283.0 14.7 %collective-permute-start.56 = (bf16[64,768]{1,0:T(8,128)(2,1)}, bf16[64,768]{1,0:T(8,128)(2,1)S(1)}, u32[]{:S(2)}, u32[]{:S(2)}) collective-permute-start(bf16[64,768]{1,0:T(8,128)(2,1)} %get-tuple-element.206), channel_id=1, source_target_pairs={{0,3},{1,2},{2,1},{3,0},{4,7},{5,6},{6,5},{7,4},{8,11},{9,10},{10,... | collective-permute-start | bytes 294920 | tf_op jit(solution)/shard_map/ppermute | solution.py:984
  (98 other events, 931.1 us)
